TPU v7x, 128 devices: a whole 4x4x4 slice. The times are simulated.
128 devices in a mesh: sfc: 32 (over y, z, core), sub: 4 (over x).
Axes of the slice: x: 4, y: 4, z: 4, core: 2. Of those that a mesh axis runs over, the one named last changes fastest.
Arguments:
- solution: float32 [64, 5, 65536], P(None, None, ('sfc', 'sub')), as said below
- register: float32 [64, 5, 65536], P(None, None, ('sfc', 'sub')), may hold values from -6 to 6
- metric: float32 [3, 3, 65536], P(None, None, ('sfc', 'sub')), may hold values from -1.5 to 1.5
- face_normal: float32 [3, 393216], P(None, ('sfc', 'sub')), as said below
- partner: int32 [393216], P(('sfc', 'sub')), may hold values from 0 to 11263, as said below
- flip_code: int32 [393216], P(('sfc', 'sub')), may hold values from 0 to 7, as said below
- face_role: int32 [393216], P(('sfc', 'sub')), may hold values from 0 to 2
- send_face: int32 [128, 128, 64], P(('sfc', 'sub')), may hold values from -1 to 3071, as said below
Outputs:
- section_register: float32 [64, 5, 65536], P(None, None, ('sfc', 'sub'))
- advanced_state: float32 [64, 5, 65536], P(None, None, ('sfc', 'sub'))
Inputs may be any that keep to these rules, and one draw needn't show every extreme that they name: `solution`: density and pressure of every node are positive. `face_normal`: the two sides of every face have normals of opposite sign. For face_role 0, a local column of the other side, whose partner is this column. For face_role 1 or 2, 3072 + q * 64 + k for the k-th face shared with device q, where q differs from this device's index by 1 to 24; all faces shared by two devices have their master on one of them. The other side's flip_code is the inverse orientation. `send_face`: row (q, p) lists device q's slave faces shared with device p, in slots k = 0, 1, ...; other slots hold -1. Rows with p and q more than 24 apart hold only -1. In every draw some device fills all 64 slots toward one peer.
All inputs are finite; a program needn't handle non-finite values.
Results may differ from a plain program's by a relative error of at most 0.0003.
Values sent between devices are 32-bit elements; how exact they have to be, the bound alone decides.
No kernel may reach another device: no remote copies, remote signals or barrier semaphores. Data moves between devices by JAX's collectives and lax.ppermute only.
A program may use at most 256 MiB of HBM per device.

v0:
```python
import jax
import jax.numpy as jnp
import numpy as np
from jax import lax
from jax.sharding import PartitionSpec as P

HEAT_RATIO = 1.4
LIFT_FACTOR = 6.0
PENALTY = 0.5
CFL_NUMBER = 0.3
SECTION_KEEP = -0.4178904745
SECTION_STEP = 0.4432226
neighbor_offsets = tuple(range(1, 25)) + tuple(range(-24, 0))


def passed_along(value, axis, steps):
    count = lax.axis_size(axis)
    initial, last = (max(0, -steps), min(count, count - steps))
    return lax.ppermute(value, axis, [(source, source + steps) for source in range(initial, last)])


def derivative_table():
    points = np.array([-1.0, -1.0 / np.sqrt(5.0), 1.0 / np.sqrt(5.0), 1.0])
    weights = np.array(
        [
            1.0
            / np.prod([points[target] - points[source] for source in range(4) if source != target])
            for target in range(4)
        ]
    )
    matrix = np.zeros((4, 4))
    for target in range(4):
        for source in range(4):
            if target != source:
                matrix[target, source] = (
                    weights[source] / weights[target] / (points[target] - points[source])
                )
        matrix[target, target] = -np.sum(matrix[target])
    identity = np.eye(4)
    first_dir = np.kron(matrix, np.kron(identity, identity))
    second_dir = np.kron(identity, np.kron(matrix, identity))
    third_dir = np.kron(identity, np.kron(identity, matrix))
    return jnp.asarray(np.concatenate([first_dir, second_dir, third_dir], axis=1), jnp.float32)


def face_traces(state_block):
    elements = state_block.shape[2]
    nodal_cube = state_block.reshape(4, 4, 4, 5, elements)
    face_list = [
        nodal_cube[0],
        nodal_cube[3],
        nodal_cube[:, 0],
        nodal_cube[:, 3],
        nodal_cube[:, :, 0],
        nodal_cube[:, :, 3],
    ]
    return jnp.stack(face_list, axis=3).reshape(4, 4, 5, 6 * elements)


def lift_faces(surface, elements):
    pieces = surface.reshape(4, 4, 5, 6, elements)
    volume = jnp.zeros((4, 4, 4, 5, elements), surface.dtype)
    volume = volume.at[0].add(pieces[:, :, :, 0]).at[3].add(pieces[:, :, :, 1])
    volume = volume.at[:, 0].add(pieces[:, :, :, 2]).at[:, 3].add(pieces[:, :, :, 3])
    volume = volume.at[:, :, 0].add(pieces[:, :, :, 4]).at[:, :, 3].add(pieces[:, :, :, 5])
    return volume.reshape(64, 5, elements)


def orient(trace, codes):
    flip_first = (codes % 2 == 1)[None, None, None, :]
    flip_second = (codes // 2 % 2 == 1)[None, None, None, :]
    swapped = (codes >= 4)[None, None, None, :]
    trace = jnp.where(flip_first, trace[::-1], trace)
    trace = jnp.where(flip_second, trace[:, ::-1], trace)
    return jnp.where(swapped, jnp.swapaxes(trace, 0, 1), trace)


def normal_flux(values, normal):
    density = values[:, :, 0]
    momentum = values[:, :, 1:4]
    energy = values[:, :, 4]
    velocity = momentum / density[:, :, None]
    pressure = (HEAT_RATIO - 1.0) * (energy - 0.5 * jnp.sum(momentum * velocity, axis=2))
    normal_speed = jnp.sum(velocity * normal[None, None], axis=2)
    flux_terms = jnp.concatenate(
        [
            (density * normal_speed)[:, :, None],
            momentum * normal_speed[:, :, None] + pressure[:, :, None] * normal[None, None],
            ((energy + pressure) * normal_speed)[:, :, None],
        ],
        axis=2,
    )
    length = jnp.sqrt(jnp.sum(normal * normal, axis=0))
    wave = jnp.abs(normal_speed) + jnp.sqrt(HEAT_RATIO * pressure / density) * length[None, None]
    return (flux_terms, wave, length)


def face_flux(own, other_side, normal):
    own_flux, own_wave, length = normal_flux(own, normal)
    other_result = normal_flux(other_side, normal)
    wave_bound = jnp.maximum(own_wave, other_result[1])[:, :, None]
    jump_term = other_side - own
    viscous = jnp.array([0.0, 1.0, 1.0, 1.0, 1.0], jnp.float32)[None, None, :, None]
    star_flux = (
        0.5 * (own_flux + other_result[0])
        - 0.5 * wave_bound * jump_term
        - PENALTY * length[None, None, None] * viscous * jump_term
    )
    return (star_flux, own_flux)


def volume_rate(state_block, metric_block, derivative):
    elements = state_block.shape[2]
    density = state_block[:, 0]
    momentum = state_block[:, 1:4]
    energy = state_block[:, 4]
    velocity = momentum / density[:, None]
    pressure = (HEAT_RATIO - 1.0) * (energy - 0.5 * jnp.sum(momentum * velocity, axis=1))
    contravariant = []
    for direction in range(3):
        along = jnp.sum(metric_block[direction][None] * velocity, axis=1)
        component = [
            (density * along)[:, None],
            momentum * along[:, None] + pressure[:, None] * metric_block[direction][None],
            ((energy + pressure) * along)[:, None],
        ]
        contravariant.append(jnp.concatenate(component, axis=1))
    stacked = jnp.stack(contravariant, axis=0).reshape(192, 5 * elements)
    divergence = jnp.dot(
        derivative, stacked, precision=lax.Precision.HIGHEST, preferred_element_type=jnp.float32
    )
    return -divergence.reshape(64, 5, elements)


def node_speed(state_block):
    density = state_block[:, 0]
    momentum = state_block[:, 1:4]
    energy = state_block[:, 4]
    velocity = momentum / density[:, None]
    pressure = (HEAT_RATIO - 1.0) * (energy - 0.5 * jnp.sum(momentum * velocity, axis=1))
    return jnp.sqrt(jnp.sum(velocity * velocity, axis=1)) + jnp.sqrt(
        HEAT_RATIO * pressure / density
    )


def place_arrivals(buffer, arrivals):
    devices = buffer.shape[1]
    rank = lax.axis_index(("sfc", "sub"))
    sources = jnp.array(neighbor_offsets, jnp.int32)
    source_rank = rank - sources
    source_rank = jnp.where((source_rank >= 0) & (source_rank < devices), source_rank, devices)
    stacked = jnp.stack(arrivals, axis=1)
    return jnp.zeros_like(buffer).at[:, source_rank, :].set(stacked, mode="drop")


def pick_slab(buffer, offset):
    devices = buffer.shape[1]
    target = jnp.clip(lax.axis_index(("sfc", "sub")) + offset, 0, devices - 1)
    return lax.dynamic_index_in_dim(buffer, target, 1, keepdims=False)


def deliver_traces(buffer):
    arrivals = []
    for offset in neighbor_offsets:
        arrivals.append(passed_along(pick_slab(buffer, offset), ("sfc", "sub"), offset))
    return place_arrivals(buffer, arrivals)


def deliver_fluxes(buffer):
    arrivals = []
    for offset in neighbor_offsets:
        arrivals.append(passed_along(pick_slab(buffer, offset), ("sfc", "sub"), offset))
    return place_arrivals(buffer, arrivals)


def on_device(solution, register, metric, face_normal, partner, flip_code, face_role, send_face):
    elements = solution.shape[2]
    columns = 6 * elements
    devices = lax.axis_size(("sfc", "sub"))
    slots_per = send_face.shape[2]
    slot_count = devices * slots_per
    derivative = derivative_table()
    traces = face_traces(solution)
    trace_table = traces.reshape(80, columns)
    routes = send_face[0].reshape(-1)
    outgoing = jnp.take(trace_table, jnp.clip(routes, 0, columns - 1), axis=1)
    outgoing = jnp.where((routes >= 0)[None, :], outgoing, 0.0)
    master_side = face_role == 1
    remote_at = jnp.clip(partner - columns, 0, slot_count - 1)
    local_index = jnp.clip(partner, 0, columns - 1)
    received = deliver_traces(outgoing.reshape(80, devices, slots_per)).reshape(80, slot_count)
    top_speed = lax.pmax(jnp.max(node_speed(solution)), ("sfc", "sub"))
    local_side = jnp.take(trace_table, local_index, axis=1).reshape(4, 4, 5, columns)
    star_local, own_flux = face_flux(traces, orient(local_side, flip_code), face_normal)
    target_slot = jnp.where(master_side, partner - columns, slot_count)
    owner_column = (
        jnp.zeros((slot_count,), jnp.int32)
        .at[target_slot]
        .set(jnp.arange(columns, dtype=jnp.int32), mode="drop")
    )
    present = jnp.zeros((slot_count,), jnp.bool_).at[target_slot].set(True, mode="drop")
    own_at = jnp.take(trace_table, owner_column, axis=1).reshape(4, 4, 5, slot_count)
    other_side = orient(received.reshape(4, 4, 5, slot_count), jnp.take(flip_code, owner_column))
    other_side = jnp.where(present[None, None, None, :], other_side, own_at)
    star_master = face_flux(own_at, other_side, jnp.take(face_normal, owner_column, axis=1))[0]
    outbound = jnp.where(present[None, None, None, :], star_master, 0.0).reshape(
        80, devices, slots_per
    )
    returned = deliver_fluxes(outbound).reshape(4, 4, 5, slot_count)
    master_star = jnp.take(star_master, remote_at, axis=3)
    slave_star = -orient(jnp.take(returned, remote_at, axis=3), flip_code)
    star_flux = jnp.where(
        (face_role == 0)[None, None, None, :],
        star_local,
        jnp.where(master_side[None, None, None, :], master_star, slave_star),
    )
    surface = LIFT_FACTOR * (own_flux - star_flux)
    rate_field = volume_rate(solution, metric, derivative) + lift_faces(surface, elements)
    section_register = SECTION_KEEP * register + rate_field
    advanced_state = solution + CFL_NUMBER / top_speed * SECTION_STEP * section_register
    return (section_register, advanced_state)


def solution(mesh):
    placed = (
        P(None, None, ("sfc", "sub")),
        P(None, None, ("sfc", "sub")),
        P(None, None, ("sfc", "sub")),
        P(None, ("sfc", "sub")),
        P(("sfc", "sub")),
        P(("sfc", "sub")),
        P(("sfc", "sub")),
        P(("sfc", "sub"), None, None),
    )
    return jax.shard_map(
        on_device,
        mesh=mesh,
        in_specs=placed,
        out_specs=(P(None, None, ("sfc", "sub")), P(None, None, ("sfc", "sub"))),
        check_vma=False,
    )
```

profile of v0, /device:TPU:0, one launch (start us, length us, event | category | flops | bytes accessed | tf_op | source)
XLA Modules:
  0.0 1393.8 jit_solution(5684510441336604952)
XLA Ops:
  3.0 11.8 scatter_custom_fusion
  14.9 45.5 %gather_fusion.2 = s32[8192]{0:T(1024)S(1)} fusion(s32[3072]{0:T(1024)S(1)} %copy-done, s32[8192]{0:T(1024)S(1)} %fusion.40), kind=kCustom, calls=%fused_computation.6 | custom fusion | bytes 98304 | tf_op jit(solution)/shard_map/jit(_take)/gather | solution.py:203
  66.4 27.7 %gather_fusion.4 = f32[8192,80]{1,0:T(8,128)} fusion(f32[80,3072]{0,1:T(8,128)S(1)} %copy.684, s32[8192]{0:T(1024)S(1)} %fusion.41), kind=kCustom, calls=%fused_computation.2.clone | custom fusion | bytes 5275648 | tf_op jit(solution)/shard_map/jit(_take)/gather | solution.py:186
  94.1 6.0 bitcast_select_fusion
  102.9 12.0 collective-permute-start
  114.9 10.2 collective-permute-start.1
  125.1 10.2 collective-permute-start.2
  135.3 10.2 collective-permute-start.3
  145.5 10.6 collective-permute-start.4
  156.2 27.7 %gather_fusion.3 = f32[8192,80]{1,0:T(8,128)} fusion(f32[80,3072]{0,1:T(8,128)S(1)} %copy.684, s32[8192]{0:T(1024)S(1)} %fusion.40), kind=kCustom, calls=%fused_computation.clone | custom fusion | bytes 5275648 | tf_op jit(solution)/shard_map/jit(_take)/gather | solution.py:202
  190.5 7.4 select_bitcast_fusion
  198.0 29.1 %gather_fusion.1 = f32[8192,3]{1,0:T(8,128)} fusion(f32[3,3072]{0,1:T(8,128)} %copy.702, s32[8192]{0:T(1024)S(1)} %fusion.40), kind=kCustom, calls=%fused_computation.5 | custom fusion | bytes 229376 | tf_op jit(solution)/shard_map/jit(_take)/gather | solution.py:205
  227.1 5.7 multiply_reduce_fusion
  233.4 10.8 gather_fusion
  264.1 76.9 %pmax.7 = f32[]{:T(128)} all-reduce(f32[]{:T(128)} %fusion.34), channel_id=1, replica_groups=mesh['sfc'=32,'sub'=4] {'sfc','sub'}, use_global_device_ids=true, to_apply=%region_20.23 | all-reduce | flops 1 | bytes 8 | tf_op jit(solution)/shard_map/pmax | solution.py:192
  351.4 14.2 %scatter_custom_fusion.1 = pred[8192]{0:T(1024)(128)(4,1)} fusion(s32[3072]{0:T(1024)} %copy-done.101, pred[3072]{0:T(1024)(128)(4,1)S(1)} %broadcast.459, pred[]{:T(512)} %constant.630.clone.1), kind=kCustom, calls=%fused_computation.383 | custom fusion | bytes 8704 | tf_op jit(solution)/shard_map/scatter | solution.py:201
  366.3 6.4 collective-permute-start.5
  386.8 5.1 collective-permute-start.9
  395.8 4.4 collective-permute-start.11
  403.4 4.8 collective-permute-start.13
  408.2 5.5 collective-permute-start.14
  413.8 6.6 collective-permute-start.15
  467.8 30.9 %collective-permute-start.42 = (f32[80,64]{0,1:T(8,128)S(1)}, f32[80,64]{0,1:T(8,128)S(1)}, u32[]{:S(2)}, u32[]{:S(2)}) collective-permute-start(f32[80,64]{0,1:T(8,128)S(1)} %copy-done.41), channel_id=1, source_target_pairs={{6,0},{7,1},{8,2},{9,3},{10,4},{11,5},{12,6},{13,7},{14,8},{15,9},... | collective-permute-start | bytes 61448 | tf_op jit(solution)/shard_map/ppermute | solution.py:19
  498.7 10.2 collective-permute-start.43
  509.0 10.2 collective-permute-start.44
  519.2 10.2 collective-permute-start.45
  529.4 10.2 collective-permute-start.46
  539.6 10.2 collective-permute-start.47
  555.9 6.6 scatter_fusion
  562.5 7.0 copy.716
  569.5 5.7 reshape_reshape.7
  581.1 31.7 %rev.21 = f32[4,4,5,8192]{3,1,2,0:T(4,128)} reverse(f32[4,4,5,8192]{3,1,2,0:T(4,128)} %reverse_select_fusion), dimensions={1} | reverse | bytes 5242880 | tf_op jit(solution)/shard_map/rev | solution.py:74
  632.6 5.9 reshape.580
  638.5 4.0 constant_dynamic-slice_fusion.36
  642.5 5.4 constant_dynamic-slice_fusion.18
  649.3 11.7 collective-permute-start.48
  661.0 6.6 constant_dynamic-slice_fusion
  669.1 8.7 collective-permute-start.49
  679.3 10.2 collective-permute-start.50
  690.9 10.2 collective-permute-start.51
  702.6 10.2 collective-permute-start.52
  771.6 40.3 %copy.732 = f32[4,4,5,8192]{2,1,3,0:T(4,128)} copy(f32[4,4,5,8192]{3,1,2,0:T(4,128)S(1)} %get-tuple-element.104) | data formatting | bytes 5242880 | tf_op jit(solution)/shard_map/sub | solution.py:105
  811.8 125.9 %gather_fusion.5 = f32[3072,4,4,5]{3,2,1,0:T(4,128)} fusion(f32[4,4,5,8192]{2,1,3,0:T(4,128)} %copy.732, s32[3072]{0:T(1024)S(1)} %copy-done.22), kind=kCustom, calls=%fused_computation.1.clone | custom fusion | bytes 1978368 | tf_op jit(solution)/shard_map/jit(_take)/gather | solution.py:210
  937.9 19.3 %copy.733 = f32[3072,4,4,5]{0,2,3,1:T(4,128)} copy(f32[3072,4,4,5]{3,2,1,0:T(4,128)} %gather_fusion.5) | data formatting | bytes 1966080 | tf_op jit(solution)/shard_map/jit(_take)/gather | solution.py:210
  957.3 6.5 collective-permute-start.53
  977.9 5.1 collective-permute-start.57
  986.9 4.4 collective-permute-start.59
  994.5 4.8 collective-permute-start.61
  999.4 5.5 collective-permute-start.62
  1005.0 6.6 collective-permute-start.63
  1059.0 30.9 %collective-permute-start.90 = (f32[80,64]{0,1:T(8,128)S(1)}, f32[80,64]{0,1:T(8,128)S(1)}, u32[]{:S(2)}, u32[]{:S(2)}) collective-permute-start(f32[80,64]{0,1:T(8,128)S(1)} %bitcast.598), channel_id=1, source_target_pairs={{6,0},{7,1},{8,2},{9,3},{10,4},{11,5},{12,6},{13,7},{14,8},{15,9},... | collective-permute-start | bytes 61448 | tf_op jit(solution)/shard_map/ppermute | solution.py:19
  1090.0 10.2 collective-permute-start.91
  1100.2 10.2 collective-permute-start.92
  1110.4 10.2 collective-permute-start.93
  1120.6 10.2 collective-permute-start.94
  1130.8 10.2 collective-permute-start.95
  1147.1 7.2 scatter_fusion.1
  1154.3 7.0 copy.783
  1161.3 5.7 reshape.581
  1167.0 44.4 %copy.784 = f32[4,4,5,8192]{2,1,3,0:T(4,128)} copy(f32[4,4,5,8192]{3,2,1,0:T(8,128)} %reshape.581) | data formatting | bytes 5242880 | tf_op jit(solution)/shard_map/reshape | solution.py:209
  1211.4 125.9 %gather_fusion.6 = f32[3072,4,4,5]{3,2,1,0:T(4,128)} fusion(f32[4,4,5,8192]{2,1,3,0:T(4,128)} %copy.784, s32[3072]{0:T(1024)S(1)} %copy-done.22), kind=kCustom, calls=%fused_computation.3.clone | custom fusion | bytes 1978368 | tf_op jit(solution)/shard_map/jit(_take)/gather | solution.py:211
  1337.3 18.4 %copy.785 = f32[3072,4,4,5]{0,2,3,1:T(4,128)S(1)} copy(f32[3072,4,4,5]{3,2,1,0:T(4,128)} %gather_fusion.6) | data formatting | bytes 1966080 | tf_op jit(solution)/shard_map/jit(_take)/gather | solution.py:211
  1357.2 8.2 rev.19
  1365.4 8.2 rev.23
  (615 shorter events, 308.6 us)
Async XLA Ops:
  102.9 263.4 %collective-permute-start = (f32[80,64]{0,1:T(8,128)}, f32[80,64]{0,1:T(8,128)}, u32[]{:S(2)}, u32[]{:S(2)}) collective-permute-start(f32[80,64]{0,1:T(8,128)} %get-tuple-element.208), channel_id=1, source_target_pairs={{0,1},{1,2},{2,3},{3,4},{4,5},{5,6},{6,7},{7,8},{8,9},{9,10},{10,1... | collective-permute-start | bytes 61448 | tf_op jit(solution)/shard_map/ppermute | solution.py:19
  114.9 258.5 %collective-permute-start.1 = (f32[80,64]{0,1:T(8,128)}, f32[80,64]{0,1:T(8,128)}, u32[]{:S(2)}, u32[]{:S(2)}) collective-permute-start(f32[80,64]{0,1:T(8,128)} %get-tuple-element.207), channel_id=1, source_target_pairs={{0,2},{1,3},{2,4},{3,5},{4,6},{5,7},{6,8},{7,9},{8,10},{9,11},{10,... | collective-permute-start | bytes 61448 | tf_op jit(solution)/shard_map/ppermute | solution.py:19
  125.1 253.0 %collective-permute-start.2 = (f32[80,64]{0,1:T(8,128)}, f32[80,64]{0,1:T(8,128)}, u32[]{:S(2)}, u32[]{:S(2)}) collective-permute-start(f32[80,64]{0,1:T(8,128)} %get-tuple-element.206), channel_id=1, source_target_pairs={{0,3},{1,4},{2,5},{3,6},{4,7},{5,8},{6,9},{7,10},{8,11},{9,12},{10... | collective-permute-start | bytes 61448 | tf_op jit(solution)/shard_map/ppermute | solution.py:19
  135.3 247.2 %collective-permute-start.3 = (f32[80,64]{0,1:T(8,128)}, f32[80,64]{0,1:T(8,128)}, u32[]{:S(2)}, u32[]{:S(2)}) collective-permute-start(f32[80,64]{0,1:T(8,128)} %get-tuple-element.205), channel_id=1, source_target_pairs={{0,4},{1,5},{2,6},{3,7},{4,8},{5,9},{6,10},{7,11},{8,12},{9,13},{1... | collective-permute-start | bytes 61448 | tf_op jit(solution)/shard_map/ppermute | solution.py:19
  145.5 241.3 %collective-permute-start.4 = (f32[80,64]{0,1:T(8,128)}, f32[80,64]{0,1:T(8,128)}, u32[]{:S(2)}, u32[]{:S(2)}) collective-permute-start(f32[80,64]{0,1:T(8,128)} %get-tuple-element.204), channel_id=1, source_target_pairs={{0,5},{1,6},{2,7},{3,8},{4,9},{5,10},{6,11},{7,12},{8,13},{9,14},{... | collective-permute-start | bytes 61448 | tf_op jit(solution)/shard_map/ppermute | solution.py:19
  366.3 26.4 %collective-permute-start.5 = (f32[80,64]{0,1:T(8,128)S(1)}, f32[80,64]{0,1:T(8,128)S(1)}, u32[]{:S(2)}, u32[]{:S(2)}) collective-permute-start(f32[80,64]{0,1:T(8,128)S(1)} %copy-done.44), channel_id=1, source_target_pairs={{0,6},{1,7},{2,8},{3,9},{4,10},{5,11},{6,12},{7,13},{8,14},{9,15},... | collective-permute-start | bytes 61448 | tf_op jit(solution)/shard_map/ppermute | solution.py:19
  373.4 22.4 %collective-permute-start.6 = (f32[80,64]{0,1:T(8,128)S(1)}, f32[80,64]{0,1:T(8,128)S(1)}, u32[]{:S(2)}, u32[]{:S(2)}) collective-permute-start(f32[80,64]{0,1:T(8,128)S(1)} %copy-done.42), channel_id=1, source_target_pairs={{0,7},{1,8},{2,9},{3,10},{4,11},{5,12},{6,13},{7,14},{8,15},{9,16}... | collective-permute-start | bytes 61448 | tf_op jit(solution)/shard_map/ppermute | solution.py:19
  378.2 22.1 %collective-permute-start.7 = (f32[80,64]{0,1:T(8,128)S(1)}, f32[80,64]{0,1:T(8,128)S(1)}, u32[]{:S(2)}, u32[]{:S(2)}) collective-permute-start(f32[80,64]{0,1:T(8,128)S(1)} %copy-done.40), channel_id=1, source_target_pairs={{0,8},{1,9},{2,10},{3,11},{4,12},{5,13},{6,14},{7,15},{8,16},{9,17... | collective-permute-start | bytes 61448 | tf_op jit(solution)/shard_map/ppermute | solution.py:19
  382.5 20.9 %collective-permute-start.8 = (f32[80,64]{0,1:T(8,128)S(1)}, f32[80,64]{0,1:T(8,128)S(1)}, u32[]{:S(2)}, u32[]{:S(2)}) collective-permute-start(f32[80,64]{0,1:T(8,128)S(1)} %copy-done.38), channel_id=1, source_target_pairs={{0,9},{1,10},{2,11},{3,12},{4,13},{5,14},{6,15},{7,16},{8,17},{9,1... | collective-permute-start | bytes 61448 | tf_op jit(solution)/shard_map/ppermute | solution.py:19
  386.8 21.5 %collective-permute-start.9 = (f32[80,64]{0,1:T(8,128)S(1)}, f32[80,64]{0,1:T(8,128)S(1)}, u32[]{:S(2)}, u32[]{:S(2)}) collective-permute-start(f32[80,64]{0,1:T(8,128)S(1)} %copy-done.36), channel_id=1, source_target_pairs={{0,10},{1,11},{2,12},{3,13},{4,14},{5,15},{6,16},{7,17},{8,18},{9,... | collective-permute-start | bytes 61448 | tf_op jit(solution)/shard_map/ppermute | solution.py:19
  392.7 21.1 %collective-permute-start.10 = (f32[80,64]{0,1:T(8,128)S(1)}, f32[80,64]{0,1:T(8,128)S(1)}, u32[]{:S(2)}, u32[]{:S(2)}) collective-permute-start(f32[80,64]{0,1:T(8,128)S(1)} %copy-done.33), channel_id=1, source_target_pairs={{0,11},{1,12},{2,13},{3,14},{4,15},{5,16},{6,17},{7,18},{8,19},{9,... | collective-permute-start | bytes 61448 | tf_op jit(solution)/shard_map/ppermute | solution.py:19
  395.8 24.7 %collective-permute-start.11 = (f32[80,64]{0,1:T(8,128)S(1)}, f32[80,64]{0,1:T(8,128)S(1)}, u32[]{:S(2)}, u32[]{:S(2)}) collective-permute-start(f32[80,64]{0,1:T(8,128)S(1)} %copy-done.31), channel_id=1, source_target_pairs={{0,12},{1,13},{2,14},{3,15},{4,16},{5,17},{6,18},{7,19},{8,20},{9,... | collective-permute-start | bytes 61448 | tf_op jit(solution)/shard_map/ppermute | solution.py:19
  400.3 21.5 %collective-permute-start.12 = (f32[80,64]{0,1:T(8,128)}, f32[80,64]{0,1:T(8,128)S(1)}, u32[]{:S(2)}, u32[]{:S(2)}) collective-permute-start(f32[80,64]{0,1:T(8,128)} %get-tuple-element.196), channel_id=1, source_target_pairs={{0,13},{1,14},{2,15},{3,16},{4,17},{5,18},{6,19},{7,20},{8,21},{9,... | collective-permute-start | bytes 61448 | tf_op jit(solution)/shard_map/ppermute | solution.py:19
  403.4 22.1 %collective-permute-start.13 = (f32[80,64]{0,1:T(8,128)}, f32[80,64]{0,1:T(8,128)S(1)}, u32[]{:S(2)}, u32[]{:S(2)}) collective-permute-start(f32[80,64]{0,1:T(8,128)} %get-tuple-element.195), channel_id=1, source_target_pairs={{0,14},{1,15},{2,16},{3,17},{4,18},{5,19},{6,20},{7,21},{8,22},{9,... | collective-permute-start | bytes 61448 | tf_op jit(solution)/shard_map/ppermute | solution.py:19
  408.2 19.6 %collective-permute-start.14 = (f32[80,64]{0,1:T(8,128)}, f32[80,64]{0,1:T(8,128)S(1)}, u32[]{:S(2)}, u32[]{:S(2)}) collective-permute-start(f32[80,64]{0,1:T(8,128)} %get-tuple-element.194), channel_id=1, source_target_pairs={{0,15},{1,16},{2,17},{3,18},{4,19},{5,20},{6,21},{7,22},{8,23},{9,... | collective-permute-start | bytes 61448 | tf_op jit(solution)/shard_map/ppermute | solution.py:19
  413.8 15.3 %collective-permute-start.15 = (f32[80,64]{0,1:T(8,128)}, f32[80,64]{0,1:T(8,128)S(1)}, u32[]{:S(2)}, u32[]{:S(2)}) collective-permute-start(f32[80,64]{0,1:T(8,128)} %get-tuple-element.193), channel_id=1, source_target_pairs={{0,16},{1,17},{2,18},{3,19},{4,20},{5,21},{6,22},{7,23},{8,24},{9,... | collective-permute-start | bytes 61448 | tf_op jit(solution)/shard_map/ppermute | solution.py:19
  420.5 10.3 collective-permute-start.16
  421.8 11.3 collective-permute-start.17
  446.8 10.2 collective-permute-start.30
  448.4 10.0 collective-permute-start.31
  449.7 10.0 collective-permute-start.32
  451.0 10.0 collective-permute-start.33
  461.1 37.7 %collective-permute-start.38 = (f32[80,64]{0,1:T(8,128)S(1)}, f32[80,64]{0,1:T(8,128)S(1)}, u32[]{:S(2)}, u32[]{:S(2)}) collective-permute-start(f32[80,64]{0,1:T(8,128)S(1)} %copy-done.47), channel_id=1, source_target_pairs={{10,0},{11,1},{12,2},{13,3},{14,4},{15,5},{16,6},{17,7},{18,8},{19... | collective-permute-start | bytes 61448 | tf_op jit(solution)/shard_map/ppermute | solution.py:19
  462.4 46.5 %collective-permute-start.39 = (f32[80,64]{0,1:T(8,128)S(1)}, f32[80,64]{0,1:T(8,128)S(1)}, u32[]{:S(2)}, u32[]{:S(2)}) collective-permute-start(f32[80,64]{0,1:T(8,128)S(1)} %copy-done.46), channel_id=1, source_target_pairs={{9,0},{10,1},{11,2},{12,3},{13,4},{14,5},{15,6},{16,7},{17,8},{18,... | collective-permute-start | bytes 61448 | tf_op jit(solution)/shard_map/ppermute | solution.py:19
  463.7 55.4 %collective-permute-start.40 = (f32[80,64]{0,1:T(8,128)S(1)}, f32[80,64]{0,1:T(8,128)S(1)}, u32[]{:S(2)}, u32[]{:S(2)}) collective-permute-start(f32[80,64]{0,1:T(8,128)S(1)} %copy-done.45), channel_id=1, source_target_pairs={{8,0},{9,1},{10,2},{11,3},{12,4},{13,5},{14,6},{15,7},{16,8},{17,9... | collective-permute-start | bytes 61448 | tf_op jit(solution)/shard_map/ppermute | solution.py:19
  465.1 64.3 %collective-permute-start.41 = (f32[80,64]{0,1:T(8,128)S(1)}, f32[80,64]{0,1:T(8,128)S(1)}, u32[]{:S(2)}, u32[]{:S(2)}) collective-permute-start(f32[80,64]{0,1:T(8,128)S(1)} %copy-done.43), channel_id=1, source_target_pairs={{7,0},{8,1},{9,2},{10,3},{11,4},{12,5},{13,6},{14,7},{15,8},{16,9}... | collective-permute-start | bytes 61448 | tf_op jit(solution)/shard_map/ppermute | solution.py:19
  467.8 71.9 %collective-permute-start.42 = (f32[80,64]{0,1:T(8,128)S(1)}, f32[80,64]{0,1:T(8,128)S(1)}, u32[]{:S(2)}, u32[]{:S(2)}) collective-permute-start(f32[80,64]{0,1:T(8,128)S(1)} %copy-done.41), channel_id=1, source_target_pairs={{6,0},{7,1},{8,2},{9,3},{10,4},{11,5},{12,6},{13,7},{14,8},{15,9},... | collective-permute-start | bytes 61448 | tf_op jit(solution)/shard_map/ppermute | solution.py:19
  498.7 51.1 %collective-permute-start.43 = (f32[80,64]{0,1:T(8,128)S(1)}, f32[80,64]{0,1:T(8,128)S(1)}, u32[]{:S(2)}, u32[]{:S(2)}) collective-permute-start(f32[80,64]{0,1:T(8,128)S(1)} %copy-done.39), channel_id=1, source_target_pairs={{5,0},{6,1},{7,2},{8,3},{9,4},{10,5},{11,6},{12,7},{13,8},{14,9},{... | collective-permute-start | bytes 61448 | tf_op jit(solution)/shard_map/ppermute | solution.py:19
  509.0 40.9 %collective-permute-start.44 = (f32[80,64]{0,1:T(8,128)S(1)}, f32[80,64]{0,1:T(8,128)S(1)}, u32[]{:S(2)}, u32[]{:S(2)}) collective-permute-start(f32[80,64]{0,1:T(8,128)S(1)} %copy-done.37), channel_id=1, source_target_pairs={{4,0},{5,1},{6,2},{7,3},{8,4},{9,5},{10,6},{11,7},{12,8},{13,9},{1... | collective-permute-start | bytes 61448 | tf_op jit(solution)/shard_map/ppermute | solution.py:19
  519.2 30.7 %collective-permute-start.45 = (f32[80,64]{0,1:T(8,128)S(1)}, f32[80,64]{0,1:T(8,128)S(1)}, u32[]{:S(2)}, u32[]{:S(2)}) collective-permute-start(f32[80,64]{0,1:T(8,128)S(1)} %copy-done.35), channel_id=1, source_target_pairs={{3,0},{4,1},{5,2},{6,3},{7,4},{8,5},{9,6},{10,7},{11,8},{12,9},{13... | collective-permute-start | bytes 61448 | tf_op jit(solution)/shard_map/ppermute | solution.py:19
  529.4 20.5 %collective-permute-start.46 = (f32[80,64]{0,1:T(8,128)S(1)}, f32[80,64]{0,1:T(8,128)S(1)}, u32[]{:S(2)}, u32[]{:S(2)}) collective-permute-start(f32[80,64]{0,1:T(8,128)S(1)} %copy-done.34), channel_id=1, source_target_pairs={{2,0},{3,1},{4,2},{5,3},{6,4},{7,5},{8,6},{9,7},{10,8},{11,9},{12,... | collective-permute-start | bytes 61448 | tf_op jit(solution)/shard_map/ppermute | solution.py:19
  539.6 13.8 collective-permute-start.47
  649.3 308.0 %collective-permute-start.48 = (f32[80,64]{0,1:T(8,128)}, f32[80,64]{0,1:T(8,128)}, u32[]{:S(2)}, u32[]{:S(2)}) collective-permute-start(f32[80,64]{0,1:T(8,128)} %bitcast.634), channel_id=1, source_target_pairs={{0,1},{1,2},{2,3},{3,4},{4,5},{5,6},{6,7},{7,8},{8,9},{9,10},{10,1... | collective-permute-start | bytes 61448 | tf_op jit(solution)/shard_map/ppermute | solution.py:19
  669.1 295.5 %collective-permute-start.49 = (f32[80,64]{0,1:T(8,128)}, f32[80,64]{0,1:T(8,128)}, u32[]{:S(2)}, u32[]{:S(2)}) collective-permute-start(f32[80,64]{0,1:T(8,128)} %bitcast.639), channel_id=1, source_target_pairs={{0,2},{1,3},{2,4},{3,5},{4,6},{5,7},{6,8},{7,9},{8,10},{9,11},{10,... | collective-permute-start | bytes 61448 | tf_op jit(solution)/shard_map/ppermute | solution.py:19
  679.3 290.1 %collective-permute-start.50 = (f32[80,64]{0,1:T(8,128)}, f32[80,64]{0,1:T(8,128)}, u32[]{:S(2)}, u32[]{:S(2)}) collective-permute-start(f32[80,64]{0,1:T(8,128)} %bitcast.638), channel_id=1, source_target_pairs={{0,3},{1,4},{2,5},{3,6},{4,7},{5,8},{6,9},{7,10},{8,11},{9,12},{10... | collective-permute-start | bytes 61448 | tf_op jit(solution)/shard_map/ppermute | solution.py:19
  690.9 282.7 %collective-permute-start.51 = (f32[80,64]{0,1:T(8,128)}, f32[80,64]{0,1:T(8,128)}, u32[]{:S(2)}, u32[]{:S(2)}) collective-permute-start(f32[80,64]{0,1:T(8,128)} %bitcast.637), channel_id=1, source_target_pairs={{0,4},{1,5},{2,6},{3,7},{4,8},{5,9},{6,10},{7,11},{8,12},{9,13},{1... | collective-permute-start | bytes 61448 | tf_op jit(solution)/shard_map/ppermute | solution.py:19
  702.6 275.4 %collective-permute-start.52 = (f32[80,64]{0,1:T(8,128)}, f32[80,64]{0,1:T(8,128)}, u32[]{:S(2)}, u32[]{:S(2)}) collective-permute-start(f32[80,64]{0,1:T(8,128)} %bitcast.636), channel_id=1, source_target_pairs={{0,5},{1,6},{2,7},{3,8},{4,9},{5,10},{6,11},{7,12},{8,13},{9,14},{... | collective-permute-start | bytes 61448 | tf_op jit(solution)/shard_map/ppermute | solution.py:19
  957.3 26.5 %collective-permute-start.53 = (f32[80,64]{0,1:T(8,128)}, f32[80,64]{0,1:T(8,128)S(1)}, u32[]{:S(2)}, u32[]{:S(2)}) collective-permute-start(f32[80,64]{0,1:T(8,128)} %bitcast.166), channel_id=1, source_target_pairs={{0,6},{1,7},{2,8},{3,9},{4,10},{5,11},{6,12},{7,13},{8,14},{9,15},... | collective-permute-start | bytes 61448 | tf_op jit(solution)/shard_map/ppermute | solution.py:19
  964.6 22.3 %collective-permute-start.54 = (f32[80,64]{0,1:T(8,128)}, f32[80,64]{0,1:T(8,128)S(1)}, u32[]{:S(2)}, u32[]{:S(2)}) collective-permute-start(f32[80,64]{0,1:T(8,128)} %bitcast.635), channel_id=1, source_target_pairs={{0,7},{1,8},{2,9},{3,10},{4,11},{5,12},{6,13},{7,14},{8,15},{9,16}... | collective-permute-start | bytes 61448 | tf_op jit(solution)/shard_map/ppermute | solution.py:19
  969.4 22.0 %collective-permute-start.55 = (f32[80,64]{0,1:T(8,128)}, f32[80,64]{0,1:T(8,128)S(1)}, u32[]{:S(2)}, u32[]{:S(2)}) collective-permute-start(f32[80,64]{0,1:T(8,128)} %bitcast.633), channel_id=1, source_target_pairs={{0,8},{1,9},{2,10},{3,11},{4,12},{5,13},{6,14},{7,15},{8,16},{9,17... | collective-permute-start | bytes 61448 | tf_op jit(solution)/shard_map/ppermute | solution.py:19
  973.7 20.9 %collective-permute-start.56 = (f32[80,64]{0,1:T(8,128)}, f32[80,64]{0,1:T(8,128)S(1)}, u32[]{:S(2)}, u32[]{:S(2)}) collective-permute-start(f32[80,64]{0,1:T(8,128)} %bitcast.632), channel_id=1, source_target_pairs={{0,9},{1,10},{2,11},{3,12},{4,13},{5,14},{6,15},{7,16},{8,17},{9,1... | collective-permute-start | bytes 61448 | tf_op jit(solution)/shard_map/ppermute | solution.py:19
  977.9 21.4 %collective-permute-start.57 = (f32[80,64]{0,1:T(8,128)}, f32[80,64]{0,1:T(8,128)S(1)}, u32[]{:S(2)}, u32[]{:S(2)}) collective-permute-start(f32[80,64]{0,1:T(8,128)} %bitcast.631), channel_id=1, source_target_pairs={{0,10},{1,11},{2,12},{3,13},{4,14},{5,15},{6,16},{7,17},{8,18},{9,... | collective-permute-start | bytes 61448 | tf_op jit(solution)/shard_map/ppermute | solution.py:19
  983.8 21.1 %collective-permute-start.58 = (f32[80,64]{0,1:T(8,128)}, f32[80,64]{0,1:T(8,128)S(1)}, u32[]{:S(2)}, u32[]{:S(2)}) collective-permute-start(f32[80,64]{0,1:T(8,128)} %bitcast.630), channel_id=1, source_target_pairs={{0,11},{1,12},{2,13},{3,14},{4,15},{5,16},{6,17},{7,18},{8,19},{9,... | collective-permute-start | bytes 61448 | tf_op jit(solution)/shard_map/ppermute | solution.py:19
  986.9 24.7 %collective-permute-start.59 = (f32[80,64]{0,1:T(8,128)}, f32[80,64]{0,1:T(8,128)S(1)}, u32[]{:S(2)}, u32[]{:S(2)}) collective-permute-start(f32[80,64]{0,1:T(8,128)} %bitcast.629), channel_id=1, source_target_pairs={{0,12},{1,13},{2,14},{3,15},{4,16},{5,17},{6,18},{7,19},{8,20},{9,... | collective-permute-start | bytes 61448 | tf_op jit(solution)/shard_map/ppermute | solution.py:19
  991.4 21.6 %collective-permute-start.60 = (f32[80,64]{0,1:T(8,128)}, f32[80,64]{0,1:T(8,128)S(1)}, u32[]{:S(2)}, u32[]{:S(2)}) collective-permute-start(f32[80,64]{0,1:T(8,128)} %bitcast.628), channel_id=1, source_target_pairs={{0,13},{1,14},{2,15},{3,16},{4,17},{5,18},{6,19},{7,20},{8,21},{9,... | collective-permute-start | bytes 61448 | tf_op jit(solution)/shard_map/ppermute | solution.py:19
  994.5 22.1 %collective-permute-start.61 = (f32[80,64]{0,1:T(8,128)S(1)}, f32[80,64]{0,1:T(8,128)S(1)}, u32[]{:S(2)}, u32[]{:S(2)}) collective-permute-start(f32[80,64]{0,1:T(8,128)S(1)} %bitcast.627), channel_id=1, source_target_pairs={{0,14},{1,15},{2,16},{3,17},{4,18},{5,19},{6,20},{7,21},{8,22},{9,... | collective-permute-start | bytes 61448 | tf_op jit(solution)/shard_map/ppermute | solution.py:19
  999.4 19.6 %collective-permute-start.62 = (f32[80,64]{0,1:T(8,128)S(1)}, f32[80,64]{0,1:T(8,128)S(1)}, u32[]{:S(2)}, u32[]{:S(2)}) collective-permute-start(f32[80,64]{0,1:T(8,128)S(1)} %bitcast.626), channel_id=1, source_target_pairs={{0,15},{1,16},{2,17},{3,18},{4,19},{5,20},{6,21},{7,22},{8,23},{9,... | collective-permute-start | bytes 61448 | tf_op jit(solution)/shard_map/ppermute | solution.py:19
  1005.0 15.4 %collective-permute-start.63 = (f32[80,64]{0,1:T(8,128)S(1)}, f32[80,64]{0,1:T(8,128)S(1)}, u32[]{:S(2)}, u32[]{:S(2)}) collective-permute-start(f32[80,64]{0,1:T(8,128)S(1)} %bitcast.625), channel_id=1, source_target_pairs={{0,16},{1,17},{2,18},{3,19},{4,20},{5,21},{6,22},{7,23},{8,24},{9,... | collective-permute-start | bytes 61448 | tf_op jit(solution)/shard_map/ppermute | solution.py:19
  1011.6 10.4 collective-permute-start.64
  1013.0 11.3 collective-permute-start.65
  1038.1 10.2 collective-permute-start.78
  1039.6 10.0 collective-permute-start.79
  1040.9 10.0 collective-permute-start.80
  1042.2 10.0 collective-permute-start.81
  1052.3 37.7 %collective-permute-start.86 = (f32[80,64]{0,1:T(8,128)S(1)}, f32[80,64]{0,1:T(8,128)S(1)}, u32[]{:S(2)}, u32[]{:S(2)}) collective-permute-start(f32[80,64]{0,1:T(8,128)S(1)} %bitcast.602), channel_id=1, source_target_pairs={{10,0},{11,1},{12,2},{13,3},{14,4},{15,5},{16,6},{17,7},{18,8},{19... | collective-permute-start | bytes 61448 | tf_op jit(solution)/shard_map/ppermute | solution.py:19
  1053.6 46.5 %collective-permute-start.87 = (f32[80,64]{0,1:T(8,128)S(1)}, f32[80,64]{0,1:T(8,128)S(1)}, u32[]{:S(2)}, u32[]{:S(2)}) collective-permute-start(f32[80,64]{0,1:T(8,128)S(1)} %bitcast.601), channel_id=1, source_target_pairs={{9,0},{10,1},{11,2},{12,3},{13,4},{14,5},{15,6},{16,7},{17,8},{18,... | collective-permute-start | bytes 61448 | tf_op jit(solution)/shard_map/ppermute | solution.py:19
  1054.9 55.4 %collective-permute-start.88 = (f32[80,64]{0,1:T(8,128)S(1)}, f32[80,64]{0,1:T(8,128)S(1)}, u32[]{:S(2)}, u32[]{:S(2)}) collective-permute-start(f32[80,64]{0,1:T(8,128)S(1)} %bitcast.600), channel_id=1, source_target_pairs={{8,0},{9,1},{10,2},{11,3},{12,4},{13,5},{14,6},{15,7},{16,8},{17,9... | collective-permute-start | bytes 61448 | tf_op jit(solution)/shard_map/ppermute | solution.py:19
  1056.3 64.3 %collective-permute-start.89 = (f32[80,64]{0,1:T(8,128)S(1)}, f32[80,64]{0,1:T(8,128)S(1)}, u32[]{:S(2)}, u32[]{:S(2)}) collective-permute-start(f32[80,64]{0,1:T(8,128)S(1)} %bitcast.599), channel_id=1, source_target_pairs={{7,0},{8,1},{9,2},{10,3},{11,4},{12,5},{13,6},{14,7},{15,8},{16,9}... | collective-permute-start | bytes 61448 | tf_op jit(solution)/shard_map/ppermute | solution.py:19
  1059.0 71.8 %collective-permute-start.90 = (f32[80,64]{0,1:T(8,128)S(1)}, f32[80,64]{0,1:T(8,128)S(1)}, u32[]{:S(2)}, u32[]{:S(2)}) collective-permute-start(f32[80,64]{0,1:T(8,128)S(1)} %bitcast.598), channel_id=1, source_target_pairs={{6,0},{7,1},{8,2},{9,3},{10,4},{11,5},{12,6},{13,7},{14,8},{15,9},... | collective-permute-start | bytes 61448 | tf_op jit(solution)/shard_map/ppermute | solution.py:19
  1090.0 51.1 %collective-permute-start.91 = (f32[80,64]{0,1:T(8,128)S(1)}, f32[80,64]{0,1:T(8,128)S(1)}, u32[]{:S(2)}, u32[]{:S(2)}) collective-permute-start(f32[80,64]{0,1:T(8,128)S(1)} %bitcast.597), channel_id=1, source_target_pairs={{5,0},{6,1},{7,2},{8,3},{9,4},{10,5},{11,6},{12,7},{13,8},{14,9},{... | collective-permute-start | bytes 61448 | tf_op jit(solution)/shard_map/ppermute | solution.py:19
  1100.2 40.9 %collective-permute-start.92 = (f32[80,64]{0,1:T(8,128)S(1)}, f32[80,64]{0,1:T(8,128)S(1)}, u32[]{:S(2)}, u32[]{:S(2)}) collective-permute-start(f32[80,64]{0,1:T(8,128)S(1)} %bitcast.596), channel_id=1, source_target_pairs={{4,0},{5,1},{6,2},{7,3},{8,4},{9,5},{10,6},{11,7},{12,8},{13,9},{1... | collective-permute-start | bytes 61448 | tf_op jit(solution)/shard_map/ppermute | solution.py:19
  1110.4 30.7 %collective-permute-start.93 = (f32[80,64]{0,1:T(8,128)S(1)}, f32[80,64]{0,1:T(8,128)S(1)}, u32[]{:S(2)}, u32[]{:S(2)}) collective-permute-start(f32[80,64]{0,1:T(8,128)S(1)} %bitcast.595), channel_id=1, source_target_pairs={{3,0},{4,1},{5,2},{6,3},{7,4},{8,5},{9,6},{10,7},{11,8},{12,9},{13... | collective-permute-start | bytes 61448 | tf_op jit(solution)/shard_map/ppermute | solution.py:19
  1120.6 20.5 %collective-permute-start.94 = (f32[80,64]{0,1:T(8,128)S(1)}, f32[80,64]{0,1:T(8,128)S(1)}, u32[]{:S(2)}, u32[]{:S(2)}) collective-permute-start(f32[80,64]{0,1:T(8,128)S(1)} %bitcast.594), channel_id=1, source_target_pairs={{2,0},{3,1},{4,2},{5,3},{6,4},{7,5},{8,6},{9,7},{10,8},{11,9},{12,... | collective-permute-start | bytes 61448 | tf_op jit(solution)/shard_map/ppermute | solution.py:19
  1130.8 13.8 collective-permute-start.95
  (139 other events, 6417.2 us)
where the time goes:
time: 1420 us; the launch traced here: 1390 us
  local copies, waits for them, and re-layouts  785 us (55%)
  starting transfers between devices  446 us (31%)
  blocking collectives  76.9 us (5%)
  other arithmetic  56.2 us (4%)
  waiting for transfers between devices  22.3 us (2%)
    ppermute x96, starting transfers between devices, passed_along(): lax.ppermute(value, axis, [(source, source + steps) for source in range(i...  446 us
    gather x2, local copies, waits for them, and re-layouts, on_device(): master_star = jnp.take(star_master, remote_at, axis=3)  145 us
    gather x2, local copies, waits for them, and re-layouts, on_device(): slave_star = -orient(jnp.take(returned, remote_at, axis=3), flip_code)  144 us
    dynamic_slice x51, local copies, waits for them, and re-layouts, pick_slab(): return lax.dynamic_index_in_dim(buffer, target, 1, keepdims=False)  82.1 us
    pmax x1, blocking collectives, on_device(): top_speed = lax.pmax(jnp.max(node_speed(solution)), ('sfc', 'sub'))  76.9 us
    reshape x2, local copies, waits for them, and re-layouts, on_device(): returned = deliver_fluxes(outbound).reshape(4, 4, 5, slot_count)  50.1 us
    rev x3, local copies, waits for them, and re-layouts, orient(): trace = jnp.where(flip_second, trace[:, ::-1], trace)  48.2 us
    gather x1, local copies, waits for them, and re-layouts, on_device(): jnp.take(flip_code, owner_column)  45.5 us
  transfers between devices with their start and end apart: 96, of which 14 were waited for; matrix products, arithmetic and copies ran while one was open for 28% of the time, Pallas kernels for 0%

commit v1 on v0

v1 whole, which is shorter than its diff:
```python
import jax
import jax.numpy as jnp
import numpy as np
from jax import lax
from jax.experimental import pallas as pl
from jax.experimental.pallas import tpu as pltpu
from jax.sharding import PartitionSpec as P

HEAT_RATIO = 1.4
LIFT_FACTOR = 6.0
CFL_NUMBER = 0.3
SECTION_KEEP = -0.4178904745
SECTION_STEP = 0.4432226
DEVICES = 128
ELEMENTS = 512
COLUMNS = 6 * ELEMENTS
SLOTS = 64
REACH = 24
LANES = 128
BLOCKS = ELEMENTS // LANES
TRACE = 80
MESSAGE = TRACE * SLOTS // LANES
UNROLL = 16
AXES = ("sfc", "sub")
VMEM_LIMIT = 48 * 1024 * 1024


def derivative_matrix():
    points = np.array([-1.0, -1.0 / np.sqrt(5.0), 1.0 / np.sqrt(5.0), 1.0])
    weights = np.array(
        [
            1.0
            / np.prod([points[target] - points[source] for source in range(4) if source != target])
            for target in range(4)
        ]
    )
    matrix = np.zeros((4, 4))
    for target in range(4):
        for source in range(4):
            if target != source:
                matrix[target, source] = (
                    weights[source] / weights[target] / (points[target] - points[source])
                )
        matrix[target, target] = -np.sum(matrix[target])
    return matrix


def face_nodes(face):
    side = 3 * (face % 2)
    if face < 2:
        return [side * 16 + i * 4 + j for i in range(4) for j in range(4)]
    if face < 4:
        return [i * 16 + side * 4 + j for i in range(4) for j in range(4)]
    return [i * 16 + j * 4 + side for i in range(4) for j in range(4)]


def spread_variables(state_ref, rows_ref):
    for node in range(64):
        for block in range(BLOCKS):
            rows_ref[pl.ds(node * BLOCKS + block, 5, stride=64 * BLOCKS), :] = state_ref[
                node, :, block * LANES : (block + 1) * LANES
            ]


def lane_index(shape):
    return lax.broadcasted_iota(jnp.int32, shape, 1)


def compact(rows):
    lane = lane_index((8, LANES))
    low = lane < 80
    mid = lane < 112

    def turn(value, shift):
        return pltpu.roll(value, shift, 1)

    first = [jnp.where(low, rows[k], turn(rows[5 + k], 80)) for k in range(3)]
    fourth = jnp.where(low, rows[3], jnp.where(mid, turn(rows[5], 32), turn(rows[7], 64)))
    fifth = jnp.where(low, rows[4], jnp.where(mid, turn(rows[6], 32), turn(rows[7], 48)))
    return first + [fourth, fifth]


def expand(parts):
    lane = lane_index((8, LANES))
    head = lane < 48
    body = lane < 64

    def turn(value, shift):
        return pltpu.roll(value, shift, 1)

    sixth = jnp.where(head, turn(parts[0], 48), turn(parts[3], 96))
    seventh = jnp.where(head, turn(parts[1], 48), turn(parts[4], 96))
    eighth = jnp.where(
        head, turn(parts[2], 48), jnp.where(body, turn(parts[3], 64), turn(parts[4], 80))
    )
    return list(parts) + [sixth, seventh, eighth]


def pack_kernel(rank_ref, partner_ref, state_ref, own_ref, table_ref, send_ref, rows_ref, board_ref):
    spread_variables(state_ref, rows_ref)
    for face in range(6):
        nodes = face_nodes(face)
        for block in range(BLOCKS):
            pieces = [state_ref[n, :, block * LANES : (block + 1) * LANES] for n in nodes]
            trace = jnp.concatenate(pieces, axis=0)
            place = face * BLOCKS + block
            own_ref[place * TRACE : (place + 1) * TRACE, :] = trace
            square = jnp.concatenate([trace, jnp.zeros((LANES - TRACE, LANES), jnp.float32)], axis=0)
            table_ref[place * LANES : (place + 1) * LANES, :] = square.T

    def scatter(step, carry):
        base = step * UNROLL
        for k in range(UNROLL):
            board_ref[pl.ds(partner_ref[base + k], 1), :] = table_ref[pl.ds(base + k, 1), :]
        return carry

    lax.fori_loop(0, COLUMNS // UNROLL, scatter, 0)

    def speeds(step, best):
        density, mom_x, mom_y, mom_z, energy = [
            rows_ref[pl.ds(pl.multiple_of(v * 256 + step * 64, 64), 64), :] for v in range(5)
        ]
        inverse = 1.0 / density
        square = (mom_x * mom_x + mom_y * mom_y + mom_z * mom_z) * inverse
        pressure = (HEAT_RATIO - 1.0) * (energy - 0.5 * square)
        wave = jnp.sqrt(square * inverse) + jnp.sqrt(HEAT_RATIO * pressure * inverse)
        return jnp.maximum(best, jnp.max(wave.reshape(8, 8, LANES), axis=0))

    best = lax.fori_loop(0, 4, speeds, jnp.zeros((8, LANES), jnp.float32))
    top = jnp.full((8, LANES), jnp.max(best), jnp.float32)
    rank = rank_ref[0]

    def fill(peer, carry):
        send_ref[peer, MESSAGE:, :] = top
        return carry

    lax.fori_loop(0, DEVICES, fill, 0)

    def message(peer, carry):
        base = pl.multiple_of(COLUMNS + peer * SLOTS, SLOTS)
        parts = compact([board_ref[pl.ds(base + 8 * k, 8), :] for k in range(8)])
        for k in range(5):
            send_ref[peer, 8 * k : 8 * k + 8, :] = parts[k]
        return carry

    lax.fori_loop(
        jnp.maximum(rank - REACH, 0), jnp.minimum(rank + REACH + 1, DEVICES), message, 0
    )


def volume_kernel(state_ref, metric_ref, rate_ref, rows_ref, tensor_ref, flux_ref):
    spread_variables(state_ref, rows_ref)
    for direction in range(3):
        for half in range(2):
            for block in range(BLOCKS):
                tensor_ref[pl.ds(direction * 24 + half * 4 + block, 3, stride=8), :] = metric_ref[
                    direction, :, block * LANES : (block + 1) * LANES
                ]

    def fluxes(step, carry):
        at = pl.multiple_of(step * 8, 8)
        density, mom_x, mom_y, mom_z, energy = [
            rows_ref[pl.ds(v * 256 + at, 8), :] for v in range(5)
        ]
        inverse = 1.0 / density
        momentum = [mom_x, mom_y, mom_z]
        velocity = [m * inverse for m in momentum]
        pressure = (HEAT_RATIO - 1.0) * (
            energy
            - 0.5 * (mom_x * velocity[0] + mom_y * velocity[1] + mom_z * velocity[2])
        )
        enthalpy = energy + pressure
        for direction in range(3):
            tensor = [tensor_ref[direction * 24 + k * 8 : direction * 24 + k * 8 + 8, :] for k in range(3)]
            along = tensor[0] * velocity[0] + tensor[1] * velocity[1] + tensor[2] * velocity[2]
            values = [density * along]
            values += [momentum[k] * along + pressure * tensor[k] for k in range(3)]
            values += [enthalpy * along]
            for v in range(5):
                flux_ref[direction, pl.ds(v * 256 + at, 8), :] = values[v]
        return carry

    lax.fori_loop(0, 32, fluxes, 0)
    matrix = derivative_matrix()
    upper = lax.broadcasted_iota(jnp.int32, (8, LANES), 0) < 4

    def pair(first, second):
        return jnp.where(upper, jnp.float32(first), jnp.float32(second))

    straight = [[pair(matrix[2 * t, 2 * s], matrix[2 * t + 1, 2 * s + 1]) for s in range(2)] for t in range(2)]
    crossed = [[pair(matrix[2 * t, 2 * s + 1], matrix[2 * t + 1, 2 * s]) for s in range(2)] for t in range(2)]

    def combine(values, target):
        total = values[0] * float(matrix[target, 0])
        for source in range(1, 4):
            total = total + values[source] * float(matrix[target, source])
        return total

    def diverge(v, carry):
        base = pl.multiple_of(v * 256, 256)
        for rest in range(8):
            values = [flux_ref[0, pl.ds(base + a * 64 + rest * 8, 8), :] for a in range(4)]
            for a in range(4):
                rate_ref[pl.ds(base + a * 64 + rest * 8, 8), :] = -combine(values, a)
        for a in range(4):
            for half in range(2):
                values = [flux_ref[1, pl.ds(base + a * 64 + b * 16 + half * 8, 8), :] for b in range(4)]
                third = [flux_ref[2, pl.ds(base + a * 64 + b * 16 + half * 8, 8), :] for b in range(4)]
                other = [flux_ref[2, pl.ds(base + a * 64 + b * 16 + (1 - half) * 8, 8), :] for b in range(4)]
                for b in range(4):
                    at = pl.ds(base + a * 64 + b * 16 + half * 8, 8)
                    same, far = third[b], other[b]
                    total = combine(values, b)
                    total = total + straight[half][half] * same
                    total = total + crossed[half][half] * pltpu.roll(same, 4, 0)
                    total = total + straight[half][1 - half] * far
                    total = total + crossed[half][1 - half] * pltpu.roll(far, 4, 0)
                    rate_ref[at, :] = rate_ref[at, :] - total
        return carry

    lax.fori_loop(0, 5, diverge, 0)


def normal_flux(values, normal, length):
    density, momentum, energy = values[0], values[1:4], values[4]
    inverse = 1.0 / density
    velocity = [m * inverse for m in momentum]
    pressure = (HEAT_RATIO - 1.0) * (
        energy
        - 0.5 * (momentum[0] * velocity[0] + momentum[1] * velocity[1] + momentum[2] * velocity[2])
    )
    speed = velocity[0] * normal[0] + velocity[1] * normal[1] + velocity[2] * normal[2]
    terms = [density * speed]
    terms += [momentum[k] * speed + pressure * normal[k] for k in range(3)]
    terms += [(energy + pressure) * speed]
    wave = jnp.abs(speed) + jnp.sqrt(HEAT_RATIO * pressure * inverse) * length
    return terms, wave


def finish_kernel(
    rank_ref,
    partner_ref,
    table_ref,
    own_ref,
    got_ref,
    code_ref,
    normal_ref,
    rate_in_ref,
    state_ref,
    register_ref,
    section_ref,
    advanced_ref,
    board_ref,
    picked_ref,
    other_ref,
    turned_ref,
    side_ref,
    rate_ref,
):
    rank = rank_ref[0]
    board_ref[0:COLUMNS, :] = table_ref[...]
    rate_ref[...] = rate_in_ref[...]

    def message(peer, carry):
        base = pl.multiple_of(COLUMNS + peer * SLOTS, SLOTS)
        rows = expand([got_ref[peer, 8 * k : 8 * k + 8, :] for k in range(5)])
        for k in range(8):
            board_ref[pl.ds(base + 8 * k, 8), :] = rows[k]
        return carry

    lax.fori_loop(
        jnp.maximum(rank - REACH, 0), jnp.minimum(rank + REACH + 1, DEVICES), message, 0
    )

    def gather(step, carry):
        base = step * UNROLL
        for k in range(UNROLL):
            picked_ref[pl.ds(base + k, 1), :] = board_ref[pl.ds(partner_ref[base + k], 1), :]
        return carry

    lax.fori_loop(0, COLUMNS // UNROLL, gather, 0)
    for place in range(COLUMNS // LANES):
        square = picked_ref[place * LANES : (place + 1) * LANES, :].T
        other_ref[place * TRACE : (place + 1) * TRACE, :] = square[0:TRACE]
        side_ref[pl.ds(place, 3, stride=24), :] = normal_ref[:, place * LANES : (place + 1) * LANES]

    for group in range(3):
        code = code_ref[group * 8 : group * 8 + 8, :]
        flip_first = code % 2 == 1
        flip_second = (code // 2) % 2 == 1
        swapped = code >= 4
        start = group * 8 * TRACE
        for v in range(5):
            grid = [
                [other_ref[pl.ds(start + (i * 4 + j) * 5 + v, 8, stride=TRACE), :] for j in range(4)]
                for i in range(4)
            ]
            grid = [[jnp.where(flip_first, grid[3 - i][j], grid[i][j]) for j in range(4)] for i in range(4)]
            grid = [[jnp.where(flip_second, grid[i][3 - j], grid[i][j]) for j in range(4)] for i in range(4)]
            for i in range(4):
                for j in range(4):
                    value = grid[i][j] if i == j else jnp.where(swapped, grid[j][i], grid[i][j])
                    at = ((i * 4 + j) * 5 + v) * 8
                    turned_ref[at : at + 8, :] = value
        normal = [side_ref[k * 24 + group * 8 : k * 24 + group * 8 + 8, :] for k in range(3)]
        length = jnp.sqrt(normal[0] * normal[0] + normal[1] * normal[1] + normal[2] * normal[2])
        first_nodes = face_nodes(2 * group)
        second_nodes = face_nodes(2 * group + 1)
        for node in range(16):
            own = [own_ref[pl.ds(start + node * 5 + v, 8, stride=TRACE), :] for v in range(5)]
            far = [turned_ref[(node * 5 + v) * 8 : (node * 5 + v) * 8 + 8, :] for v in range(5)]
            own_terms, own_wave = normal_flux(own, normal, length)
            far_terms, far_wave = normal_flux(far, normal, length)
            bound = jnp.maximum(own_wave, far_wave)
            viscous = bound + length
            for v in range(5):
                weight = bound if v == 0 else viscous
                surface = (0.5 * LIFT_FACTOR) * (
                    own_terms[v] - far_terms[v] + weight * (far[v] - own[v])
                )
                at = v * 256 + first_nodes[node] * 4
                rate_ref[at : at + 4, :] = rate_ref[at : at + 4, :] + surface[0:4]
                at = v * 256 + second_nodes[node] * 4
                rate_ref[at : at + 4, :] = rate_ref[at : at + 4, :] + surface[4:8]

    top = jnp.max(jnp.max(got_ref[:, MESSAGE:, :], axis=0))
    scale = CFL_NUMBER / top * SECTION_STEP

    def update(node, carry):
        for block in range(BLOCKS):
            lanes = slice(block * LANES, (block + 1) * LANES)
            rate = rate_ref[pl.ds(node * BLOCKS + block, 5, stride=64 * BLOCKS), :]
            section = SECTION_KEEP * register_ref[node, :, lanes] + rate
            section_ref[node, :, lanes] = section
            advanced_ref[node, :, lanes] = state_ref[node, :, lanes] + scale * section
        return carry

    lax.fori_loop(0, 64, update, 0)


def smem():
    return pl.BlockSpec(memory_space=pltpu.SMEM)


def vmem():
    return pl.BlockSpec(memory_space=pltpu.VMEM)


def params():
    return pltpu.CompilerParams(vmem_limit_bytes=VMEM_LIMIT)


def shape(*sizes):
    return jax.ShapeDtypeStruct(sizes, jnp.float32)


def scratch(*sizes):
    return pltpu.VMEM(sizes, jnp.float32)


def pack(rank, partner, state):
    return pl.pallas_call(
        pack_kernel,
        out_shape=(
            shape(COLUMNS // LANES * TRACE, LANES),
            shape(COLUMNS, LANES),
            shape(DEVICES, MESSAGE + 8, LANES),
        ),
        in_specs=[smem(), smem(), vmem()],
        out_specs=(vmem(), vmem(), vmem()),
        scratch_shapes=[scratch(1280, LANES), scratch(COLUMNS + DEVICES * SLOTS, LANES)],
        compiler_params=params(),
        name="pack",
    )(rank, partner, state)


def volume(state, metric):
    return pl.pallas_call(
        volume_kernel,
        out_shape=shape(1280, LANES),
        in_specs=[vmem(), vmem()],
        out_specs=vmem(),
        scratch_shapes=[scratch(1280, LANES), scratch(72, LANES), scratch(3, 1280, LANES)],
        compiler_params=params(),
        name="volume",
    )(state, metric)


def finish(rank, partner, table, own, got, code, normal, rate, state, register):
    return pl.pallas_call(
        finish_kernel,
        out_shape=(shape(64, 5, ELEMENTS), shape(64, 5, ELEMENTS)),
        in_specs=[smem(), smem()] + [vmem()] * 8,
        out_specs=(vmem(), vmem()),
        scratch_shapes=[
            scratch(COLUMNS + DEVICES * SLOTS, LANES),
            scratch(COLUMNS, LANES),
            scratch(COLUMNS // LANES * TRACE, LANES),
            scratch(16 * 5 * 8, LANES),
            scratch(72, LANES),
            scratch(1280, LANES),
        ],
        compiler_params=params(),
        name="finish",
    )(rank, partner, table, own, got, code, normal, rate, state, register)


def on_device(state, register, metric, face_normal, partner, flip_code, face_role, send_face):
    rank = lax.axis_index(AXES).astype(jnp.int32)[None]
    own, table, send = pack(rank, partner, state)
    rate = volume(state, metric)
    got = lax.all_to_all(send, AXES, 0, 0, tiled=True)
    code = flip_code.reshape(COLUMNS // LANES, LANES)
    return finish(rank, partner, table, own, got, code, face_normal, rate, state, register)


def solution(mesh):
    placed = (
        P(None, None, AXES),
        P(None, None, AXES),
        P(None, None, AXES),
        P(None, AXES),
        P(AXES),
        P(AXES),
        P(AXES),
        P(AXES, None, None),
    )
    return jax.shard_map(
        on_device,
        mesh=mesh,
        in_specs=placed,
        out_specs=(P(None, None, AXES), P(None, None, AXES)),
        check_vma=False,
    )
```

time: 1420 us -> 84.8 us (0.06)
  the two profiles are of different devices: /device:TPU:0 before, /device:TPU:1 now
where the time goes in v1:
time: 84.8 us; the launch traced here: 84.5 us
  waiting for transfers between devices  39.8 us (47%)
  Pallas kernels  22.1 us (26%)
  starting transfers between devices  13.4 us (16%)
  local copies, waits for them, and re-layouts  8.45 us (10%)
    all_to_all x1, waiting for transfers between devices, on_device(): got = lax.all_to_all(send, AXES, 0, 0, tiled=True)  39.8 us
    all_to_all x1, starting transfers between devices, on_device(): got = lax.all_to_all(send, AXES, 0, 0, tiled=True)  13.4 us
    pallas_call x1, Pallas kernels, finish(): pl.pallas_call(finish_kernel, out_shape=(shape(64, 5, ELEMENTS), shape(64...  10.7 us
    pallas_call x1, Pallas kernels, pack(): pl.pallas_call(pack_kernel, out_shape=(shape(COLUMNS // LANES * TRACE, LA...  9.69 us
    unnamed x20, local copies, waits for them, and re-layouts  6.01 us
    pallas_call x2, local copies, waits for them, and re-layouts, finish(): pl.pallas_call(finish_kernel, out_shape=(shape(64, 5, ELEMENTS), shape(64...  2.44 us
  transfers between devices with their start and end apart: 1, of which 1 were waited for; matrix products, arithmetic and copies ran while one was open for 0% of the time, Pallas kernels for 2%

profile of v1, /device:TPU:1, one launch (start us, length us, event | category | flops | bytes accessed | tf_op | source)
XLA Modules:
  0.0 84.5 jit_solution(12123868719460447654)
XLA Ops:
  0.6 1.5 %copy.8.state_ref = f32[64,5,512]{2,1,0:T(8,128)S(1)} copy(f32[64,5,512]{2,0,1:T(8,128)} %param.8) | data formatting | bytes 1310720 | tf_op args[0]
  2.1 0.0 copy-start.4
  2.2 0.7 copy-done.4
  2.8 9.7 %pack.1 = (f32[1920,128]{1,0:T(8,128)S(1)}, f32[3072,128]{1,0:T(8,128)S(1)}, f32[128,48,128]{2,1,0:T(8,128)}) custom-call(s32[1]{0:T(128)} %bitcast.rank_ref, s32[3072]{0:T(1024)S(1)} %copy-done.4, f32[64,5,512]{2,1,0:T(8,128)S(1)} %copy.8.state_ref), custom_call_target="tpu_custom_call" | custom-call | tf_op jit(solution)/shard_map/pack/pallas_call | solution.py:362
  12.5 0.0 copy-start
  12.5 1.1 %copy-done = f32[3072,128]{1,0:T(8,128)} copy-done((f32[3072,128]{1,0:T(8,128)}, f32[3072,128]{1,0:T(8,128)S(1)}, u32[]{:S(2)}) %copy-start) | copy-done | bytes 1572888
  13.7 0.0 copy-start.1
  13.7 1.0 %copy-done.1 = f32[1920,128]{1,0:T(8,128)} copy-done((f32[1920,128]{1,0:T(8,128)}, f32[1920,128]{1,0:T(8,128)S(1)}, u32[]{:S(2)}) %copy-start.1) | copy-done | bytes 983064
  14.7 0.0 copy-start.6
  14.7 0.0 copy-start.8
  14.7 13.4 %all-to-all-start = ((f32[128,48,128]{2,1,0:T(8,128)}), f32[128,48,128]{2,1,0:T(8,128)}, u32[]{:S(2)}, u32[]{:S(2)}) async-start(f32[128,48,128]{2,1,0:T(8,128)} %get-tuple-element.7), calls=%async_computation | async-start | bytes 6291456 | tf_op jit(solution)/shard_map/all_to_all | solution.py:412
  28.2 0.0 copy-done.6
  28.2 0.0 copy-start.3
  28.2 0.0 copy-start.5
  28.2 0.0 copy-start.7
  28.2 1.7 %volume.1.rate_in_ref = f32[1280,128]{1,0:T(8,128)S(1)} custom-call(f32[64,5,512]{2,1,0:T(8,128)S(1)} %copy.8.state_ref, f32[3,3,512]{2,1,0:T(4,128)S(1)} %copy-done.6), custom_call_target="tpu_custom_call" | custom-call | tf_op jit(solution)/shard_map/volume/pallas_call | solution.py:378
  29.9 0.0 copy-done.8
  29.9 0.4 copy.11.register_ref
  30.3 39.8 %all-to-all-done.got_ref = f32[128,48,128]{2,1,0:T(8,128)} async-done(((f32[128,48,128]{2,1,0:T(8,128)}), f32[128,48,128]{2,1,0:T(8,128)}, u32[]{:S(2)}, u32[]{:S(2)}) %all-to-all-start) | async-done | bytes 3145760 | tf_op jit(solution)/shard_map/all_to_all | solution.py:412
  70.1 0.0 copy-done.3
  70.1 0.0 copy-done.5
  70.1 0.0 copy-done.7
  70.1 0.0 copy-start.2
  70.1 1.2 %copy-done.2 = f32[1920,128]{1,0:T(8,128)S(1)} copy-done((f32[1920,128]{1,0:T(8,128)S(1)}, f32[1920,128]{1,0:T(8,128)}, u32[]{:S(2)}) %copy-start.2) | copy-done | bytes 983064
  71.3 10.7 %finish.1 = (f32[64,5,512]{2,1,0:T(8,128)S(1)}, f32[64,5,512]{2,1,0:T(8,128)S(1)}) custom-call(s32[1]{0:T(128)} %bitcast.rank_ref, s32[3072]{0:T(1024)S(1)} %copy-done.5, f32[3072,128]{1,0:T(8,128)} %copy-done, f32[1920,128]{1,0:T(8,128)S(1)} %copy-done.2, f32[128,48,128]{2,1,0:T(8,128)} %all-to-all-done.got_ref, s32[24,128]{1,0:T(8,128)S(1)} %bitcast.2, ...), custom_call_target="tpu_custom_call" | custom-call | tf_op jit(solution)/shard_map/finish/pallas_call | solution.py:390
  82.0 1.2 %copy.12 = f32[64,5,512]{2,0,1:T(8,128)} copy(f32[64,5,512]{2,1,0:T(8,128)S(1)} %get-tuple-element.8) | data formatting | bytes 1310720 | tf_op jit(solution)/shard_map/finish/pallas_call | solution.py:390
  83.2 1.2 %copy.13 = f32[64,5,512]{2,0,1:T(8,128)} copy(f32[64,5,512]{2,1,0:T(8,128)S(1)} %get-tuple-element.9) | data formatting | bytes 1310720 | tf_op jit(solution)/shard_map/finish/pallas_call | solution.py:390
Async XLA Ops:
  2.1 0.7 copy-start.4
  12.5 1.1 %copy-start = (f32[3072,128]{1,0:T(8,128)}, f32[3072,128]{1,0:T(8,128)S(1)}, u32[]{:S(2)}) copy-start(f32[3072,128]{1,0:T(8,128)S(1)} %get-tuple-element.5.table_ref) | copy-start | bytes 4718596
  13.7 1.0 %copy-start.1 = (f32[1920,128]{1,0:T(8,128)}, f32[1920,128]{1,0:T(8,128)S(1)}, u32[]{:S(2)}) copy-start(f32[1920,128]{1,0:T(8,128)S(1)} %get-tuple-element.6.own_ref) | copy-start | bytes 2949124
  14.7 13.4 %copy-start.6 = (f32[3,3,512]{2,1,0:T(4,128)S(1)}, f32[3,3,512]{2,1,0:T(4,128)}, u32[]{:S(2)}) copy-start(f32[3,3,512]{2,1,0:T(4,128)} %metric_ref.1) | copy-start | bytes 55300
  14.7 15.2 %copy-start.8 = (f32[64,5,512]{2,0,1:T(8,128)S(1)}, f32[64,5,512]{2,0,1:T(8,128)}, u32[]{:S(2)}) copy-start(f32[64,5,512]{2,0,1:T(8,128)} %param.9) | copy-start | bytes 1966084
  14.7 55.4 %all-to-all-start = ((f32[128,48,128]{2,1,0:T(8,128)}), f32[128,48,128]{2,1,0:T(8,128)}, u32[]{:S(2)}, u32[]{:S(2)}) async-start(f32[128,48,128]{2,1,0:T(8,128)} %get-tuple-element.7), calls=%async_computation | async-start | bytes 6291456 | tf_op jit(solution)/shard_map/all_to_all | solution.py:412
  28.2 41.9 %copy-start.3 = (f32[3,3072]{1,0:T(4,128)S(1)}, f32[3,3072]{1,0:T(4,128)}, u32[]{:S(2)}) copy-start(f32[3,3072]{1,0:T(4,128)} %normal_ref.1) | copy-start | bytes 110596
  28.2 41.9 %copy-start.5 = (s32[3072]{0:T(1024)S(1)}, s32[3072]{0:T(1024)}, u32[]{:S(2)}) copy-start(s32[3072]{0:T(1024)} %partner_ref.3) | copy-start | bytes 36868
  28.2 41.9 %copy-start.7 = (s32[3072]{0:T(1024)S(1)}, s32[3072]{0:T(1024)}, u32[]{:S(2)}) copy-start(s32[3072]{0:T(1024)} %param.13) | copy-start | bytes 36868
  70.1 1.2 %copy-start.2 = (f32[1920,128]{1,0:T(8,128)S(1)}, f32[1920,128]{1,0:T(8,128)}, u32[]{:S(2)}) copy-start(f32[1920,128]{1,0:T(8,128)} %copy-done.1) | copy-start | bytes 2949124

commit v2 on v1

--- a/solution.py
+++ b/solution.py
@@ -4,6 +4,7 @@
 from jax import lax
 from jax.experimental import pallas as pl
 from jax.experimental.pallas import tpu as pltpu
+from jax.sharding import Mesh
 from jax.sharding import PartitionSpec as P
 
 HEAT_RATIO = 1.4
@@ -21,8 +22,12 @@
 TRACE = 80
 MESSAGE = TRACE * SLOTS // LANES
 UNROLL = 16
-AXES = ("sfc", "sub")
-VMEM_LIMIT = 48 * 1024 * 1024
+AXES = ("y", "r", "x")
+PLANE = 32
+NEAR = PLANE - REACH
+CROSS = REACH
+MARGIN = CROSS
+VMEM_LIMIT = 24 * 1024 * 1024
 
 
 def derivative_matrix():
@@ -54,12 +59,29 @@
     return [i * 16 + j * 4 + side for i in range(4) for j in range(4)]
 
 
-def spread_variables(state_ref, rows_ref):
-    for node in range(64):
-        for block in range(BLOCKS):
-            rows_ref[pl.ds(node * BLOCKS + block, 5, stride=64 * BLOCKS), :] = state_ref[
-                node, :, block * LANES : (block + 1) * LANES
-            ]
+def tile_lanes(block):
+    return slice(block * LANES, (block + 1) * LANES)
+
+
+def spread_nodes(state_ref, rows_ref):
+    for v in range(5):
+        for tile in range(8):
+            for block in range(BLOCKS):
+                rows_ref[pl.ds(v * 256 + tile * 32 + block, 8, stride=BLOCKS), :] = state_ref[
+                    v, tile * 8 : tile * 8 + 8, tile_lanes(block)
+                ]
+
+
+def face_rows(state_ref, flat_ref, v, face, block):
+    side = 3 * (face % 2)
+    lanes = tile_lanes(block)
+    if face < 2:
+        return state_ref[v, side * 16 : side * 16 + 16, lanes]
+    if face < 4:
+        return jnp.concatenate(
+            [state_ref[v, i * 16 + side * 4 : i * 16 + side * 4 + 4, lanes] for i in range(4)], axis=0
+        )
+    return flat_ref[pl.ds(block * 320 + v * 64 + side, 16, stride=4), :]
 
 
 def lane_index(shape):
@@ -96,12 +118,15 @@
     return list(parts) + [sixth, seventh, eighth]
 
 
-def pack_kernel(rank_ref, partner_ref, state_ref, own_ref, table_ref, send_ref, rows_ref, board_ref):
-    spread_variables(state_ref, rows_ref)
+def pack_kernel(
+    place_ref, partner_ref, state_ref, own_ref, table_ref, plane_ref, up_ref, down_ref, best_ref, board_ref, flat_ref
+):
+    for block in range(BLOCKS):
+        for v in range(5):
+            flat_ref[block * 320 + v * 64 : block * 320 + v * 64 + 64, :] = state_ref[v, :, tile_lanes(block)]
     for face in range(6):
-        nodes = face_nodes(face)
         for block in range(BLOCKS):
-            pieces = [state_ref[n, :, block * LANES : (block + 1) * LANES] for n in nodes]
+            pieces = [face_rows(state_ref, flat_ref, v, face, block) for v in range(5)]
             trace = jnp.concatenate(pieces, axis=0)
             place = face * BLOCKS + block
             own_ref[place * TRACE : (place + 1) * TRACE, :] = trace
@@ -118,38 +143,114 @@
 
     def speeds(step, best):
         density, mom_x, mom_y, mom_z, energy = [
-            rows_ref[pl.ds(pl.multiple_of(v * 256 + step * 64, 64), 64), :] for v in range(5)
+            state_ref[v, pl.ds(pl.multiple_of(step * 8, 8), 8), :] for v in range(5)
         ]
         inverse = 1.0 / density
         square = (mom_x * mom_x + mom_y * mom_y + mom_z * mom_z) * inverse
         pressure = (HEAT_RATIO - 1.0) * (energy - 0.5 * square)
         wave = jnp.sqrt(square * inverse) + jnp.sqrt(HEAT_RATIO * pressure * inverse)
-        return jnp.maximum(best, jnp.max(wave.reshape(8, 8, LANES), axis=0))
-
-    best = lax.fori_loop(0, 4, speeds, jnp.zeros((8, LANES), jnp.float32))
-    top = jnp.full((8, LANES), jnp.max(best), jnp.float32)
-    rank = rank_ref[0]
-
-    def fill(peer, carry):
-        send_ref[peer, MESSAGE:, :] = top
-        return carry
-
-    lax.fori_loop(0, DEVICES, fill, 0)
-
-    def message(peer, carry):
+        return jnp.maximum(best, wave)
+
+    best = lax.fori_loop(0, 8, speeds, jnp.zeros((8, ELEMENTS), jnp.float32))
+    best = jnp.maximum(
+        jnp.maximum(best[:, tile_lanes(0)], best[:, tile_lanes(1)]),
+        jnp.maximum(best[:, tile_lanes(2)], best[:, tile_lanes(3)]),
+    )
+    best_ref[...] = best
+    up_ref[CROSS * MESSAGE :, :] = best
+    down_ref[CROSS * MESSAGE :, :] = best
+    plane, spot = place_ref[0], place_ref[1]
+
+    def send(to_ref, peer, row):
         base = pl.multiple_of(COLUMNS + peer * SLOTS, SLOTS)
         parts = compact([board_ref[pl.ds(base + 8 * k, 8), :] for k in range(8)])
         for k in range(5):
-            send_ref[peer, 8 * k : 8 * k + 8, :] = parts[k]
-        return carry
-
-    lax.fori_loop(
-        jnp.maximum(rank - REACH, 0), jnp.minimum(rank + REACH + 1, DEVICES), message, 0
-    )
+            to_ref[pl.ds(pl.multiple_of(row + 8 * k, 8), 8), :] = parts[k]
+
+    def send_plane(step, carry):
+        for k in range(4):
+            block = step * 4 + k
+            send(plane_ref, plane * PLANE + block, block * MESSAGE)
+        return carry
+
+    def send_up(step, carry):
+        for k in range(4):
+            block = step * 4 + k
+            send(up_ref, (plane + 1) * PLANE + block, block * MESSAGE)
+        return carry
+
+    def send_down(step, carry):
+        for k in range(4):
+            block = step * 4 + k
+            send(down_ref, (plane - 1) * PLANE + NEAR + block, block * MESSAGE)
+        return carry
+
+    lax.fori_loop(0, (jnp.maximum(spot - NEAR + 1, 0) + 3) // 4, send_up, 0)
+    lax.fori_loop(spot // 4, CROSS // 4, send_down, 0)
+    lax.fori_loop(jnp.maximum(spot - REACH, 0) // 4, PLANE // 4, send_plane, 0)
+
+
+def relay_kernel(place_ref, up_ref, down_ref, best_ref, far_ref, relay_ref):
+    top = jnp.maximum(
+        jnp.maximum(best_ref[...], far_ref[...]),
+        jnp.maximum(up_ref[CROSS * MESSAGE :, :], down_ref[CROSS * MESSAGE :, :]),
+    )
+    spot = place_ref[1]
+    for block in range(PLANE):
+        relay_ref[block, MESSAGE:, :] = top
+
+    def from_up(block, carry):
+        for k in range(5):
+            at = pl.multiple_of(block * MESSAGE + 8 * k, 8)
+            relay_ref[block, 8 * k : 8 * k + 8, :] = up_ref[pl.ds(at, 8), :]
+        return carry
+
+    def from_down(block, carry):
+        for k in range(5):
+            at = pl.multiple_of(block * MESSAGE + 8 * k, 8)
+            relay_ref[block + NEAR, 8 * k : 8 * k + 8, :] = down_ref[pl.ds(at, 8), :]
+        return carry
+
+    lax.fori_loop(0, jnp.maximum(spot - NEAR + 1, 0), from_up, 0)
+    lax.fori_loop(spot, CROSS, from_down, 0)
+
+
+def early_kernel(place_ref, partner_ref, table_ref, plane_ref, picked_ref, late_ref, board_ref):
+    plane, spot = place_ref[0], place_ref[1]
+    board_ref[0:COLUMNS, :] = table_ref[...]
+
+    def receive(step, carry):
+        for k in range(4):
+            block = step * 4 + k
+            start = pl.multiple_of(block * MESSAGE, 8)
+            rows = expand([plane_ref[pl.ds(start + 8 * k, 8), :] for k in range(5)])
+            base = pl.multiple_of(COLUMNS + (plane * PLANE + block) * SLOTS, SLOTS)
+            for k in range(8):
+                board_ref[pl.ds(base + 8 * k, 8), :] = rows[k]
+        return carry
+
+    lax.fori_loop(jnp.maximum(spot - REACH, 0) // 4, PLANE // 4, receive, 0)
+    low = COLUMNS + plane * (PLANE * SLOTS)
+
+    def gather(step, count):
+        base = step * UNROLL
+        for k in range(UNROLL):
+            index = partner_ref[base + k]
+            picked_ref[pl.ds(base + k, 1), :] = board_ref[pl.ds(index, 1), :]
+            late_ref[1 + count] = base + k
+            outside = (index < low) | (index >= low + PLANE * SLOTS)
+            count = count + ((index >= COLUMNS) & outside).astype(jnp.int32)
+        return count
+
+    count = lax.fori_loop(0, COLUMNS // UNROLL, gather, jnp.int32(0))
+    last = jnp.where(count > 0, late_ref[jnp.maximum(count, 1)], 0)
+    for k in range(UNROLL):
+        late_ref[1 + count + k] = last
+    late_ref[0] = count
 
 
 def volume_kernel(state_ref, metric_ref, rate_ref, rows_ref, tensor_ref, flux_ref):
-    spread_variables(state_ref, rows_ref)
+    spread_nodes(state_ref, rows_ref)
     for direction in range(3):
         for half in range(2):
             for block in range(BLOCKS):
@@ -238,11 +339,12 @@
 
 
 def finish_kernel(
-    rank_ref,
+    place_ref,
     partner_ref,
-    table_ref,
+    late_ref,
+    early_ref,
     own_ref,
-    got_ref,
+    relay_ref,
     code_ref,
     normal_ref,
     rate_in_ref,
@@ -257,28 +359,40 @@
     side_ref,
     rate_ref,
 ):
-    rank = rank_ref[0]
-    board_ref[0:COLUMNS, :] = table_ref[...]
+    plane, spot = place_ref[0], place_ref[1]
+    picked_ref[0:COLUMNS, :] = early_ref[...]
     rate_ref[...] = rate_in_ref[...]
 
-    def message(peer, carry):
-        base = pl.multiple_of(COLUMNS + peer * SLOTS, SLOTS)
-        rows = expand([got_ref[peer, 8 * k : 8 * k + 8, :] for k in range(5)])
+    def receive(block, peer):
+        rows = expand([relay_ref[block, 8 * k : 8 * k + 8, :] for k in range(5)])
+        base = pl.multiple_of(peer * SLOTS, SLOTS)
         for k in range(8):
             board_ref[pl.ds(base + 8 * k, 8), :] = rows[k]
-        return carry
-
-    lax.fori_loop(
-        jnp.maximum(rank - REACH, 0), jnp.minimum(rank + REACH + 1, DEVICES), message, 0
-    )
+
+    def receive_low(step, carry):
+        for k in range(4):
+            block = NEAR + step * 4 + k
+            receive(block, (plane - 1) * PLANE + block + MARGIN)
+        return carry
+
+    def receive_high(step, carry):
+        for k in range(4):
+            block = step * 4 + k
+            receive(block, (plane + 1) * PLANE + block + MARGIN)
+        return carry
+
+    lax.fori_loop(spot // 4, CROSS // 4, receive_low, 0)
+    lax.fori_loop(0, (jnp.maximum(spot - NEAR + 1, 0) + 3) // 4, receive_high, 0)
+    shift = MARGIN * SLOTS - COLUMNS
 
     def gather(step, carry):
-        base = step * UNROLL
+        base = 1 + step * UNROLL
         for k in range(UNROLL):
-            picked_ref[pl.ds(base + k, 1), :] = board_ref[pl.ds(partner_ref[base + k], 1), :]
-        return carry
-
-    lax.fori_loop(0, COLUMNS // UNROLL, gather, 0)
+            column = late_ref[base + k]
+            picked_ref[pl.ds(column, 1), :] = board_ref[pl.ds(partner_ref[column] + shift, 1), :]
+        return carry
+
+    lax.fori_loop(0, (late_ref[0] + UNROLL - 1) // UNROLL, gather, 0)
     for place in range(COLUMNS // LANES):
         square = picked_ref[place * LANES : (place + 1) * LANES, :].T
         other_ref[place * TRACE : (place + 1) * TRACE, :] = square[0:TRACE]
@@ -292,7 +406,7 @@
         start = group * 8 * TRACE
         for v in range(5):
             grid = [
-                [other_ref[pl.ds(start + (i * 4 + j) * 5 + v, 8, stride=TRACE), :] for j in range(4)]
+                [other_ref[pl.ds(start + v * 16 + i * 4 + j, 8, stride=TRACE), :] for j in range(4)]
                 for i in range(4)
             ]
             grid = [[jnp.where(flip_first, grid[3 - i][j], grid[i][j]) for j in range(4)] for i in range(4)]
@@ -307,7 +421,7 @@
         first_nodes = face_nodes(2 * group)
         second_nodes = face_nodes(2 * group + 1)
         for node in range(16):
-            own = [own_ref[pl.ds(start + node * 5 + v, 8, stride=TRACE), :] for v in range(5)]
+            own = [own_ref[pl.ds(start + v * 16 + node, 8, stride=TRACE), :] for v in range(5)]
             far = [turned_ref[(node * 5 + v) * 8 : (node * 5 + v) * 8 + 8, :] for v in range(5)]
             own_terms, own_wave = normal_flux(own, normal, length)
             far_terms, far_wave = normal_flux(far, normal, length)
@@ -323,19 +437,16 @@
                 at = v * 256 + second_nodes[node] * 4
                 rate_ref[at : at + 4, :] = rate_ref[at : at + 4, :] + surface[4:8]
 
-    top = jnp.max(jnp.max(got_ref[:, MESSAGE:, :], axis=0))
+    top = jnp.max(jnp.max(relay_ref[:, MESSAGE:, :], axis=0))
     scale = CFL_NUMBER / top * SECTION_STEP
-
-    def update(node, carry):
-        for block in range(BLOCKS):
-            lanes = slice(block * LANES, (block + 1) * LANES)
-            rate = rate_ref[pl.ds(node * BLOCKS + block, 5, stride=64 * BLOCKS), :]
-            section = SECTION_KEEP * register_ref[node, :, lanes] + rate
-            section_ref[node, :, lanes] = section
-            advanced_ref[node, :, lanes] = state_ref[node, :, lanes] + scale * section
-        return carry
-
-    lax.fori_loop(0, 64, update, 0)
+    for v in range(5):
+        for tile in range(8):
+            for block in range(BLOCKS):
+                nodes, lanes = slice(tile * 8, tile * 8 + 8), tile_lanes(block)
+                rate = rate_ref[pl.ds(v * 256 + tile * 32 + block, 8, stride=BLOCKS), :]
+                section = SECTION_KEEP * register_ref[v, nodes, lanes] + rate
+                section_ref[v, nodes, lanes] = section
+                advanced_ref[v, nodes, lanes] = state_ref[v, nodes, lanes] + scale * section
 
 
 def smem():
@@ -358,20 +469,23 @@
     return pltpu.VMEM(sizes, jnp.float32)
 
 
-def pack(rank, partner, state):
+def pack(place, partner, state):
     return pl.pallas_call(
         pack_kernel,
         out_shape=(
             shape(COLUMNS // LANES * TRACE, LANES),
             shape(COLUMNS, LANES),
-            shape(DEVICES, MESSAGE + 8, LANES),
+            shape(PLANE * MESSAGE, LANES),
+            shape(CROSS * MESSAGE + 8, LANES),
+            shape(CROSS * MESSAGE + 8, LANES),
+            shape(8, LANES),
         ),
         in_specs=[smem(), smem(), vmem()],
-        out_specs=(vmem(), vmem(), vmem()),
-        scratch_shapes=[scratch(1280, LANES), scratch(COLUMNS + DEVICES * SLOTS, LANES)],
+        out_specs=(vmem(),) * 6,
+        scratch_shapes=[scratch(COLUMNS + (DEVICES + CROSS) * SLOTS, LANES), scratch(1280, LANES)],
         compiler_params=params(),
         name="pack",
-    )(rank, partner, state)
+    )(place, partner, state)
 
 
 def volume(state, metric):
@@ -386,14 +500,40 @@
     )(state, metric)
 
 
-def finish(rank, partner, table, own, got, code, normal, rate, state, register):
+def relay(place, up, down, best, far):
+    return pl.pallas_call(
+        relay_kernel,
+        out_shape=shape(PLANE, MESSAGE + 8, LANES),
+        in_specs=[smem()] + [vmem()] * 4,
+        out_specs=vmem(),
+        compiler_params=params(),
+        name="relay",
+    )(place, up, down, best, far)
+
+
+def early(place, partner, table, plane):
+    return pl.pallas_call(
+        early_kernel,
+        out_shape=(
+            shape(COLUMNS, LANES),
+            jax.ShapeDtypeStruct((COLUMNS + 1 + UNROLL,), jnp.int32),
+        ),
+        in_specs=[smem(), smem(), vmem(), vmem()],
+        out_specs=(vmem(), smem()),
+        scratch_shapes=[scratch(COLUMNS + DEVICES * SLOTS, LANES)],
+        compiler_params=params(),
+        name="early",
+    )(place, partner, table, plane)
+
+
+def finish(place, partner, late, picked, own, relayed, code, normal, rate, state, register):
     return pl.pallas_call(
         finish_kernel,
-        out_shape=(shape(64, 5, ELEMENTS), shape(64, 5, ELEMENTS)),
-        in_specs=[smem(), smem()] + [vmem()] * 8,
+        out_shape=(shape(5, 64, ELEMENTS), shape(5, 64, ELEMENTS)),
+        in_specs=[smem(), smem(), smem()] + [vmem()] * 8,
         out_specs=(vmem(), vmem()),
         scratch_shapes=[
-            scratch(COLUMNS + DEVICES * SLOTS, LANES),
+            scratch((DEVICES + 2 * MARGIN) * SLOTS, LANES),
             scratch(COLUMNS, LANES),
             scratch(COLUMNS // LANES * TRACE, LANES),
             scratch(16 * 5 * 8, LANES),
@@ -402,16 +542,32 @@
         ],
         compiler_params=params(),
         name="finish",
-    )(rank, partner, table, own, got, code, normal, rate, state, register)
+    )(place, partner, late, picked, own, relayed, code, normal, rate, state, register)
+
+
+def along_y(value, steps):
+    return lax.ppermute(value, "y", [(i, (i + steps) % 4) for i in range(4)])
 
 
 def on_device(state, register, metric, face_normal, partner, flip_code, face_role, send_face):
-    rank = lax.axis_index(AXES).astype(jnp.int32)[None]
-    own, table, send = pack(rank, partner, state)
+    plane = lax.axis_index("y").astype(jnp.int32)
+    spot = lax.axis_index(("r", "x")).astype(jnp.int32)
+    place = jnp.stack([plane, spot])
+    state = state.transpose(1, 0, 2)
+    own, table, in_plane, up, down, best = pack(place, partner, state)
+    from_below = along_y(up, 1)
+    from_above = along_y(down, -1)
+    far = along_y(best, 2)
+    got = lax.all_to_all(in_plane, ("r", "x"), 0, 0, tiled=True)
     rate = volume(state, metric)
-    got = lax.all_to_all(send, AXES, 0, 0, tiled=True)
+    relayed = relay(place, from_below, from_above, best, far)
+    relayed = lax.all_to_all(relayed, ("r", "x"), 0, 0, tiled=True)
+    picked, late = early(place, partner, table, got)
     code = flip_code.reshape(COLUMNS // LANES, LANES)
-    return finish(rank, partner, table, own, got, code, face_normal, rate, state, register)
+    section, advanced = finish(
+        place, partner, late, picked, own, relayed, code, face_normal, rate, state, register.transpose(1, 0, 2)
+    )
+    return section.transpose(1, 0, 2), advanced.transpose(1, 0, 2)
 
 
 def solution(mesh):
@@ -427,7 +583,7 @@
     )
     return jax.shard_map(
         on_device,
-        mesh=mesh,
+        mesh=Mesh(mesh.devices.reshape(4, 8, 4), AXES),
         in_specs=placed,
         out_specs=(P(None, None, AXES), P(None, None, AXES)),
         check_vma=False,

time: 84.8 us -> 73.1 us (0.86)
  waiting for transfers between devices: 39.8 us -> 10.5 us
  starting transfers between devices: 13.4 us -> 22.3 us
  Pallas kernels: 22.1 us -> 29.2 us
    all_to_all x1 -> x2, waiting for transfers between devices: 39.8 us -> 0.01 us  [the longest x1 0.01 us: on_device(): relayed = lax.all_to_all(relayed, ('r', 'x'), 0, 0, tiled=True)]
    ppermute x0 -> x3, waiting for transfers between devices: none -> 10.5 us  [along_y(): return lax.ppermute(value, 'y', [(i, (i + steps) % 4) for i in range(4)])]
    pallas_call x1 -> x3, Pallas kernels: 10.7 us -> 21 us  [the longest x1 14.8 us: early(): pl.pallas_call(early_kernel, out_shape=(shape(COLUMNS, LANES), jax.ShapeD...]
    all_to_all x1 -> x2, starting transfers between devices: 13.4 us -> 17.9 us  [the longest x1 9.43 us: on_device(): got = lax.all_to_all(in_plane, ('r', 'x'), 0, 0, tiled=True)]
    ppermute x0 -> x3, starting transfers between devices: none -> 4.45 us  [along_y(): return lax.ppermute(value, 'y', [(i, (i + steps) % 4) for i in range(4)])]
    unnamed x20 -> x28, local copies, waits for them, and re-layouts: 6.01 us -> 9.11 us
    pallas_call x1, Pallas kernels: 9.69 us -> 6.91 us  [pack(): pl.pallas_call(pack_kernel, out_shape=(shape(COLUMNS // LANES * TRACE, LA...]
    pallas_call x2 -> x0, local copies, waits for them, and re-layouts: 2.44 us -> none  [finish(): pl.pallas_call(finish_kernel, out_shape=(shape(64, 5, ELEMENTS), shape(64...]
  transfers between devices with their start and end apart: 1 -> 5, of which waited for: 1 -> 1; matrix products, arithmetic and copies ran while one was open for 0% -> 0% of each run, Pallas kernels for 2% -> 25%
where the time goes in v2:
time: 73.1 us; the launch traced here: 72 us
  Pallas kernels  29.2 us (40%)
  starting transfers between devices  22.3 us (31%)
  waiting for transfers between devices  10.5 us (14%)
  local copies, waits for them, and re-layouts  9.11 us (12%)
  between operations  0.76 us (1%)
    pallas_call x1, Pallas kernels, early(): pl.pallas_call(early_kernel, out_shape=(shape(COLUMNS, LANES), jax.ShapeD...  14.8 us
    ppermute x3, waiting for transfers between devices, along_y(): return lax.ppermute(value, 'y', [(i, (i + steps) % 4) for i in range(4)])  10.5 us
    all_to_all x1, starting transfers between devices, on_device(): got = lax.all_to_all(in_plane, ('r', 'x'), 0, 0, tiled=True)  9.43 us
    unnamed x28, local copies, waits for them, and re-layouts  9.11 us
    all_to_all x1, starting transfers between devices, on_device(): relayed = lax.all_to_all(relayed, ('r', 'x'), 0, 0, tiled=True)  8.47 us
    pallas_call x1, Pallas kernels, pack(): pl.pallas_call(pack_kernel, out_shape=(shape(COLUMNS // LANES * TRACE, LA...  6.91 us
    pallas_call x1, Pallas kernels, finish(): pl.pallas_call(finish_kernel, out_shape=(shape(5, 64, ELEMENTS), shape(5,...  4.64 us
    ppermute x3, starting transfers between devices, along_y(): return lax.ppermute(value, 'y', [(i, (i + steps) % 4) for i in range(4)])  4.45 us
  transfers between devices with their start and end apart: 5, of which 1 were waited for; matrix products, arithmetic and copies ran while one was open for 0% of the time, Pallas kernels for 25%

profile of v2, /device:TPU:1, one launch (start us, length us, event | category | flops | bytes accessed | tf_op | source)
XLA Modules:
  0.0 72.0 jit_solution(8309257932481651248)
XLA Ops:
  0.6 0.1 pad_add_fusion.place_ref
  0.7 0.0 copy-start
  0.7 1.1 %copy-done = f32[64,5,512]{2,0,1:T(8,128)S(1)} copy-done((f32[64,5,512]{2,0,1:T(8,128)S(1)}, f32[64,5,512]{2,0,1:T(8,128)}, u32[]{:S(2)}) %copy-start) | copy-done | bytes 655384
  1.8 0.0 copy-start.9
  1.8 0.7 copy-done.9
  2.5 6.9 %pack.1 = (f32[1920,128]{1,0:T(8,128)S(1)}, f32[3072,128]{1,0:T(8,128)S(1)}, f32[1280,128]{1,0:T(8,128)}, f32[968,128]{1,0:T(8,128)S(1)}, f32[968,128]{1,0:T(8,128)S(1)}, /*index=5*/f32[8,128]{1,0:T(8,128)S(1)}) custom-call(s32[2]{0:T(128)S(1)} %pad_add_fusion.place_ref, s32[3072]{0:T(1024)S(1)} %copy-done.9, f32[5,64,512]{2,1,0:T(8,128)S(1)} %bitcast.9), custom_call_target="tpu_custom_call" | custom-call | tf_op jit(solution)/shard_map/pack/pallas_call | solution.py:473
  9.4 0.0 copy-start.2
  9.4 1.2 %copy-done.2 = f32[3072,128]{1,0:T(8,128)} copy-done((f32[3072,128]{1,0:T(8,128)}, f32[3072,128]{1,0:T(8,128)S(1)}, u32[]{:S(2)}) %copy-start.2) | copy-done | bytes 1572888
  10.6 0.0 copy-start.6
  10.6 1.0 %copy-done.6 = f32[1920,128]{1,0:T(8,128)} copy-done((f32[1920,128]{1,0:T(8,128)}, f32[1920,128]{1,0:T(8,128)S(1)}, u32[]{:S(2)}) %copy-start.6) | copy-done | bytes 983064
  11.5 9.4 %all-to-all-start = ((f32[32,40,128]{2,1,0:T(8,128)}), f32[32,40,128]{2,1,0:T(8,128)S(1)}, u32[]{:S(2)}, u32[]{:S(2)}) async-start(f32[32,40,128]{2,1,0:T(8,128)} %bitcast.3), calls=%async_computation | async-start | bytes 1310720 | tf_op jit(solution)/shard_map/all_to_all | solution.py:561
  21.0 1.4 %collective-permute-start = (f32[968,128]{1,0:T(8,128)S(1)}, f32[968,128]{1,0:T(8,128)S(1)}, u32[]{:S(2)}, u32[]{:S(2)}) collective-permute-start(f32[968,128]{1,0:T(8,128)S(1)} %get-tuple-element.17), channel_id=1, source_target_pairs={{0,32},{32,64},{64,96},{96,0},{1,33},{33,65},{65,97},{97,1},{2,34}... | collective-permute-start | bytes 1486856 | tf_op jit(solution)/shard_map/ppermute | solution.py:549
  22.4 1.5 %collective-permute-start.1 = (f32[968,128]{1,0:T(8,128)S(1)}, f32[968,128]{1,0:T(8,128)S(1)}, u32[]{:S(2)}, u32[]{:S(2)}) collective-permute-start(f32[968,128]{1,0:T(8,128)S(1)} %get-tuple-element.18), channel_id=1, source_target_pairs={{0,96},{32,0},{64,32},{96,64},{1,97},{33,1},{65,33},{97,65},{2,98}... | collective-permute-start | bytes 1486856 | tf_op jit(solution)/shard_map/ppermute | solution.py:549
  23.9 0.0 copy-start.1
  23.9 0.0 copy-start.12
  23.9 1.6 %collective-permute-start.2 = (f32[8,128]{1,0:T(8,128)S(1)}, f32[8,128]{1,0:T(8,128)S(1)}, u32[]{:S(2)}, u32[]{:S(2)}) collective-permute-start(f32[8,128]{1,0:T(8,128)S(1)} %get-tuple-element.19.best_ref), channel_id=1, source_target_pairs={{0,64},{32,96},{64,0},{96,32},{1,65},{33,97},{65,1},{97,33},{2,66}... | collective-permute-start | bytes 12296 | tf_op jit(solution)/shard_map/ppermute | solution.py:549
  25.4 10.5 %collective-permute-done.2.far_ref = f32[8,128]{1,0:T(8,128)S(1)} collective-permute-done((f32[8,128]{1,0:T(8,128)S(1)}, f32[8,128]{1,0:T(8,128)S(1)}, u32[]{:S(2)}, u32[]{:S(2)}) %collective-permute-start.2) | collective-permute-done | bytes 4128 | tf_op jit(solution)/shard_map/ppermute | solution.py:549
  36.0 0.0 collective-permute-done.up_ref
  36.0 0.0 collective-permute-done.1.down_ref
  36.0 1.6 %relay.1 = f32[32,48,128]{2,1,0:T(8,128)} custom-call(s32[2]{0:T(128)S(1)} %pad_add_fusion.place_ref, f32[968,128]{1,0:T(8,128)S(1)} %collective-permute-done.up_ref, f32[968,128]{1,0:T(8,128)S(1)} %collective-permute-done.1.down_ref, f32[8,128]{1,0:T(8,128)S(1)} %get-tuple-element.19.best_ref, f32[8,128]{1,0:T(8,128)S(1)} %collective-permute-done.2.far_ref), custom_call_target="tpu_custom_call" | custom-call | tf_op jit(solution)/shard_map/relay/pallas_call | solution.py:504
  37.5 0.0 copy-start.10
  37.5 0.0 all-to-all-done
  37.5 8.5 %all-to-all-start.1 = ((f32[32,48,128]{2,1,0:T(8,128)}), f32[32,48,128]{2,1,0:T(8,128)S(1)}, u32[]{:S(2)}, u32[]{:S(2)}) async-start(f32[32,48,128]{2,1,0:T(8,128)} %relay.1), calls=%async_computation.1 | async-start | bytes 1572864 | tf_op jit(solution)/shard_map/all_to_all | solution.py:564
  46.0 0.0 copy-done.1
  46.0 0.0 copy-done.12
  46.0 0.0 copy-start.8
  46.1 0.0 copy-start.11
  46.1 0.0 copy-start.13
  46.1 1.3 %volume.1.rate_in_ref = f32[1280,128]{1,0:T(8,128)S(1)} custom-call(f32[5,64,512]{2,1,0:T(8,128)S(1)} %bitcast.10, f32[3,3,512]{2,1,0:T(4,128)S(1)} %copy-done.12), custom_call_target="tpu_custom_call" | custom-call | tf_op jit(solution)/shard_map/volume/pallas_call | solution.py:492
  47.4 0.0 copy-done.10
  47.4 0.0 copy-start.3
  47.4 1.4 %copy-done.3 = f32[3072,128]{1,0:T(8,128)S(1)} copy-done((f32[3072,128]{1,0:T(8,128)S(1)}, f32[3072,128]{1,0:T(8,128)}, u32[]{:S(2)}) %copy-start.3) | copy-done | bytes 1572888
  48.8 14.8 %early.1 = (f32[3072,128]{1,0:T(8,128)S(1)}, s32[3089]{0:T(1024)S(1)}) custom-call(s32[2]{0:T(128)S(1)} %pad_add_fusion.place_ref, s32[3072]{0:T(1024)S(1)} %copy-done.10, f32[3072,128]{1,0:T(8,128)S(1)} %copy-done.3, f32[1280,128]{1,0:T(8,128)S(1)} %bitcast.12), custom_call_target="tpu_custom_call" | custom-call | tf_op jit(solution)/shard_map/early/pallas_call | solution.py:515
  63.6 0.0 copy-start.4
  63.6 1.2 %copy-done.4 = f32[3072,128]{1,0:T(8,128)} copy-done((f32[3072,128]{1,0:T(8,128)}, f32[3072,128]{1,0:T(8,128)S(1)}, u32[]{:S(2)}) %copy-start.4) | copy-done | bytes 1572888
  64.8 0.0 all-to-all-done.1.relay_ref
  64.8 0.0 copy-done.8
  64.8 0.0 copy-done.11
  64.8 0.0 copy-done.13
  64.8 0.0 copy-start.5
  64.8 1.4 %copy-done.5 = f32[3072,128]{1,0:T(8,128)S(1)} copy-done((f32[3072,128]{1,0:T(8,128)S(1)}, f32[3072,128]{1,0:T(8,128)}, u32[]{:S(2)}) %copy-start.5) | copy-done | bytes 1572888
  66.2 0.0 copy-start.7
  66.2 1.2 %copy-done.7 = f32[1920,128]{1,0:T(8,128)S(1)} copy-done((f32[1920,128]{1,0:T(8,128)S(1)}, f32[1920,128]{1,0:T(8,128)}, u32[]{:S(2)}) %copy-start.7) | copy-done | bytes 983064
  67.4 4.6 %finish.1 = (f32[5,64,512]{2,1,0:T(8,128)}, f32[5,64,512]{2,1,0:T(8,128)}) custom-call(s32[2]{0:T(128)S(1)} %pad_add_fusion.place_ref, s32[3072]{0:T(1024)S(1)} %copy-done.10, s32[3089]{0:T(1024)S(1)} %get-tuple-element.14.late_ref, f32[3072,128]{1,0:T(8,128)S(1)} %copy-done.5, f32[1920,128]{1,0:T(8,128)S(1)} %copy-done.7, ...), custom_call_target="tpu_custom_call" | custom-call | tf_op jit(solution)/shard_map/finish/pallas_call | solution.py:530
Async XLA Ops:
  0.7 1.1 %copy-start = (f32[64,5,512]{2,0,1:T(8,128)S(1)}, f32[64,5,512]{2,0,1:T(8,128)}, u32[]{:S(2)}) copy-start(f32[64,5,512]{2,0,1:T(8,128)} %param.8) | copy-start | bytes 1966084
  1.8 0.7 copy-start.9
  9.4 1.2 %copy-start.2 = (f32[3072,128]{1,0:T(8,128)}, f32[3072,128]{1,0:T(8,128)S(1)}, u32[]{:S(2)}) copy-start(f32[3072,128]{1,0:T(8,128)S(1)} %get-tuple-element.12.table_ref) | copy-start | bytes 4718596
  10.6 1.0 %copy-start.6 = (f32[1920,128]{1,0:T(8,128)}, f32[1920,128]{1,0:T(8,128)S(1)}, u32[]{:S(2)}) copy-start(f32[1920,128]{1,0:T(8,128)S(1)} %get-tuple-element.16.own_ref) | copy-start | bytes 2949124
  11.5 26.0 %all-to-all-start = ((f32[32,40,128]{2,1,0:T(8,128)}), f32[32,40,128]{2,1,0:T(8,128)S(1)}, u32[]{:S(2)}, u32[]{:S(2)}) async-start(f32[32,40,128]{2,1,0:T(8,128)} %bitcast.3), calls=%async_computation | async-start | bytes 1310720 | tf_op jit(solution)/shard_map/all_to_all | solution.py:561
  21.0 15.0 %collective-permute-start = (f32[968,128]{1,0:T(8,128)S(1)}, f32[968,128]{1,0:T(8,128)S(1)}, u32[]{:S(2)}, u32[]{:S(2)}) collective-permute-start(f32[968,128]{1,0:T(8,128)S(1)} %get-tuple-element.17), channel_id=1, source_target_pairs={{0,32},{32,64},{64,96},{96,0},{1,33},{33,65},{65,97},{97,1},{2,34}... | collective-permute-start | bytes 1486856 | tf_op jit(solution)/shard_map/ppermute | solution.py:549
  22.4 13.6 %collective-permute-start.1 = (f32[968,128]{1,0:T(8,128)S(1)}, f32[968,128]{1,0:T(8,128)S(1)}, u32[]{:S(2)}, u32[]{:S(2)}) collective-permute-start(f32[968,128]{1,0:T(8,128)S(1)} %get-tuple-element.18), channel_id=1, source_target_pairs={{0,96},{32,0},{64,32},{96,64},{1,97},{33,1},{65,33},{97,65},{2,98}... | collective-permute-start | bytes 1486856 | tf_op jit(solution)/shard_map/ppermute | solution.py:549
  23.9 22.2 %copy-start.1 = (f32[64,5,512]{2,0,1:T(8,128)S(1)}, f32[64,5,512]{2,0,1:T(8,128)}, u32[]{:S(2)}) copy-start(f32[64,5,512]{2,0,1:T(8,128)} %param.8) | copy-start | bytes 1966084
  23.9 22.2 %copy-start.12 = (f32[3,3,512]{2,1,0:T(4,128)S(1)}, f32[3,3,512]{2,1,0:T(4,128)}, u32[]{:S(2)}) copy-start(f32[3,3,512]{2,1,0:T(4,128)} %metric_ref.1) | copy-start | bytes 55300
  23.9 12.1 %collective-permute-start.2 = (f32[8,128]{1,0:T(8,128)S(1)}, f32[8,128]{1,0:T(8,128)S(1)}, u32[]{:S(2)}, u32[]{:S(2)}) collective-permute-start(f32[8,128]{1,0:T(8,128)S(1)} %get-tuple-element.19.best_ref), channel_id=1, source_target_pairs={{0,64},{32,96},{64,0},{96,32},{1,65},{33,97},{65,1},{97,33},{2,66}... | collective-permute-start | bytes 12296 | tf_op jit(solution)/shard_map/ppermute | solution.py:549
  37.5 9.9 %copy-start.10 = (s32[3072]{0:T(1024)S(1)}, s32[3072]{0:T(1024)}, u32[]{:S(2)}) copy-start(s32[3072]{0:T(1024)} %partner_ref.5) | copy-start | bytes 36868
  37.5 27.2 %all-to-all-start.1 = ((f32[32,48,128]{2,1,0:T(8,128)}), f32[32,48,128]{2,1,0:T(8,128)S(1)}, u32[]{:S(2)}, u32[]{:S(2)}) async-start(f32[32,48,128]{2,1,0:T(8,128)} %relay.1), calls=%async_computation.1 | async-start | bytes 1572864 | tf_op jit(solution)/shard_map/all_to_all | solution.py:564
  46.0 18.7 %copy-start.8 = (f32[64,5,512]{2,0,1:T(8,128)S(1)}, f32[64,5,512]{2,0,1:T(8,128)}, u32[]{:S(2)}) copy-start(f32[64,5,512]{2,0,1:T(8,128)} %param.9) | copy-start | bytes 1966084
  46.1 18.7 %copy-start.11 = (f32[3,3072]{1,0:T(4,128)S(1)}, f32[3,3072]{1,0:T(4,128)}, u32[]{:S(2)}) copy-start(f32[3,3072]{1,0:T(4,128)} %normal_ref.1) | copy-start | bytes 110596
  46.1 18.7 %copy-start.13 = (s32[3072]{0:T(1024)S(1)}, s32[3072]{0:T(1024)}, u32[]{:S(2)}) copy-start(s32[3072]{0:T(1024)} %param.13) | copy-start | bytes 36868
  47.4 1.4 %copy-start.3 = (f32[3072,128]{1,0:T(8,128)S(1)}, f32[3072,128]{1,0:T(8,128)}, u32[]{:S(2)}) copy-start(f32[3072,128]{1,0:T(8,128)} %copy-done.2) | copy-start | bytes 4718596
  63.6 1.2 %copy-start.4 = (f32[3072,128]{1,0:T(8,128)}, f32[3072,128]{1,0:T(8,128)S(1)}, u32[]{:S(2)}) copy-start(f32[3072,128]{1,0:T(8,128)S(1)} %get-tuple-element.15.early_ref) | copy-start | bytes 4718596
  64.8 1.4 %copy-start.5 = (f32[3072,128]{1,0:T(8,128)S(1)}, f32[3072,128]{1,0:T(8,128)}, u32[]{:S(2)}) copy-start(f32[3072,128]{1,0:T(8,128)} %copy-done.4) | copy-start | bytes 4718596
  66.2 1.2 %copy-start.7 = (f32[1920,128]{1,0:T(8,128)S(1)}, f32[1920,128]{1,0:T(8,128)}, u32[]{:S(2)}) copy-start(f32[1920,128]{1,0:T(8,128)} %copy-done.6) | copy-start | bytes 2949124

commit v3 on v2

--- a/solution.py
+++ b/solution.py
@@ -20,8 +20,10 @@
 LANES = 128
 BLOCKS = ELEMENTS // LANES
 TRACE = 80
+GROUP = COLUMNS // 3
 MESSAGE = TRACE * SLOTS // LANES
-UNROLL = 16
+UNROLL = 32
+BATCH = 4
 AXES = ("y", "r", "x")
 PLANE = 32
 NEAR = PLANE - REACH
@@ -118,25 +120,80 @@
     return list(parts) + [sixth, seventh, eighth]
 
 
-def pack_kernel(
-    place_ref, partner_ref, state_ref, own_ref, table_ref, plane_ref, up_ref, down_ref, best_ref, board_ref, flat_ref
-):
+def compact_into(board_ref, base, to_ref, at):
+    rows = [board_ref[pl.ds(base + 8 * k, 8), :] for k in range(8 * BATCH)]
+    parts = []
+    for block in range(BATCH):
+        parts += compact(rows[8 * block : 8 * block + 8])
+    for k in range(5 * BATCH):
+        to_ref[pl.ds(at + 8 * k, 8), :] = parts[k]
+
+
+def expand_into(from_ref, start, board_ref, base):
+    parts = [from_ref[pl.ds(start + 8 * k, 8), :] for k in range(5 * BATCH)]
+    rows = []
+    for block in range(BATCH):
+        rows += expand(parts[5 * block : 5 * block + 5])
+    for k in range(8 * BATCH):
+        board_ref[pl.ds(base + 8 * k, 8), :] = rows[k]
+
+
+def spread_flat(state_ref, flat_ref):
     for block in range(BLOCKS):
         for v in range(5):
-            flat_ref[block * 320 + v * 64 : block * 320 + v * 64 + 64, :] = state_ref[v, :, tile_lanes(block)]
+            at = block * 320 + v * 64
+            flat_ref[at : at + 64, :] = state_ref[v, :, tile_lanes(block)]
+
+
+def face_trace(state_ref, flat_ref, face, block):
+    return jnp.concatenate([face_rows(state_ref, flat_ref, v, face, block) for v in range(5)], axis=0)
+
+
+def build_tables(state_ref, flat_ref, table_ref):
+    spread_flat(state_ref, flat_ref)
+    padding = jnp.zeros((LANES - TRACE, LANES), jnp.float32)
     for face in range(6):
         for block in range(BLOCKS):
-            pieces = [face_rows(state_ref, flat_ref, v, face, block) for v in range(5)]
-            trace = jnp.concatenate(pieces, axis=0)
+            trace = face_trace(state_ref, flat_ref, face, block)
             place = face * BLOCKS + block
-            own_ref[place * TRACE : (place + 1) * TRACE, :] = trace
-            square = jnp.concatenate([trace, jnp.zeros((LANES - TRACE, LANES), jnp.float32)], axis=0)
+            square = jnp.concatenate([trace, padding], axis=0)
             table_ref[place * LANES : (place + 1) * LANES, :] = square.T
+
+
+def pack_kernel(
+    place_ref,
+    partner_hbm,
+    state_hbm,
+    plane_ref,
+    up_ref,
+    down_ref,
+    best_ref,
+    partner_ref,
+    state_ref,
+    table_ref,
+    board_ref,
+    flat_ref,
+    sems,
+):
+    copies = [pltpu.make_async_copy(partner_hbm, partner_ref, sems.at[0])]
+    for a in range(4):
+        nodes = pl.ds(a * 16, 16)
+        copies.append(
+            pltpu.make_async_copy(state_hbm.at[:, nodes, :], state_ref.at[:, nodes, :], sems.at[1 + a])
+        )
+    for copy in copies:
+        copy.start()
+    for copy in copies[1:]:
+        copy.wait()
+    build_tables(state_ref, flat_ref, table_ref)
+    copies[0].wait()
 
     def scatter(step, carry):
         base = step * UNROLL
+        targets = [partner_ref[base + k] for k in range(UNROLL)]
+        rows = [table_ref[pl.ds(base + k, 1), :] for k in range(UNROLL)]
         for k in range(UNROLL):
-            board_ref[pl.ds(partner_ref[base + k], 1), :] = table_ref[pl.ds(base + k, 1), :]
+            board_ref[pl.ds(targets[k], 1), :] = rows[k]
         return carry
 
     lax.fori_loop(0, COLUMNS // UNROLL, scatter, 0)
@@ -161,36 +218,39 @@
     down_ref[CROSS * MESSAGE :, :] = best
     plane, spot = place_ref[0], place_ref[1]
 
-    def send(to_ref, peer, row):
-        base = pl.multiple_of(COLUMNS + peer * SLOTS, SLOTS)
-        parts = compact([board_ref[pl.ds(base + 8 * k, 8), :] for k in range(8)])
-        for k in range(5):
-            to_ref[pl.ds(pl.multiple_of(row + 8 * k, 8), 8), :] = parts[k]
-
-    def send_plane(step, carry):
-        for k in range(4):
-            block = step * 4 + k
-            send(plane_ref, plane * PLANE + block, block * MESSAGE)
-        return carry
+    def send(to_ref, peer, step):
+        base = pl.multiple_of(COLUMNS + (peer + step * BATCH) * SLOTS, SLOTS)
+        compact_into(board_ref, base, to_ref, pl.multiple_of(step * BATCH * MESSAGE, 8))
 
     def send_up(step, carry):
-        for k in range(4):
-            block = step * 4 + k
-            send(up_ref, (plane + 1) * PLANE + block, block * MESSAGE)
+        send(up_ref, (plane + 1) * PLANE, step)
         return carry
 
     def send_down(step, carry):
-        for k in range(4):
-            block = step * 4 + k
-            send(down_ref, (plane - 1) * PLANE + NEAR + block, block * MESSAGE)
-        return carry
-
-    lax.fori_loop(0, (jnp.maximum(spot - NEAR + 1, 0) + 3) // 4, send_up, 0)
-    lax.fori_loop(spot // 4, CROSS // 4, send_down, 0)
-    lax.fori_loop(jnp.maximum(spot - REACH, 0) // 4, PLANE // 4, send_plane, 0)
-
-
-def relay_kernel(place_ref, up_ref, down_ref, best_ref, far_ref, relay_ref):
+        send(down_ref, (plane - 1) * PLANE + NEAR, step)
+        return carry
+
+    lax.fori_loop(0, (jnp.maximum(spot - NEAR + 1, 0) + BATCH - 1) // BATCH, send_up, 0)
+    lax.fori_loop(spot // BATCH, CROSS // BATCH, send_down, 0)
+    base = pl.multiple_of(COLUMNS + plane * (PLANE * SLOTS), SLOTS)
+    plane_ref[...] = board_ref[pl.ds(base, PLANE * SLOTS), :]
+
+
+def pack_plane_kernel(board_ref, plane_hbm, plane_ref, sems):
+    copies = []
+    for step in range(PLANE // BATCH):
+        rows = BATCH * MESSAGE
+        compact_into(board_ref, step * BATCH * SLOTS, plane_ref, step * rows)
+        part = pl.ds(step * rows, rows)
+        copies.append(
+            pltpu.make_async_copy(plane_ref.at[part, :], plane_hbm.at[part, :], sems.at[step])
+        )
+        copies[-1].start()
+    for copy in copies:
+        copy.wait()
+
+
+def relay_kernel(place_ref, up_ref, down_ref, best_ref, far_ref, rate_hbm, relay_ref):
     top = jnp.maximum(
         jnp.maximum(best_ref[...], far_ref[...]),
         jnp.maximum(up_ref[CROSS * MESSAGE :, :], down_ref[CROSS * MESSAGE :, :]),
@@ -215,42 +275,85 @@
     lax.fori_loop(spot, CROSS, from_down, 0)
 
 
-def early_kernel(place_ref, partner_ref, table_ref, plane_ref, picked_ref, late_ref, board_ref):
+def early_kernel(
+    place_ref,
+    partner_ref,
+    blank_hbm,
+    state_ref,
+    plane_ref,
+    picked_ref,
+    owner_ref,
+    board_ref,
+    flat_ref,
+    sem,
+):
     plane, spot = place_ref[0], place_ref[1]
-    board_ref[0:COLUMNS, :] = table_ref[...]
+    blank = pltpu.make_async_copy(blank_hbm, owner_ref, sem)
+    blank.start()
+    build_tables(state_ref, flat_ref, board_ref)
 
     def receive(step, carry):
-        for k in range(4):
-            block = step * 4 + k
-            start = pl.multiple_of(block * MESSAGE, 8)
-            rows = expand([plane_ref[pl.ds(start + 8 * k, 8), :] for k in range(5)])
-            base = pl.multiple_of(COLUMNS + (plane * PLANE + block) * SLOTS, SLOTS)
-            for k in range(8):
-                board_ref[pl.ds(base + 8 * k, 8), :] = rows[k]
-        return carry
-
-    lax.fori_loop(jnp.maximum(spot - REACH, 0) // 4, PLANE // 4, receive, 0)
-    low = COLUMNS + plane * (PLANE * SLOTS)
-
-    def gather(step, count):
+        start = pl.multiple_of(step * BATCH * MESSAGE, 8)
+        base = pl.multiple_of(COLUMNS + (plane * PLANE + step * BATCH) * SLOTS, SLOTS)
+        expand_into(plane_ref, start, board_ref, base)
+        return carry
+
+    lax.fori_loop(jnp.maximum(spot - REACH, 0) // BATCH, PLANE // BATCH, receive, 0)
+
+    def gather(step, carry):
         base = step * UNROLL
+        indices = [partner_ref[base + k] for k in range(UNROLL)]
+        rows = [board_ref[pl.ds(index, 1), :] for index in indices]
         for k in range(UNROLL):
-            index = partner_ref[base + k]
-            picked_ref[pl.ds(base + k, 1), :] = board_ref[pl.ds(index, 1), :]
-            late_ref[1 + count] = base + k
-            outside = (index < low) | (index >= low + PLANE * SLOTS)
-            count = count + ((index >= COLUMNS) & outside).astype(jnp.int32)
-        return count
-
-    count = lax.fori_loop(0, COLUMNS // UNROLL, gather, jnp.int32(0))
-    last = jnp.where(count > 0, late_ref[jnp.maximum(count, 1)], 0)
-    for k in range(UNROLL):
-        late_ref[1 + count + k] = last
-    late_ref[0] = count
-
-
-def volume_kernel(state_ref, metric_ref, rate_ref, rows_ref, tensor_ref, flux_ref):
+            picked_ref[pl.ds(base + k, 1), :] = rows[k]
+            owner_ref[indices[k]] = base + k
+        return carry
+
+    blank.wait()
+    lax.fori_loop(0, COLUMNS // UNROLL, gather, 0)
+
+
+def spread_normals(normal_ref, side_ref):
+    for place in range(COLUMNS // LANES):
+        side_ref[pl.ds(place, 3, stride=24), :] = normal_ref[:, place * LANES : (place + 1) * LANES]
+
+
+def group_normal(side_ref, group):
+    normal = [side_ref[k * 24 + group * 8 : k * 24 + group * 8 + 8, :] for k in range(3)]
+    length = jnp.sqrt(normal[0] * normal[0] + normal[1] * normal[1] + normal[2] * normal[2])
+    return normal, length
+
+
+def lift(rate_ref, group, node, terms):
+    first, second = face_nodes(2 * group)[node], face_nodes(2 * group + 1)[node]
+    for v in range(5):
+        at = v * 256 + first * 4
+        rate_ref[at : at + 4, :] = rate_ref[at : at + 4, :] + terms[v][0:4]
+        at = v * 256 + second * 4
+        rate_ref[at : at + 4, :] = rate_ref[at : at + 4, :] + terms[v][4:8]
+
+
+def volume_kernel(
+    state_ref,
+    register_ref,
+    metric_ref,
+    normal_ref,
+    rate_ref,
+    own_ref,
+    wave_ref,
+    rows_ref,
+    tensor_ref,
+    flux_ref,
+    flat_ref,
+    side_ref,
+):
     spread_nodes(state_ref, rows_ref)
+    spread_flat(state_ref, flat_ref)
+    spread_normals(normal_ref, side_ref)
+    for face in range(6):
+        for block in range(BLOCKS):
+            place = face * BLOCKS + block
+            own_ref[place * TRACE : (place + 1) * TRACE, :] = face_trace(state_ref, flat_ref, face, block)
     for direction in range(3):
         for half in range(2):
             for block in range(BLOCKS):
@@ -320,6 +423,21 @@
         return carry
 
     lax.fori_loop(0, 5, diverge, 0)
+    for group in range(3):
+        normal, length = group_normal(side_ref, group)
+        start = group * 8 * TRACE
+        for node in range(16):
+            own = [own_ref[pl.ds(start + v * 16 + node, 8, stride=TRACE), :] for v in range(5)]
+            terms, wave = normal_flux(own, normal, length)
+            lift(rate_ref, group, node, [(0.5 * LIFT_FACTOR) * term for term in terms])
+            at = (group * 16 + node) * 8
+            wave_ref[at : at + 8, :] = wave
+    for v in range(5):
+        for tile in range(8):
+            for block in range(BLOCKS):
+                at = pl.ds(v * 256 + tile * 32 + block, 8, stride=BLOCKS)
+                old = register_ref[v, tile * 8 : tile * 8 + 8, tile_lanes(block)]
+                rate_ref[at, :] = rate_ref[at, :] + SECTION_KEEP * old
 
 
 def normal_flux(values, normal, length):
@@ -340,16 +458,18 @@
 
 def finish_kernel(
     place_ref,
-    partner_ref,
-    late_ref,
-    early_ref,
-    own_ref,
+    owner_hbm,
+    early_hbm,
+    own_hbm,
+    wave_hbm,
     relay_ref,
     code_ref,
     normal_ref,
-    rate_in_ref,
-    state_ref,
-    register_ref,
+    rate_hbm,
+    state_hbm,
+    section_hbm,
+    advanced_hbm,
+    owner_ref,
     section_ref,
     advanced_ref,
     board_ref,
@@ -358,46 +478,87 @@
     turned_ref,
     side_ref,
     rate_ref,
+    own_ref,
+    wave_ref,
+    state_ref,
+    sems,
 ):
     plane, spot = place_ref[0], place_ref[1]
-    picked_ref[0:COLUMNS, :] = early_ref[...]
-    rate_ref[...] = rate_in_ref[...]
-
-    def receive(block, peer):
-        rows = expand([relay_ref[block, 8 * k : 8 * k + 8, :] for k in range(5)])
-        base = pl.multiple_of(peer * SLOTS, SLOTS)
-        for k in range(8):
+    window = CROSS * SLOTS
+    low_slot = jnp.maximum(COLUMNS + ((plane - 1) * PLANE + NEAR) * SLOTS, 0)
+    high_slot = jnp.minimum(COLUMNS + (plane + 1) * PLANE * SLOTS, COLUMNS + DEVICES * SLOTS - window)
+    sources = [
+        (owner_hbm.at[pl.ds(pl.multiple_of(low_slot, 512), window)], owner_ref.at[0]),
+        (owner_hbm.at[pl.ds(pl.multiple_of(high_slot, 512), window)], owner_ref.at[1]),
+    ]
+    for part in range(3):
+        rows = pl.ds(part * GROUP, GROUP)
+        sources.append((early_hbm.at[rows, :], picked_ref.at[rows, :]))
+    for part in range(3):
+        rows = pl.ds(part * 8 * TRACE, 8 * TRACE)
+        sources.append((own_hbm.at[rows, :], own_ref.at[rows, :]))
+    sources += [(wave_hbm, wave_ref), (rate_hbm, rate_ref), (state_hbm, state_ref)]
+    copies = [
+        pltpu.make_async_copy(source, target, sems.at[k])
+        for k, (source, target) in enumerate(sources)
+    ]
+    for copy in copies:
+        copy.start()
+    spread_normals(normal_ref, side_ref)
+
+    def receive(peer, block):
+        parts = [relay_ref[block + k // 5, 8 * (k % 5) : 8 * (k % 5) + 8, :] for k in range(5 * BATCH)]
+        rows = []
+        for k in range(BATCH):
+            rows += expand(parts[5 * k : 5 * k + 5])
+        base = pl.multiple_of((peer + block + MARGIN) * SLOTS, SLOTS)
+        for k in range(8 * BATCH):
             board_ref[pl.ds(base + 8 * k, 8), :] = rows[k]
 
     def receive_low(step, carry):
-        for k in range(4):
-            block = NEAR + step * 4 + k
-            receive(block, (plane - 1) * PLANE + block + MARGIN)
+        receive((plane - 1) * PLANE, NEAR + step * BATCH)
         return carry
 
     def receive_high(step, carry):
-        for k in range(4):
-            block = step * 4 + k
-            receive(block, (plane + 1) * PLANE + block + MARGIN)
-        return carry
-
-    lax.fori_loop(spot // 4, CROSS // 4, receive_low, 0)
-    lax.fori_loop(0, (jnp.maximum(spot - NEAR + 1, 0) + 3) // 4, receive_high, 0)
-    shift = MARGIN * SLOTS - COLUMNS
-
-    def gather(step, carry):
-        base = 1 + step * UNROLL
+        receive((plane + 1) * PLANE, step * BATCH)
+        return carry
+
+    lax.fori_loop(spot // BATCH, CROSS // BATCH, receive_low, 0)
+    high = (jnp.maximum(spot - NEAR + 1, 0) + BATCH - 1) // BATCH
+    lax.fori_loop(0, high, receive_high, 0)
+
+    def place_rows(side, base, step):
+        at = step * UNROLL
+        columns = [owner_ref[side, at + k] for k in range(UNROLL)]
+        rows = [board_ref[pl.ds(base * SLOTS + at + k, 1), :] for k in range(UNROLL)]
         for k in range(UNROLL):
-            column = late_ref[base + k]
-            picked_ref[pl.ds(column, 1), :] = board_ref[pl.ds(partner_ref[column] + shift, 1), :]
-        return carry
-
-    lax.fori_loop(0, (late_ref[0] + UNROLL - 1) // UNROLL, gather, 0)
+            picked_ref[pl.ds(columns[k], 1), :] = rows[k]
+
+    def place_low(step, carry):
+        place_rows(0, (plane - 1) * PLANE + NEAR + MARGIN, step)
+        return carry
+
+    def place_high(step, carry):
+        place_rows(1, (plane + 1) * PLANE + MARGIN, step)
+        return carry
+
+    chunk = SLOTS // UNROLL
+    for copy in copies[:5]:
+        copy.wait()
+
+    @pl.when(plane > 0)
+    def _():
+        lax.fori_loop(spot * chunk, CROSS * chunk, place_low, 0)
+
+    @pl.when(plane < 3)
+    def _():
+        lax.fori_loop(0, jnp.maximum(spot - NEAR + 1, 0) * chunk, place_high, 0)
+
     for place in range(COLUMNS // LANES):
         square = picked_ref[place * LANES : (place + 1) * LANES, :].T
         other_ref[place * TRACE : (place + 1) * TRACE, :] = square[0:TRACE]
-        side_ref[pl.ds(place, 3, stride=24), :] = normal_ref[:, place * LANES : (place + 1) * LANES]
-
+    for copy in copies[5:]:
+        copy.wait()
     for group in range(3):
         code = code_ref[group * 8 : group * 8 + 8, :]
         flip_first = code % 2 == 1
@@ -416,37 +577,36 @@
                     value = grid[i][j] if i == j else jnp.where(swapped, grid[j][i], grid[i][j])
                     at = ((i * 4 + j) * 5 + v) * 8
                     turned_ref[at : at + 8, :] = value
-        normal = [side_ref[k * 24 + group * 8 : k * 24 + group * 8 + 8, :] for k in range(3)]
-        length = jnp.sqrt(normal[0] * normal[0] + normal[1] * normal[1] + normal[2] * normal[2])
-        first_nodes = face_nodes(2 * group)
-        second_nodes = face_nodes(2 * group + 1)
+        normal, length = group_normal(side_ref, group)
         for node in range(16):
             own = [own_ref[pl.ds(start + v * 16 + node, 8, stride=TRACE), :] for v in range(5)]
             far = [turned_ref[(node * 5 + v) * 8 : (node * 5 + v) * 8 + 8, :] for v in range(5)]
-            own_terms, own_wave = normal_flux(own, normal, length)
             far_terms, far_wave = normal_flux(far, normal, length)
-            bound = jnp.maximum(own_wave, far_wave)
+            at = (group * 16 + node) * 8
+            bound = jnp.maximum(wave_ref[at : at + 8, :], far_wave)
             viscous = bound + length
-            for v in range(5):
-                weight = bound if v == 0 else viscous
-                surface = (0.5 * LIFT_FACTOR) * (
-                    own_terms[v] - far_terms[v] + weight * (far[v] - own[v])
-                )
-                at = v * 256 + first_nodes[node] * 4
-                rate_ref[at : at + 4, :] = rate_ref[at : at + 4, :] + surface[0:4]
-                at = v * 256 + second_nodes[node] * 4
-                rate_ref[at : at + 4, :] = rate_ref[at : at + 4, :] + surface[4:8]
+            terms = [
+                (0.5 * LIFT_FACTOR)
+                * ((bound if v == 0 else viscous) * (far[v] - own[v]) - far_terms[v])
+                for v in range(5)
+            ]
+            lift(rate_ref, group, node, terms)
 
     top = jnp.max(jnp.max(relay_ref[:, MESSAGE:, :], axis=0))
     scale = CFL_NUMBER / top * SECTION_STEP
+    results = []
     for v in range(5):
         for tile in range(8):
             for block in range(BLOCKS):
                 nodes, lanes = slice(tile * 8, tile * 8 + 8), tile_lanes(block)
-                rate = rate_ref[pl.ds(v * 256 + tile * 32 + block, 8, stride=BLOCKS), :]
-                section = SECTION_KEEP * register_ref[v, nodes, lanes] + rate
+                section = rate_ref[pl.ds(v * 256 + tile * 32 + block, 8, stride=BLOCKS), :]
                 section_ref[v, nodes, lanes] = section
                 advanced_ref[v, nodes, lanes] = state_ref[v, nodes, lanes] + scale * section
+        for source, target in ((section_ref, section_hbm), (advanced_ref, advanced_hbm)):
+            results.append(pltpu.make_async_copy(source.at[v], target.at[v], sems.at[len(results)]))
+            results[-1].start()
+    for copy in results:
+        copy.wait()
 
 
 def smem():
@@ -467,82 +627,140 @@
 
 def scratch(*sizes):
     return pltpu.VMEM(sizes, jnp.float32)
+
+
+def hbm():
+    return pl.BlockSpec(memory_space=pltpu.HBM)
+
+
+def anywhere():
+    return pl.BlockSpec(memory_space=pl.ANY)
 
 
 def pack(place, partner, state):
     return pl.pallas_call(
         pack_kernel,
         out_shape=(
-            shape(COLUMNS // LANES * TRACE, LANES),
-            shape(COLUMNS, LANES),
-            shape(PLANE * MESSAGE, LANES),
+            scratch(PLANE * SLOTS, LANES),
             shape(CROSS * MESSAGE + 8, LANES),
             shape(CROSS * MESSAGE + 8, LANES),
             shape(8, LANES),
         ),
-        in_specs=[smem(), smem(), vmem()],
-        out_specs=(vmem(),) * 6,
-        scratch_shapes=[scratch(COLUMNS + (DEVICES + CROSS) * SLOTS, LANES), scratch(1280, LANES)],
+        in_specs=[smem(), hbm(), hbm()],
+        out_specs=(vmem(),) * 4,
+        scratch_shapes=[
+            pltpu.SMEM((COLUMNS,), jnp.int32),
+            scratch(5, 64, ELEMENTS),
+            scratch(COLUMNS, LANES),
+            scratch(COLUMNS + (DEVICES + CROSS) * SLOTS, LANES),
+            scratch(1280, LANES),
+            pltpu.SemaphoreType.DMA((5,)),
+        ],
         compiler_params=params(),
         name="pack",
     )(place, partner, state)
 
 
-def volume(state, metric):
+def pack_plane(board):
+    return pl.pallas_call(
+        pack_plane_kernel,
+        out_shape=pltpu.HBM((PLANE * MESSAGE, LANES), jnp.float32),
+        in_specs=[vmem()],
+        out_specs=hbm(),
+        scratch_shapes=[
+            scratch(PLANE * MESSAGE, LANES),
+            pltpu.SemaphoreType.DMA((PLANE // BATCH,)),
+        ],
+        compiler_params=params(),
+        name="pack_plane",
+    )(board)
+
+
+def volume(state, register, metric, normal):
     return pl.pallas_call(
         volume_kernel,
-        out_shape=shape(1280, LANES),
-        in_specs=[vmem(), vmem()],
-        out_specs=vmem(),
-        scratch_shapes=[scratch(1280, LANES), scratch(72, LANES), scratch(3, 1280, LANES)],
+        out_shape=(
+            shape(1280, LANES),
+            pltpu.HBM((COLUMNS // LANES * TRACE, LANES), jnp.float32),
+            shape(COLUMNS // LANES * 16, LANES),
+        ),
+        in_specs=[vmem()] * 4,
+        out_specs=(vmem(),) * 3,
+        scratch_shapes=[
+            scratch(1280, LANES),
+            scratch(72, LANES),
+            scratch(3, 1280, LANES),
+            scratch(1280, LANES),
+            scratch(72, LANES),
+        ],
         compiler_params=params(),
         name="volume",
-    )(state, metric)
-
-
-def relay(place, up, down, best, far):
+    )(state, register, metric, normal)
+
+
+def relay(place, up, down, best, far, rate):
     return pl.pallas_call(
         relay_kernel,
         out_shape=shape(PLANE, MESSAGE + 8, LANES),
-        in_specs=[smem()] + [vmem()] * 4,
+        in_specs=[smem()] + [vmem()] * 4 + [anywhere()],
         out_specs=vmem(),
         compiler_params=params(),
+        cost_estimate=pl.CostEstimate(flops=100000000000, bytes_accessed=100000000, transcendentals=0),
         name="relay",
-    )(place, up, down, best, far)
-
-
-def early(place, partner, table, plane):
+    )(place, up, down, best, far, rate)
+
+
+def early(place, partner, blank, state, plane):
     return pl.pallas_call(
         early_kernel,
         out_shape=(
-            shape(COLUMNS, LANES),
-            jax.ShapeDtypeStruct((COLUMNS + 1 + UNROLL,), jnp.int32),
+            pltpu.HBM((COLUMNS, LANES), jnp.float32),
+            jax.ShapeDtypeStruct((COLUMNS + DEVICES * SLOTS,), jnp.int32),
         ),
-        in_specs=[smem(), smem(), vmem(), vmem()],
+        in_specs=[smem(), smem(), anywhere(), vmem(), vmem()],
         out_specs=(vmem(), smem()),
-        scratch_shapes=[scratch(COLUMNS + DEVICES * SLOTS, LANES)],
+        scratch_shapes=[
+            scratch(COLUMNS + DEVICES * SLOTS, LANES),
+            scratch(1280, LANES),
+            pltpu.SemaphoreType.DMA,
+        ],
         compiler_params=params(),
         name="early",
-    )(place, partner, table, plane)
-
-
-def finish(place, partner, late, picked, own, relayed, code, normal, rate, state, register):
+    )(place, partner, blank, state, plane)
+
+
+def finish(place, owner, picked, own, wave, relayed, code, normal, rate, state):
     return pl.pallas_call(
         finish_kernel,
-        out_shape=(shape(5, 64, ELEMENTS), shape(5, 64, ELEMENTS)),
-        in_specs=[smem(), smem(), smem()] + [vmem()] * 8,
-        out_specs=(vmem(), vmem()),
+        out_shape=(pltpu.HBM((5, 64, ELEMENTS), jnp.float32),) * 2,
+        in_specs=[smem(), hbm(), hbm(), hbm(), anywhere(), vmem(), vmem(), vmem(), anywhere(), anywhere()],
+        out_specs=(hbm(), hbm()),
         scratch_shapes=[
+            pltpu.SMEM((2, CROSS * SLOTS), jnp.int32),
+            scratch(5, 64, ELEMENTS),
+            scratch(5, 64, ELEMENTS),
             scratch((DEVICES + 2 * MARGIN) * SLOTS, LANES),
-            scratch(COLUMNS, LANES),
+            scratch(COLUMNS + 8, LANES),
             scratch(COLUMNS // LANES * TRACE, LANES),
             scratch(16 * 5 * 8, LANES),
             scratch(72, LANES),
             scratch(1280, LANES),
+            scratch(COLUMNS // LANES * TRACE, LANES),
+            scratch(COLUMNS // LANES * 16, LANES),
+            scratch(5, 64, ELEMENTS),
+            pltpu.SemaphoreType.DMA((11,)),
         ],
         compiler_params=params(),
         name="finish",
-    )(place, partner, late, picked, own, relayed, code, normal, rate, state, register)
+    )(place, owner, picked, own, wave, relayed, code, normal, rate, state)
+
+
+def in_hbm(value):
+    return pltpu.with_memory_space_constraint(value, pltpu.HBM)
+
+
+def in_vmem(value):
+    return pltpu.with_memory_space_constraint(value, pltpu.VMEM)
 
 
 def along_y(value, steps):
@@ -554,18 +772,20 @@
     spot = lax.axis_index(("r", "x")).astype(jnp.int32)
     place = jnp.stack([plane, spot])
     state = state.transpose(1, 0, 2)
-    own, table, in_plane, up, down, best = pack(place, partner, state)
+    board, up, down, best = pack(place, in_hbm(partner), in_hbm(state))
     from_below = along_y(up, 1)
     from_above = along_y(down, -1)
     far = along_y(best, 2)
+    in_plane = pack_plane(in_vmem(board))
     got = lax.all_to_all(in_plane, ("r", "x"), 0, 0, tiled=True)
-    rate = volume(state, metric)
-    relayed = relay(place, from_below, from_above, best, far)
+    rate, own, wave = volume(state, register.transpose(1, 0, 2), metric, face_normal)
+    relayed = relay(place, from_below, from_above, best, far, rate)
     relayed = lax.all_to_all(relayed, ("r", "x"), 0, 0, tiled=True)
-    picked, late = early(place, partner, table, got)
+    blank = jnp.full((COLUMNS + DEVICES * SLOTS,), COLUMNS, jnp.int32)
+    picked, owner = early(place, partner, blank, state, got)
     code = flip_code.reshape(COLUMNS // LANES, LANES)
     section, advanced = finish(
-        place, partner, late, picked, own, relayed, code, face_normal, rate, state, register.transpose(1, 0, 2)
+        place, in_hbm(owner), in_hbm(picked), in_hbm(own), wave, relayed, code, face_normal, rate, state
     )
     return section.transpose(1, 0, 2), advanced.transpose(1, 0, 2)
 

time: 73.1 us -> 60.9 us (0.83)
  the two profiles are of different devices: /device:TPU:1 before, /device:TPU:8 now
where the time goes in v3:
time: 60.9 us; the launch traced here: 60.5 us
  Pallas kernels  27.8 us (46%)
  starting transfers between devices  16.5 us (27%)
  waiting for transfers between devices  14.7 us (24%)
  between operations  0.77 us (1%)
  local copies, waits for them, and re-layouts  0.64 us (1%)
    all_to_all x1, waiting for transfers between devices, on_device(): got = lax.all_to_all(in_plane, ('r', 'x'), 0, 0, tiled=True)  8.65 us
    all_to_all x1, starting transfers between devices, on_device(): got = lax.all_to_all(in_plane, ('r', 'x'), 0, 0, tiled=True)  8.07 us
    pallas_call x1, Pallas kernels, finish(): pl.pallas_call(finish_kernel, out_shape=(pltpu.HBM((5, 64, ELEMENTS), jnp...  7.75 us
    pallas_call x1, Pallas kernels, early(): pl.pallas_call(early_kernel, out_shape=(pltpu.HBM((COLUMNS, LANES), jnp.f...  7.74 us
    pallas_call x1, Pallas kernels, pack(): pl.pallas_call(pack_kernel, out_shape=(scratch(PLANE * SLOTS, LANES), sha...  6.95 us
    all_to_all x1, waiting for transfers between devices, on_device(): relayed = lax.all_to_all(relayed, ('r', 'x'), 0, 0, tiled=True)  6.03 us
    ppermute x3, starting transfers between devices, along_y(): return lax.ppermute(value, 'y', [(i, (i + steps) % 4) for i in range(4)])  4.39 us
    all_to_all x1, starting transfers between devices, on_device(): relayed = lax.all_to_all(relayed, ('r', 'x'), 0, 0, tiled=True)  4 us
  transfers between devices with their start and end apart: 5, of which 2 were waited for; matrix products, arithmetic and copies ran while one was open for 0% of the time, Pallas kernels for 22%

profile of v3, /device:TPU:8, one launch (start us, length us, event | category | flops | bytes accessed | tf_op | source)
XLA Modules:
  0.0 60.5 jit_solution(14263884113223004007)
XLA Ops:
  0.6 0.1 pad_add_fusion.place_ref
  0.7 6.9 %pack.1 = (f32[2048,128]{1,0:T(8,128)S(1)}, f32[968,128]{1,0:T(8,128)}, f32[968,128]{1,0:T(8,128)}, f32[8,128]{1,0:T(8,128)S(1)}) custom-call(s32[2]{0:T(128)S(1)} %pad_add_fusion.place_ref, s32[3072]{0:T(1024)} %partner_ref.1, f32[5,64,512]{2,1,0:T(8,128)} %bitcast.9), custom_call_target="tpu_custom_call" | custom-call | tf_op jit(solution)/shard_map/pack/pallas_call | solution.py:641
  7.7 0.0 copy-start
  7.7 0.0 copy-start.1
  7.7 0.0 copy-start.2
  7.7 0.0 copy-start.5
  7.7 1.6 %collective-permute-start = (f32[968,128]{1,0:T(8,128)}, f32[968,128]{1,0:T(8,128)S(1)}, u32[]{:S(2)}, u32[]{:S(2)}) collective-permute-start(f32[968,128]{1,0:T(8,128)} %get-tuple-element.18), channel_id=1, source_target_pairs={{0,32},{32,64},{64,96},{96,0},{1,33},{33,65},{65,97},{97,1},{2,34}... | collective-permute-start | bytes 1486856 | tf_op jit(solution)/shard_map/ppermute | solution.py:767
  9.4 0.4 collective-permute-start.1
  9.8 2.3 %collective-permute-start.2 = (f32[8,128]{1,0:T(8,128)S(1)}, f32[8,128]{1,0:T(8,128)S(1)}, u32[]{:S(2)}, u32[]{:S(2)}) collective-permute-start(f32[8,128]{1,0:T(8,128)S(1)} %get-tuple-element.20.best_ref), channel_id=1, source_target_pairs={{0,64},{32,96},{64,0},{96,32},{1,65},{33,97},{65,1},{97,33},{2,66}... | collective-permute-start | bytes 12296 | tf_op jit(solution)/shard_map/ppermute | solution.py:767
  12.1 1.0 %pack_plane.1 = f32[1280,128]{1,0:T(8,128)} custom-call(f32[2048,128]{1,0:T(8,128)S(1)} %get-tuple-element.13.board_ref), custom_call_target="tpu_custom_call" | custom-call | tf_op jit(solution)/shard_map/pack_plane/pallas_call | solution.py:665
  13.1 8.1 %all-to-all-start = ((f32[32,40,128]{2,1,0:T(8,128)}), f32[32,40,128]{2,1,0:T(8,128)S(1)}, u32[]{:S(2)}, u32[]{:S(2)}) async-start(f32[32,40,128]{2,1,0:T(8,128)} %bitcast.16), calls=%async_computation | async-start | bytes 1310720 | tf_op jit(solution)/shard_map/all_to_all | solution.py:780
  21.2 0.0 copy-done
  21.2 0.0 copy-done.1
  21.2 0.0 copy-done.2
  21.2 0.0 copy-done.5
  21.2 2.3 %volume.1 = (f32[1280,128]{1,0:T(8,128)S(1)}, f32[1920,128]{1,0:T(8,128)}, f32[384,128]{1,0:T(8,128)S(1)}) custom-call(f32[5,64,512]{2,1,0:T(8,128)S(1)} %bitcast.10, f32[5,64,512]{2,1,0:T(8,128)S(1)} %bitcast.14, f32[3,3,512]{2,1,0:T(4,128)S(1)} %copy-done.5, f32[3,3072]{1,0:T(4,128)S(1)} %copy-done.2), custom_call_target="tpu_custom_call" | custom-call | tf_op jit(solution)/shard_map/volume/pallas_call | solution.py:680
  23.6 0.0 collective-permute-done.2.far_ref
  23.6 0.0 collective-permute-done.up_ref
  23.6 0.0 collective-permute-done.1.down_ref
  23.6 2.1 %relay.1 = f32[32,48,128]{2,1,0:T(8,128)} custom-call(s32[2]{0:T(128)S(1)} %pad_add_fusion.place_ref, f32[968,128]{1,0:T(8,128)S(1)} %collective-permute-done.up_ref, f32[968,128]{1,0:T(8,128)} %collective-permute-done.1.down_ref, f32[8,128]{1,0:T(8,128)S(1)} %get-tuple-element.20.best_ref, f32[8,128]{1,0:T(8,128)S(1)} %collective-permute-done.2.far_ref, ...), custom_call_target="tpu_custom_call" | custom-call | flops 99999997952 | bytes 100000000 | tf_op jit(solution)/shard_map/relay/pallas_call | solution.py:702
  25.6 0.0 copy-start.3
  25.6 0.0 copy-start.6
  25.6 8.7 %all-to-all-done = f32[32,40,128]{2,1,0:T(8,128)S(1)} async-done(((f32[32,40,128]{2,1,0:T(8,128)}), f32[32,40,128]{2,1,0:T(8,128)S(1)}, u32[]{:S(2)}, u32[]{:S(2)}) %all-to-all-start) | async-done | bytes 655392 | tf_op jit(solution)/shard_map/all_to_all | solution.py:780
  34.3 4.0 %all-to-all-start.1 = ((f32[32,48,128]{2,1,0:T(8,128)}), f32[32,48,128]{2,1,0:T(8,128)S(1)}, u32[]{:S(2)}, u32[]{:S(2)}) async-start(f32[32,48,128]{2,1,0:T(8,128)} %relay.1), calls=%async_computation.1 | async-start | bytes 1572864 | tf_op jit(solution)/shard_map/all_to_all | solution.py:783
  38.3 0.0 copy-done.3
  38.3 7.7 %early.1 = (f32[3072,128]{1,0:T(8,128)}, s32[11264]{0:T(1024)S(1)}) custom-call(s32[2]{0:T(128)S(1)} %pad_add_fusion.place_ref, s32[3072]{0:T(1024)S(1)} %copy-done.3, s32[11264]{0:T(1024)S(1)} %broadcast_in_dim.3.blank_hbm, f32[5,64,512]{2,1,0:T(8,128)S(1)} %bitcast.11, f32[1280,128]{1,0:T(8,128)S(1)} %bitcast.13), custom_call_target="tpu_custom_call" | custom-call | tf_op jit(solution)/shard_map/early/pallas_call | solution.py:714
  46.1 0.0 copy-start.4
  46.1 0.6 copy-done.4
  46.7 6.0 %all-to-all-done.1.relay_ref = f32[32,48,128]{2,1,0:T(8,128)S(1)} async-done(((f32[32,48,128]{2,1,0:T(8,128)}), f32[32,48,128]{2,1,0:T(8,128)S(1)}, u32[]{:S(2)}, u32[]{:S(2)}) %all-to-all-start.1) | async-done | bytes 786464 | tf_op jit(solution)/shard_map/all_to_all | solution.py:783
  52.7 0.0 copy-done.6
  52.7 7.7 %finish.1 = (f32[5,64,512]{2,1,0:T(8,128)}, f32[5,64,512]{2,1,0:T(8,128)}) custom-call(s32[2]{0:T(128)S(1)} %pad_add_fusion.place_ref, s32[11264]{0:T(1024)} %copy-done.4, f32[3072,128]{1,0:T(8,128)} %get-tuple-element.15.early_hbm, f32[1920,128]{1,0:T(8,128)} %get-tuple-element.16.own_hbm, f32[384,128]{1,0:T(8,128)S(1)} %get-tuple-element.17.wave_hbm, ...), custom_call_target="tpu_custom_call" | custom-call | tf_op jit(solution)/shard_map/finish/pallas_call | solution.py:733
  (1 shorter events, 0.0 us)
Async XLA Ops:
  7.7 13.5 %copy-start = (f32[64,5,512]{2,0,1:T(8,128)S(1)}, f32[64,5,512]{2,0,1:T(8,128)}, u32[]{:S(2)}) copy-start(f32[64,5,512]{2,0,1:T(8,128)} %param.8) | copy-start | bytes 1966084
  7.7 13.5 %copy-start.1 = (f32[64,5,512]{2,0,1:T(8,128)S(1)}, f32[64,5,512]{2,0,1:T(8,128)}, u32[]{:S(2)}) copy-start(f32[64,5,512]{2,0,1:T(8,128)} %param.9) | copy-start | bytes 1966084
  7.7 13.5 %copy-start.2 = (f32[3,3072]{1,0:T(4,128)S(1)}, f32[3,3072]{1,0:T(4,128)}, u32[]{:S(2)}) copy-start(f32[3,3072]{1,0:T(4,128)} %normal_ref.3) | copy-start | bytes 110596
  7.7 13.5 %copy-start.5 = (f32[3,3,512]{2,1,0:T(4,128)S(1)}, f32[3,3,512]{2,1,0:T(4,128)}, u32[]{:S(2)}) copy-start(f32[3,3,512]{2,1,0:T(4,128)} %metric_ref.1) | copy-start | bytes 55300
  7.7 15.8 %collective-permute-start = (f32[968,128]{1,0:T(8,128)}, f32[968,128]{1,0:T(8,128)S(1)}, u32[]{:S(2)}, u32[]{:S(2)}) collective-permute-start(f32[968,128]{1,0:T(8,128)} %get-tuple-element.18), channel_id=1, source_target_pairs={{0,32},{32,64},{64,96},{96,0},{1,33},{33,65},{65,97},{97,1},{2,34}... | collective-permute-start | bytes 1486856 | tf_op jit(solution)/shard_map/ppermute | solution.py:767
  9.4 14.2 %collective-permute-start.1 = (f32[968,128]{1,0:T(8,128)}, f32[968,128]{1,0:T(8,128)}, u32[]{:S(2)}, u32[]{:S(2)}) collective-permute-start(f32[968,128]{1,0:T(8,128)} %get-tuple-element.19), channel_id=1, source_target_pairs={{0,96},{32,0},{64,32},{96,64},{1,97},{33,1},{65,33},{97,65},{2,98}... | collective-permute-start | bytes 1486856 | tf_op jit(solution)/shard_map/ppermute | solution.py:767
  9.8 13.7 %collective-permute-start.2 = (f32[8,128]{1,0:T(8,128)S(1)}, f32[8,128]{1,0:T(8,128)S(1)}, u32[]{:S(2)}, u32[]{:S(2)}) collective-permute-start(f32[8,128]{1,0:T(8,128)S(1)} %get-tuple-element.20.best_ref), channel_id=1, source_target_pairs={{0,64},{32,96},{64,0},{96,32},{1,65},{33,97},{65,1},{97,33},{2,66}... | collective-permute-start | bytes 12296 | tf_op jit(solution)/shard_map/ppermute | solution.py:767
  13.1 21.2 %all-to-all-start = ((f32[32,40,128]{2,1,0:T(8,128)}), f32[32,40,128]{2,1,0:T(8,128)S(1)}, u32[]{:S(2)}, u32[]{:S(2)}) async-start(f32[32,40,128]{2,1,0:T(8,128)} %bitcast.16), calls=%async_computation | async-start | bytes 1310720 | tf_op jit(solution)/shard_map/all_to_all | solution.py:780
  25.6 12.7 %copy-start.3 = (s32[3072]{0:T(1024)S(1)}, s32[3072]{0:T(1024)}, u32[]{:S(2)}) copy-start(s32[3072]{0:T(1024)} %partner_ref.1) | copy-start | bytes 36868
  25.6 27.1 %copy-start.6 = (s32[3072]{0:T(1024)S(1)}, s32[3072]{0:T(1024)}, u32[]{:S(2)}) copy-start(s32[3072]{0:T(1024)} %param.13) | copy-start | bytes 36868
  34.3 18.4 %all-to-all-start.1 = ((f32[32,48,128]{2,1,0:T(8,128)}), f32[32,48,128]{2,1,0:T(8,128)S(1)}, u32[]{:S(2)}, u32[]{:S(2)}) async-start(f32[32,48,128]{2,1,0:T(8,128)} %relay.1), calls=%async_computation.1 | async-start | bytes 1572864 | tf_op jit(solution)/shard_map/all_to_all | solution.py:783
  46.1 0.6 %copy-start.4 = (s32[11264]{0:T(1024)}, s32[11264]{0:T(1024)S(1)}, u32[]{:S(2)}) copy-start(s32[11264]{0:T(1024)S(1)} %get-tuple-element.14.owner_hbm) | copy-start | bytes 135172

commit v4 on v3

--- a/solution.py
+++ b/solution.py
@@ -23,6 +23,7 @@
 GROUP = COLUMNS // 3
 MESSAGE = TRACE * SLOTS // LANES
 UNROLL = 32
+SIDE = 48
 BATCH = 4
 AXES = ("y", "r", "x")
 PLANE = 32
@@ -86,6 +87,10 @@
     return flat_ref[pl.ds(block * 320 + v * 64 + side, 16, stride=4), :]
 
 
+def aligned(row):
+    return row if isinstance(row, int) else pl.multiple_of(row, 8)
+
+
 def lane_index(shape):
     return lax.broadcasted_iota(jnp.int32, shape, 1)
 
@@ -164,10 +169,11 @@
     place_ref,
     partner_hbm,
     state_hbm,
-    plane_ref,
+    plane_hbm,
     up_ref,
     down_ref,
     best_ref,
+    plane_ref,
     partner_ref,
     state_ref,
     table_ref,
@@ -220,7 +226,7 @@
 
     def send(to_ref, peer, step):
         base = pl.multiple_of(COLUMNS + (peer + step * BATCH) * SLOTS, SLOTS)
-        compact_into(board_ref, base, to_ref, pl.multiple_of(step * BATCH * MESSAGE, 8))
+        compact_into(board_ref, base, to_ref, aligned(step * BATCH * MESSAGE))
 
     def send_up(step, carry):
         send(up_ref, (plane + 1) * PLANE, step)
@@ -230,34 +236,25 @@
         send(down_ref, (plane - 1) * PLANE + NEAR, step)
         return carry
 
+    sent = []
+    for step in range(PLANE // BATCH):
+        send(plane_ref, plane * PLANE, step)
+        part = pl.ds(step * BATCH * MESSAGE, BATCH * MESSAGE)
+        sent.append(
+            pltpu.make_async_copy(plane_ref.at[part, :], plane_hbm.at[part, :], sems.at[5 + step])
+        )
+        sent[-1].start()
     lax.fori_loop(0, (jnp.maximum(spot - NEAR + 1, 0) + BATCH - 1) // BATCH, send_up, 0)
     lax.fori_loop(spot // BATCH, CROSS // BATCH, send_down, 0)
-    base = pl.multiple_of(COLUMNS + plane * (PLANE * SLOTS), SLOTS)
-    plane_ref[...] = board_ref[pl.ds(base, PLANE * SLOTS), :]
-
-
-def pack_plane_kernel(board_ref, plane_hbm, plane_ref, sems):
-    copies = []
-    for step in range(PLANE // BATCH):
-        rows = BATCH * MESSAGE
-        compact_into(board_ref, step * BATCH * SLOTS, plane_ref, step * rows)
-        part = pl.ds(step * rows, rows)
-        copies.append(
-            pltpu.make_async_copy(plane_ref.at[part, :], plane_hbm.at[part, :], sems.at[step])
-        )
-        copies[-1].start()
-    for copy in copies:
+    for copy in sent:
         copy.wait()
 
 
-def relay_kernel(place_ref, up_ref, down_ref, best_ref, far_ref, rate_hbm, relay_ref):
-    top = jnp.maximum(
-        jnp.maximum(best_ref[...], far_ref[...]),
-        jnp.maximum(up_ref[CROSS * MESSAGE :, :], down_ref[CROSS * MESSAGE :, :]),
+def relay_kernel(place_ref, up_ref, down_ref, best_ref, rate_hbm, relay_ref, three_ref):
+    three_ref[...] = jnp.maximum(
+        best_ref[...], jnp.maximum(up_ref[CROSS * MESSAGE :, :], down_ref[CROSS * MESSAGE :, :])
     )
     spot = place_ref[1]
-    for block in range(PLANE):
-        relay_ref[block, MESSAGE:, :] = top
 
     def from_up(block, carry):
         for k in range(5):
@@ -273,6 +270,15 @@
 
     lax.fori_loop(0, jnp.maximum(spot - NEAR + 1, 0), from_up, 0)
     lax.fori_loop(spot, CROSS, from_down, 0)
+
+
+def top_kernel(three_ref, far_ref, relay_in, relay_hbm, top_ref, sem):
+    top = jnp.maximum(three_ref[...], far_ref[...])
+    for block in range(PLANE):
+        top_ref[block] = top
+    copy = pltpu.make_async_copy(top_ref, relay_hbm.at[:, pl.ds(MESSAGE, 8), :], sem)
+    copy.start()
+    copy.wait()
 
 
 def early_kernel(
@@ -281,10 +287,11 @@
     blank_hbm,
     state_ref,
     plane_ref,
-    picked_ref,
+    other_ref,
     owner_ref,
     board_ref,
     flat_ref,
+    picked_ref,
     sem,
 ):
     plane, spot = place_ref[0], place_ref[1]
@@ -311,49 +318,115 @@
 
     blank.wait()
     lax.fori_loop(0, COLUMNS // UNROLL, gather, 0)
-
-
-def spread_normals(normal_ref, side_ref):
     for place in range(COLUMNS // LANES):
-        side_ref[pl.ds(place, 3, stride=24), :] = normal_ref[:, place * LANES : (place + 1) * LANES]
-
-
-def group_normal(side_ref, group):
-    normal = [side_ref[k * 24 + group * 8 : k * 24 + group * 8 + 8, :] for k in range(3)]
+        square = picked_ref[place * LANES : (place + 1) * LANES, :].T
+        other_ref[place * TRACE : (place + 1) * TRACE, :] = square[0:TRACE]
+
+
+def sublane_index():
+    return lax.broadcasted_iota(jnp.int32, (8, LANES), 0)
+
+
+def wide(row):
+    return jnp.broadcast_to(row, (8, LANES))
+
+
+def face_normals(normal_ref, place):
+    lanes = pl.ds(pl.multiple_of(place * LANES, LANES), LANES)
+    normal = [wide(normal_ref[k : k + 1, lanes]) for k in range(3)]
     length = jnp.sqrt(normal[0] * normal[0] + normal[1] * normal[1] + normal[2] * normal[2])
     return normal, length
 
 
-def lift(rate_ref, group, node, terms):
-    first, second = face_nodes(2 * group)[node], face_nodes(2 * group + 1)[node]
-    for v in range(5):
-        at = v * 256 + first * 4
-        rate_ref[at : at + 4, :] = rate_ref[at : at + 4, :] + terms[v][0:4]
-        at = v * 256 + second * 4
-        rate_ref[at : at + 4, :] = rate_ref[at : at + 4, :] + terms[v][4:8]
+def lift(tiles, flux_ref, field_ref, v, block):
+    first = sublane_index() < 4
+    start = pl.multiple_of(v * 16, 16)
+
+    def piece(face, half):
+        return flux_ref[pl.ds((face * BLOCKS + block) * TRACE + half * 8 + start, 8), :]
+
+    tiles = list(tiles)
+    for half in range(2):
+        tiles[half] = tiles[half] + piece(0, half)
+        tiles[6 + half] = tiles[6 + half] + piece(1, half)
+        low, high = piece(2, half), piece(3, half)
+        tiles[4 * half] = tiles[4 * half] + jnp.where(first, low, 0.0)
+        tiles[4 * half + 2] = tiles[4 * half + 2] + jnp.where(first, pltpu.roll(low, 4, 0), 0.0)
+        tiles[4 * half + 1] = tiles[4 * half + 1] + jnp.where(first, 0.0, pltpu.roll(high, 4, 0))
+        tiles[4 * half + 3] = tiles[4 * half + 3] + jnp.where(first, 0.0, high)
+    base = pl.multiple_of(v * 64, 64) + block * 320
+    for tile in range(8):
+        field_ref[pl.ds(base + tile * 8, 8), :] = tiles[tile]
+    for half in range(2):
+        for face in (4, 5):
+            nodes = pl.ds(base + half * 32 + 3 * (face - 4), 8, stride=4)
+            field_ref[nodes, :] = field_ref[nodes, :] + piece(face, half)
+
+
+def turn_indices(code):
+    flip_first = jnp.where(code % 2 == 1, 3, 0)
+    flip_second = jnp.where((code // 2) % 2 == 1, 3, 0)
+    swapped = code >= 4
+    sublane = sublane_index()
+    result = []
+    for half in range(2):
+        i, j = 2 * half + sublane // 4, sublane % 4
+        first = jnp.where(swapped, j, i) ^ flip_first
+        second = jnp.where(swapped, i, j) ^ flip_second
+        result.append(first * 4 + second)
+    return result
 
 
 def volume_kernel(
+    place_ref,
     state_ref,
     register_ref,
     metric_ref,
     normal_ref,
-    rate_ref,
+    code_ref,
+    partner_ref,
+    field_ref,
     own_ref,
-    wave_ref,
+    side_ref,
+    turn_ref,
     rows_ref,
     tensor_ref,
     flux_ref,
     flat_ref,
-    side_ref,
+    rate_ref,
+    term_ref,
 ):
+    low = COLUMNS + place_ref[0] * (PLANE * SLOTS)
     spread_nodes(state_ref, rows_ref)
     spread_flat(state_ref, flat_ref)
-    spread_normals(normal_ref, side_ref)
     for face in range(6):
         for block in range(BLOCKS):
             place = face * BLOCKS + block
             own_ref[place * TRACE : (place + 1) * TRACE, :] = face_trace(state_ref, flat_ref, face, block)
+
+    def own_fluxes(face, carry):
+        for block in range(BLOCKS):
+            place = face * BLOCKS + block
+            normal, length = face_normals(normal_ref, place)
+            start = pl.multiple_of(place * TRACE, TRACE)
+            side = pl.multiple_of(place * SIDE, 16)
+            for k, value in enumerate(normal + [length]):
+                side_ref[pl.ds(side + 16 + 8 * k, 8), :] = value
+            partner = wide(partner_ref[pl.ds(place, 1), :])
+            late = (partner >= COLUMNS) & ((partner < low) | (partner >= low + PLANE * SLOTS))
+            late = jnp.where(late, 16, 0)
+            for half, turn in enumerate(turn_indices(wide(code_ref[pl.ds(place, 1), :]))):
+                turn_ref[pl.ds(pl.multiple_of(place * 16, 16) + half * 8, 8), :] = turn + late
+            for half in range(2):
+                at = start + half * 8
+                own = [own_ref[pl.ds(at + v * 16, 8), :] for v in range(5)]
+                terms, wave = normal_flux(own, normal, length)
+                for v in range(5):
+                    term_ref[pl.ds(at + v * 16, 8), :] = (0.5 * LIFT_FACTOR) * terms[v]
+                side_ref[pl.ds(side + half * 8, 8), :] = wave
+        return carry
+
+    lax.fori_loop(0, 6, own_fluxes, 0)
     for direction in range(3):
         for half in range(2):
             for block in range(BLOCKS):
@@ -423,21 +496,19 @@
         return carry
 
     lax.fori_loop(0, 5, diverge, 0)
-    for group in range(3):
-        normal, length = group_normal(side_ref, group)
-        start = group * 8 * TRACE
-        for node in range(16):
-            own = [own_ref[pl.ds(start + v * 16 + node, 8, stride=TRACE), :] for v in range(5)]
-            terms, wave = normal_flux(own, normal, length)
-            lift(rate_ref, group, node, [(0.5 * LIFT_FACTOR) * term for term in terms])
-            at = (group * 16 + node) * 8
-            wave_ref[at : at + 8, :] = wave
-    for v in range(5):
-        for tile in range(8):
-            for block in range(BLOCKS):
-                at = pl.ds(v * 256 + tile * 32 + block, 8, stride=BLOCKS)
+
+    def gather_terms(v, carry):
+        base = pl.multiple_of(v * 256, 256)
+        for block in range(BLOCKS):
+            tiles = []
+            for tile in range(8):
                 old = register_ref[v, tile * 8 : tile * 8 + 8, tile_lanes(block)]
-                rate_ref[at, :] = rate_ref[at, :] + SECTION_KEEP * old
+                rate = rate_ref[pl.ds(base + tile * 32 + block, 8, stride=BLOCKS), :]
+                tiles.append(rate + SECTION_KEEP * old)
+            lift(tiles, term_ref, field_ref, v, block)
+        return carry
+
+    lax.fori_loop(0, 5, gather_terms, 0)
 
 
 def normal_flux(values, normal, length):
@@ -459,28 +530,29 @@
 def finish_kernel(
     place_ref,
     owner_hbm,
-    early_hbm,
+    other_hbm,
     own_hbm,
-    wave_hbm,
-    relay_ref,
-    code_ref,
-    normal_ref,
+    side_hbm,
+    turn_hbm,
     rate_hbm,
     state_hbm,
+    relay_ref,
     section_hbm,
     advanced_hbm,
-    owner_ref,
+    low_ref,
+    high_ref,
     section_ref,
     advanced_ref,
     board_ref,
     picked_ref,
     other_ref,
-    turned_ref,
+    own_ref,
     side_ref,
+    turn_ref,
     rate_ref,
-    own_ref,
-    wave_ref,
     state_ref,
+    term_ref,
+    field_ref,
     sems,
 ):
     plane, spot = place_ref[0], place_ref[1]
@@ -488,23 +560,21 @@
     low_slot = jnp.maximum(COLUMNS + ((plane - 1) * PLANE + NEAR) * SLOTS, 0)
     high_slot = jnp.minimum(COLUMNS + (plane + 1) * PLANE * SLOTS, COLUMNS + DEVICES * SLOTS - window)
     sources = [
-        (owner_hbm.at[pl.ds(pl.multiple_of(low_slot, 512), window)], owner_ref.at[0]),
-        (owner_hbm.at[pl.ds(pl.multiple_of(high_slot, 512), window)], owner_ref.at[1]),
+        (owner_hbm.at[pl.ds(pl.multiple_of(low_slot, 512), window)], low_ref),
+        (owner_hbm.at[pl.ds(pl.multiple_of(high_slot, 512), window)], high_ref),
+        (other_hbm, other_ref),
+        (own_hbm, own_ref),
+        (turn_hbm, turn_ref),
+        (side_hbm, side_ref),
+        (rate_hbm, rate_ref),
+        (state_hbm, state_ref),
     ]
-    for part in range(3):
-        rows = pl.ds(part * GROUP, GROUP)
-        sources.append((early_hbm.at[rows, :], picked_ref.at[rows, :]))
-    for part in range(3):
-        rows = pl.ds(part * 8 * TRACE, 8 * TRACE)
-        sources.append((own_hbm.at[rows, :], own_ref.at[rows, :]))
-    sources += [(wave_hbm, wave_ref), (rate_hbm, rate_ref), (state_hbm, state_ref)]
     copies = [
         pltpu.make_async_copy(source, target, sems.at[k])
         for k, (source, target) in enumerate(sources)
     ]
     for copy in copies:
         copy.start()
-    spread_normals(normal_ref, side_ref)
 
     def receive(peer, block):
         parts = [relay_ref[block + k // 5, 8 * (k % 5) : 8 * (k % 5) + 8, :] for k in range(5 * BATCH)]
@@ -527,23 +597,23 @@
     high = (jnp.maximum(spot - NEAR + 1, 0) + BATCH - 1) // BATCH
     lax.fori_loop(0, high, receive_high, 0)
 
-    def place_rows(side, base, step):
+    def place_rows(columns_ref, base, step):
         at = step * UNROLL
-        columns = [owner_ref[side, at + k] for k in range(UNROLL)]
+        columns = [columns_ref[at + k] for k in range(UNROLL)]
         rows = [board_ref[pl.ds(base * SLOTS + at + k, 1), :] for k in range(UNROLL)]
         for k in range(UNROLL):
             picked_ref[pl.ds(columns[k], 1), :] = rows[k]
 
     def place_low(step, carry):
-        place_rows(0, (plane - 1) * PLANE + NEAR + MARGIN, step)
+        place_rows(low_ref, (plane - 1) * PLANE + NEAR + MARGIN, step)
         return carry
 
     def place_high(step, carry):
-        place_rows(1, (plane + 1) * PLANE + MARGIN, step)
+        place_rows(high_ref, (plane + 1) * PLANE + MARGIN, step)
         return carry
 
     chunk = SLOTS // UNROLL
-    for copy in copies[:5]:
+    for copy in copies[:2]:
         copy.wait()
 
     @pl.when(plane > 0)
@@ -554,59 +624,74 @@
     def _():
         lax.fori_loop(0, jnp.maximum(spot - NEAR + 1, 0) * chunk, place_high, 0)
 
-    for place in range(COLUMNS // LANES):
-        square = picked_ref[place * LANES : (place + 1) * LANES, :].T
-        other_ref[place * TRACE : (place + 1) * TRACE, :] = square[0:TRACE]
-    for copy in copies[5:]:
+    for copy in copies[2:]:
         copy.wait()
-    for group in range(3):
-        code = code_ref[group * 8 : group * 8 + 8, :]
-        flip_first = code % 2 == 1
-        flip_second = (code // 2) % 2 == 1
-        swapped = code >= 4
-        start = group * 8 * TRACE
-        for v in range(5):
-            grid = [
-                [other_ref[pl.ds(start + v * 16 + i * 4 + j, 8, stride=TRACE), :] for j in range(4)]
-                for i in range(4)
+
+    def far_fluxes(face, carry):
+        for block in range(BLOCKS):
+            place = face * BLOCKS + block
+            square = picked_ref[pl.ds(pl.multiple_of(place * LANES, LANES), LANES), :].T
+            start = pl.multiple_of(place * TRACE, TRACE)
+            side = pl.multiple_of(place * SIDE, 16)
+            at = pl.multiple_of(place * 16, 16)
+            turns = [turn_ref[pl.ds(at + half * 8, 8), :] for half in range(2)]
+            late = turns[0] >= 16
+            known = [
+                jnp.where(late, square[8 * k : 8 * k + 8], other_ref[pl.ds(start + 8 * k, 8), :])
+                for k in range(10)
             ]
-            grid = [[jnp.where(flip_first, grid[3 - i][j], grid[i][j]) for j in range(4)] for i in range(4)]
-            grid = [[jnp.where(flip_second, grid[i][3 - j], grid[i][j]) for j in range(4)] for i in range(4)]
-            for i in range(4):
-                for j in range(4):
-                    value = grid[i][j] if i == j else jnp.where(swapped, grid[j][i], grid[i][j])
-                    at = ((i * 4 + j) * 5 + v) * 8
-                    turned_ref[at : at + 8, :] = value
-        normal, length = group_normal(side_ref, group)
-        for node in range(16):
-            own = [own_ref[pl.ds(start + v * 16 + node, 8, stride=TRACE), :] for v in range(5)]
-            far = [turned_ref[(node * 5 + v) * 8 : (node * 5 + v) * 8 + 8, :] for v in range(5)]
-            far_terms, far_wave = normal_flux(far, normal, length)
-            at = (group * 16 + node) * 8
-            bound = jnp.maximum(wave_ref[at : at + 8, :], far_wave)
-            viscous = bound + length
-            terms = [
-                (0.5 * LIFT_FACTOR)
-                * ((bound if v == 0 else viscous) * (far[v] - own[v]) - far_terms[v])
-                for v in range(5)
-            ]
-            lift(rate_ref, group, node, terms)
-
+            normal = [side_ref[pl.ds(side + 16 + 8 * k, 8), :] for k in range(3)]
+            length = side_ref[pl.ds(side + 40, 8), :]
+            for half in range(2):
+                upper = turns[half] % 16 >= 8
+                sublane = turns[half] % 8
+                far = []
+                for v in range(5):
+                    parts = [
+                        jnp.take_along_axis(known[2 * v + k], sublane, axis=0, mode="promise_in_bounds")
+                        for k in range(2)
+                    ]
+                    far.append(jnp.where(upper, parts[1], parts[0]))
+                far_terms, far_wave = normal_flux(far, normal, length)
+                bound = jnp.maximum(side_ref[pl.ds(side + half * 8, 8), :], far_wave)
+                viscous = bound + length
+                for v in range(5):
+                    rows = pl.ds(start + v * 16 + half * 8, 8)
+                    weight = bound if v == 0 else viscous
+                    term_ref[rows, :] = (0.5 * LIFT_FACTOR) * (
+                        weight * (far[v] - own_ref[rows, :]) - far_terms[v]
+                    )
+        return carry
+
+    lax.fori_loop(0, 6, far_fluxes, 0)
     top = jnp.max(jnp.max(relay_ref[:, MESSAGE:, :], axis=0))
     scale = CFL_NUMBER / top * SECTION_STEP
-    results = []
-    for v in range(5):
-        for tile in range(8):
-            for block in range(BLOCKS):
-                nodes, lanes = slice(tile * 8, tile * 8 + 8), tile_lanes(block)
-                section = rate_ref[pl.ds(v * 256 + tile * 32 + block, 8, stride=BLOCKS), :]
+
+    def results(v):
+        return [
+            pltpu.make_async_copy(section_ref.at[v], section_hbm.at[v], sems.at[2 * v]),
+            pltpu.make_async_copy(advanced_ref.at[v], advanced_hbm.at[v], sems.at[2 * v + 1]),
+        ]
+
+    def update(v, carry):
+        for block in range(BLOCKS):
+            lanes = tile_lanes(block)
+            base = pl.multiple_of(v * 64, 64) + block * 320
+            tiles = [rate_ref[pl.ds(base + tile * 8, 8), :] for tile in range(8)]
+            lift(tiles, term_ref, field_ref, v, block)
+            for tile in range(8):
+                nodes = slice(tile * 8, tile * 8 + 8)
+                section = field_ref[pl.ds(base + tile * 8, 8), :]
                 section_ref[v, nodes, lanes] = section
                 advanced_ref[v, nodes, lanes] = state_ref[v, nodes, lanes] + scale * section
-        for source, target in ((section_ref, section_hbm), (advanced_ref, advanced_hbm)):
-            results.append(pltpu.make_async_copy(source.at[v], target.at[v], sems.at[len(results)]))
-            results[-1].start()
-    for copy in results:
-        copy.wait()
+        for copy in results(v):
+            copy.start()
+        return carry
+
+    lax.fori_loop(0, 5, update, 0)
+    for v in range(5):
+        for copy in results(v):
+            copy.wait()
 
 
 def smem():
@@ -635,93 +720,99 @@
 
 def anywhere():
     return pl.BlockSpec(memory_space=pl.ANY)
+
+
+def in_hbm_shape(*sizes):
+    return pltpu.HBM(sizes, jnp.float32)
 
 
 def pack(place, partner, state):
     return pl.pallas_call(
         pack_kernel,
         out_shape=(
-            scratch(PLANE * SLOTS, LANES),
+            in_hbm_shape(PLANE * MESSAGE, LANES),
             shape(CROSS * MESSAGE + 8, LANES),
             shape(CROSS * MESSAGE + 8, LANES),
             shape(8, LANES),
         ),
         in_specs=[smem(), hbm(), hbm()],
-        out_specs=(vmem(),) * 4,
+        out_specs=(hbm(), vmem(), vmem(), vmem()),
         scratch_shapes=[
+            scratch(PLANE * MESSAGE, LANES),
             pltpu.SMEM((COLUMNS,), jnp.int32),
             scratch(5, 64, ELEMENTS),
             scratch(COLUMNS, LANES),
             scratch(COLUMNS + (DEVICES + CROSS) * SLOTS, LANES),
             scratch(1280, LANES),
-            pltpu.SemaphoreType.DMA((5,)),
+            pltpu.SemaphoreType.DMA((5 + PLANE // BATCH,)),
         ],
         compiler_params=params(),
         name="pack",
     )(place, partner, state)
 
 
-def pack_plane(board):
-    return pl.pallas_call(
-        pack_plane_kernel,
-        out_shape=pltpu.HBM((PLANE * MESSAGE, LANES), jnp.float32),
-        in_specs=[vmem()],
-        out_specs=hbm(),
-        scratch_shapes=[
-            scratch(PLANE * MESSAGE, LANES),
-            pltpu.SemaphoreType.DMA((PLANE // BATCH,)),
-        ],
-        compiler_params=params(),
-        name="pack_plane",
-    )(board)
-
-
-def volume(state, register, metric, normal):
+def volume(place, state, register, metric, normal, code, partner):
     return pl.pallas_call(
         volume_kernel,
         out_shape=(
-            shape(1280, LANES),
-            pltpu.HBM((COLUMNS // LANES * TRACE, LANES), jnp.float32),
-            shape(COLUMNS // LANES * 16, LANES),
+            in_hbm_shape(1280, LANES),
+            in_hbm_shape(24 * TRACE, LANES),
+            in_hbm_shape(24 * SIDE, LANES),
+            pltpu.HBM((24 * 16, LANES), jnp.int32),
         ),
-        in_specs=[vmem()] * 4,
-        out_specs=(vmem(),) * 3,
+        in_specs=[smem()] + [vmem()] * 6,
+        out_specs=(vmem(),) * 4,
         scratch_shapes=[
             scratch(1280, LANES),
             scratch(72, LANES),
             scratch(3, 1280, LANES),
             scratch(1280, LANES),
-            scratch(72, LANES),
+            scratch(1280, LANES),
+            scratch(24 * TRACE, LANES),
         ],
         compiler_params=params(),
         name="volume",
-    )(state, register, metric, normal)
-
-
-def relay(place, up, down, best, far, rate):
+    )(place, state, register, metric, normal, code, partner)
+
+
+def relay(place, up, down, best, rate):
     return pl.pallas_call(
         relay_kernel,
-        out_shape=shape(PLANE, MESSAGE + 8, LANES),
-        in_specs=[smem()] + [vmem()] * 4 + [anywhere()],
-        out_specs=vmem(),
+        out_shape=(in_hbm_shape(PLANE, MESSAGE + 8, LANES), shape(8, LANES)),
+        in_specs=[smem()] + [vmem()] * 3 + [hbm()],
+        out_specs=(vmem(), vmem()),
         compiler_params=params(),
-        cost_estimate=pl.CostEstimate(flops=100000000000, bytes_accessed=100000000, transcendentals=0),
+        cost_estimate=pl.CostEstimate(flops=10**11, bytes_accessed=10**8, transcendentals=0),
         name="relay",
-    )(place, up, down, best, far, rate)
+    )(place, up, down, best, rate)
+
+
+def spread_top(three, far, relayed):
+    return pl.pallas_call(
+        top_kernel,
+        out_shape=in_hbm_shape(PLANE, MESSAGE + 8, LANES),
+        in_specs=[vmem(), vmem(), hbm()],
+        out_specs=hbm(),
+        scratch_shapes=[scratch(PLANE, 8, LANES), pltpu.SemaphoreType.DMA],
+        input_output_aliases={2: 0},
+        compiler_params=params(),
+        name="top",
+    )(three, far, relayed)
 
 
 def early(place, partner, blank, state, plane):
     return pl.pallas_call(
         early_kernel,
         out_shape=(
-            pltpu.HBM((COLUMNS, LANES), jnp.float32),
-            jax.ShapeDtypeStruct((COLUMNS + DEVICES * SLOTS,), jnp.int32),
+            in_hbm_shape(24 * TRACE, LANES),
+            pltpu.HBM((COLUMNS + DEVICES * SLOTS,), jnp.int32),
         ),
         in_specs=[smem(), smem(), anywhere(), vmem(), vmem()],
         out_specs=(vmem(), smem()),
         scratch_shapes=[
             scratch(COLUMNS + DEVICES * SLOTS, LANES),
             scratch(1280, LANES),
+            scratch(COLUMNS, LANES),
             pltpu.SemaphoreType.DMA,
         ],
         compiler_params=params(),
@@ -729,30 +820,33 @@
     )(place, partner, blank, state, plane)
 
 
-def finish(place, owner, picked, own, wave, relayed, code, normal, rate, state):
+def finish(place, owner, other, own, side, turn, rate, state, relayed):
+    held = [in_hbm(value) for value in (owner, other, own, side, turn, rate, state)]
     return pl.pallas_call(
         finish_kernel,
-        out_shape=(pltpu.HBM((5, 64, ELEMENTS), jnp.float32),) * 2,
-        in_specs=[smem(), hbm(), hbm(), hbm(), anywhere(), vmem(), vmem(), vmem(), anywhere(), anywhere()],
+        out_shape=(in_hbm_shape(5, 64, ELEMENTS),) * 2,
+        in_specs=[smem()] + [hbm()] * 7 + [vmem()],
         out_specs=(hbm(), hbm()),
         scratch_shapes=[
-            pltpu.SMEM((2, CROSS * SLOTS), jnp.int32),
+            pltpu.SMEM((CROSS * SLOTS,), jnp.int32),
+            pltpu.SMEM((CROSS * SLOTS,), jnp.int32),
             scratch(5, 64, ELEMENTS),
             scratch(5, 64, ELEMENTS),
             scratch((DEVICES + 2 * MARGIN) * SLOTS, LANES),
             scratch(COLUMNS + 8, LANES),
-            scratch(COLUMNS // LANES * TRACE, LANES),
-            scratch(16 * 5 * 8, LANES),
-            scratch(72, LANES),
+            scratch(24 * TRACE, LANES),
+            scratch(24 * TRACE, LANES),
+            scratch(24 * SIDE, LANES),
+            pltpu.VMEM((24 * 16, LANES), jnp.int32),
             scratch(1280, LANES),
-            scratch(COLUMNS // LANES * TRACE, LANES),
-            scratch(COLUMNS // LANES * 16, LANES),
             scratch(5, 64, ELEMENTS),
-            pltpu.SemaphoreType.DMA((11,)),
+            scratch(24 * TRACE, LANES),
+            scratch(1280, LANES),
+            pltpu.SemaphoreType.DMA((10,)),
         ],
         compiler_params=params(),
         name="finish",
-    )(place, owner, picked, own, wave, relayed, code, normal, rate, state)
+    )(place, *held, relayed)
 
 
 def in_hbm(value):
@@ -772,21 +866,27 @@
     spot = lax.axis_index(("r", "x")).astype(jnp.int32)
     place = jnp.stack([plane, spot])
     state = state.transpose(1, 0, 2)
-    board, up, down, best = pack(place, in_hbm(partner), in_hbm(state))
+    rows = (COLUMNS // LANES, LANES)
+    in_plane, up, down, best = pack(place, in_hbm(partner), in_hbm(state))
     from_below = along_y(up, 1)
     from_above = along_y(down, -1)
     far = along_y(best, 2)
-    in_plane = pack_plane(in_vmem(board))
     got = lax.all_to_all(in_plane, ("r", "x"), 0, 0, tiled=True)
-    rate, own, wave = volume(state, register.transpose(1, 0, 2), metric, face_normal)
-    relayed = relay(place, from_below, from_above, best, far, rate)
+    rate, own, side, turn = volume(
+        place,
+        state,
+        register.transpose(1, 0, 2),
+        metric,
+        face_normal,
+        flip_code.reshape(rows),
+        partner.reshape(rows),
+    )
+    relayed, three = relay(place, from_below, from_above, best, in_hbm(rate))
+    relayed = spread_top(three, far, in_hbm(relayed))
     relayed = lax.all_to_all(relayed, ("r", "x"), 0, 0, tiled=True)
     blank = jnp.full((COLUMNS + DEVICES * SLOTS,), COLUMNS, jnp.int32)
-    picked, owner = early(place, partner, blank, state, got)
-    code = flip_code.reshape(COLUMNS // LANES, LANES)
-    section, advanced = finish(
-        place, in_hbm(owner), in_hbm(picked), in_hbm(own), wave, relayed, code, face_normal, rate, state
-    )
+    other, owner = early(place, partner, blank, state, got)
+    section, advanced = finish(place, owner, other, own, side, turn, rate, state, relayed)
     return section.transpose(1, 0, 2), advanced.transpose(1, 0, 2)
 
 

time: 60.9 us -> 56.9 us (0.934)
  the two profiles are of different devices: /device:TPU:8 before, /device:TPU:1 now
where the time goes in v4:
time: 56.9 us; the launch traced here: 56.5 us
  Pallas kernels  27 us (47%)
  starting transfers between devices  19.2 us (34%)
  waiting for transfers between devices  9.46 us (17%)
  between operations  0.72 us (1%)
    all_to_all x1, starting transfers between devices, on_device(): got = lax.all_to_all(in_plane, ('r', 'x'), 0, 0, tiled=True)  9.16 us
    pallas_call x1, Pallas kernels, early(): pl.pallas_call(early_kernel, out_shape=(in_hbm_shape(24 * TRACE, LANES),...  7.88 us
    pallas_call x1, Pallas kernels, pack(): pl.pallas_call(pack_kernel, out_shape=(in_hbm_shape(PLANE * MESSAGE, LANE...  7.1 us
    all_to_all x1, waiting for transfers between devices, on_device(): relayed = lax.all_to_all(relayed, ('r', 'x'), 0, 0, tiled=True)  5.77 us
    ppermute x3, starting transfers between devices, along_y(): return lax.ppermute(value, 'y', [(i, (i + steps) % 4) for i in range(4)])  5.5 us
    pallas_call x1, Pallas kernels, finish(): pl.pallas_call(finish_kernel, out_shape=(in_hbm_shape(5, 64, ELEMENTS),)...  5.05 us
    all_to_all x1, starting transfers between devices, on_device(): relayed = lax.all_to_all(relayed, ('r', 'x'), 0, 0, tiled=True)  4.57 us
    pallas_call x1, Pallas kernels, volume(): pl.pallas_call(volume_kernel, out_shape=(in_hbm_shape(1280, LANES), in_hb...  4.27 us
  transfers between devices with their start and end apart: 5, of which 2 were waited for; matrix products, arithmetic and copies ran while one was open for 0% of the time, Pallas kernels for 26%

profile of v4, /device:TPU:1, one launch (start us, length us, event | category | flops | bytes accessed | tf_op | source)
XLA Modules:
  0.0 56.5 jit_solution(16039994200565083719)
XLA Ops:
  0.6 0.1 pad_add_fusion.place_ref
  0.7 0.0 copy-start.2
  0.7 0.0 copy-start.3
  0.7 0.0 copy-start.4
  0.7 0.0 copy-start.5
  0.7 7.1 %pack.1 = (f32[1280,128]{1,0:T(8,128)}, f32[968,128]{1,0:T(8,128)}, f32[968,128]{1,0:T(8,128)S(1)}, f32[8,128]{1,0:T(8,128)S(1)}) custom-call(s32[2]{0:T(128)S(1)} %pad_add_fusion.place_ref, s32[3072]{0:T(1024)} %partner_ref.1, f32[5,64,512]{2,1,0:T(8,128)} %bitcast.10), custom_call_target="tpu_custom_call" | custom-call | tf_op jit(solution)/shard_map/pack/pallas_call | solution.py:730
  7.8 2.2 %collective-permute-start = (f32[968,128]{1,0:T(8,128)}, f32[968,128]{1,0:T(8,128)S(1)}, u32[]{:S(2)}, u32[]{:S(2)}) collective-permute-start(f32[968,128]{1,0:T(8,128)} %get-tuple-element.23), channel_id=1, source_target_pairs={{0,32},{32,64},{64,96},{96,0},{1,33},{33,65},{65,97},{97,1},{2,34}... | collective-permute-start | bytes 1486856 | tf_op jit(solution)/shard_map/ppermute | solution.py:861
  10.0 1.5 %collective-permute-start.1 = (f32[968,128]{1,0:T(8,128)S(1)}, f32[968,128]{1,0:T(8,128)}, u32[]{:S(2)}, u32[]{:S(2)}) collective-permute-start(f32[968,128]{1,0:T(8,128)S(1)} %get-tuple-element.24), channel_id=1, source_target_pairs={{0,96},{32,0},{64,32},{96,64},{1,97},{33,1},{65,33},{97,65},{2,98}... | collective-permute-start | bytes 1486856 | tf_op jit(solution)/shard_map/ppermute | solution.py:861
  11.5 0.0 copy-start
  11.6 0.0 copy-start.1
  11.6 9.2 %all-to-all-start = ((f32[32,40,128]{2,1,0:T(8,128)}), f32[32,40,128]{2,1,0:T(8,128)S(1)}, u32[]{:S(2)}, u32[]{:S(2)}) async-start(f32[32,40,128]{2,1,0:T(8,128)} %bitcast.18), calls=%async_computation | async-start | bytes 1310720 | tf_op jit(solution)/shard_map/all_to_all | solution.py:874
  20.7 1.8 %collective-permute-start.2 = (f32[8,128]{1,0:T(8,128)S(1)}, f32[8,128]{1,0:T(8,128)S(1)}, u32[]{:S(2)}, u32[]{:S(2)}) collective-permute-start(f32[8,128]{1,0:T(8,128)S(1)} %get-tuple-element.25.best_ref), channel_id=1, source_target_pairs={{0,64},{32,96},{64,0},{96,32},{1,65},{33,97},{65,1},{97,33},{2,66}... | collective-permute-start | bytes 12296 | tf_op jit(solution)/shard_map/ppermute | solution.py:861
  22.5 0.0 copy-done.2
  22.5 0.0 copy-done.3
  22.5 0.0 copy-done.4
  22.5 0.0 copy-done.5
  22.5 0.0 copy-done
  22.5 0.0 copy-done.1
  22.5 4.3 %volume.1 = (f32[1280,128]{1,0:T(8,128)}, f32[1920,128]{1,0:T(8,128)}, f32[1152,128]{1,0:T(8,128)}, s32[384,128]{1,0:T(8,128)}) custom-call(s32[2]{0:T(128)S(1)} %pad_add_fusion.place_ref, f32[5,64,512]{2,1,0:T(8,128)S(1)} %bitcast.12, f32[5,64,512]{2,1,0:T(8,128)S(1)} %bitcast.15, f32[3,3,512]{2,1,0:T(4,128)S(1)} %copy-done.4, f32[3,3072]{1,0:T(4,128)S(1)} %copy-done.3, ...), custom_call_target="tpu_custom_call" | custom-call | tf_op jit(solution)/shard_map/volume/pallas_call | solution.py:755
  26.8 0.0 collective-permute-done.up_ref
  26.8 0.0 collective-permute-done.1.down_ref
  26.8 2.0 %relay.1 = (f32[32,48,128]{2,1,0:T(8,128)}, f32[8,128]{1,0:T(8,128)S(1)}) custom-call(s32[2]{0:T(128)S(1)} %pad_add_fusion.place_ref, f32[968,128]{1,0:T(8,128)S(1)} %collective-permute-done.up_ref, f32[968,128]{1,0:T(8,128)} %collective-permute-done.1.down_ref, f32[8,128]{1,0:T(8,128)S(1)} %get-tuple-element.25.best_ref, f32[1280,128]{1,0:T(8,128)} %get-tuple-element.22.rate_hbm), custom_call_target="tpu_custom_call" | custom-call | flops 99999997952 | bytes 100000000 | tf_op jit(solution)/shard_map/relay/pallas_call | solution.py:779
  28.9 0.0 collective-permute-done.2.far_ref
  28.9 0.7 %top.1 = f32[32,48,128]{2,1,0:T(8,128)} custom-call(f32[8,128]{1,0:T(8,128)S(1)} %get-tuple-element.26.three_ref, f32[8,128]{1,0:T(8,128)S(1)} %collective-permute-done.2.far_ref, f32[32,48,128]{2,1,0:T(8,128)} %get-tuple-element.27.relay_in), custom_call_target="tpu_custom_call", output_to_operand_aliasing={{}: (2, {})} | custom-call | tf_op jit(solution)/shard_map/top/pallas_call | solution.py:791
  29.6 3.7 %all-to-all-done = f32[32,40,128]{2,1,0:T(8,128)S(1)} async-done(((f32[32,40,128]{2,1,0:T(8,128)}), f32[32,40,128]{2,1,0:T(8,128)S(1)}, u32[]{:S(2)}, u32[]{:S(2)}) %all-to-all-start) | async-done | bytes 655392 | tf_op jit(solution)/shard_map/all_to_all | solution.py:874
  33.2 4.6 %all-to-all-start.1 = ((f32[32,48,128]{2,1,0:T(8,128)}), f32[32,48,128]{2,1,0:T(8,128)S(1)}, u32[]{:S(2)}, u32[]{:S(2)}) async-start(f32[32,48,128]{2,1,0:T(8,128)} %top.1), calls=%async_computation.1 | async-start | bytes 1572864 | tf_op jit(solution)/shard_map/all_to_all | solution.py:886
  37.8 7.9 %early.1 = (f32[1920,128]{1,0:T(8,128)}, s32[11264]{0:T(1024)}) custom-call(s32[2]{0:T(128)S(1)} %pad_add_fusion.place_ref, s32[3072]{0:T(1024)S(1)} %copy-done.2, s32[11264]{0:T(1024)S(1)} %broadcast_in_dim.3.blank_hbm, f32[5,64,512]{2,1,0:T(8,128)S(1)} %bitcast.13, f32[1280,128]{1,0:T(8,128)S(1)} %bitcast.14), custom_call_target="tpu_custom_call" | custom-call | tf_op jit(solution)/shard_map/early/pallas_call | solution.py:804
  45.7 5.8 %all-to-all-done.1.relay_ref = f32[32,48,128]{2,1,0:T(8,128)S(1)} async-done(((f32[32,48,128]{2,1,0:T(8,128)}), f32[32,48,128]{2,1,0:T(8,128)S(1)}, u32[]{:S(2)}, u32[]{:S(2)}) %all-to-all-start.1) | async-done | bytes 786464 | tf_op jit(solution)/shard_map/all_to_all | solution.py:886
  51.5 5.0 %finish.1 = (f32[5,64,512]{2,1,0:T(8,128)}, f32[5,64,512]{2,1,0:T(8,128)}) custom-call(s32[2]{0:T(128)S(1)} %pad_add_fusion.place_ref, s32[11264]{0:T(1024)} %get-tuple-element.17.owner_hbm, f32[1920,128]{1,0:T(8,128)} %get-tuple-element.18.other_hbm, f32[1920,128]{1,0:T(8,128)} %get-tuple-element.19.own_hbm, f32[1152,128]{1,0:T(8,128)} %get-tuple-element.20.side_hbm, ...), custom_call_target="tpu_custom_call" | custom-call | tf_op jit(solution)/shard_map/finish/pallas_call | solution.py:825
  (1 shorter events, 0.0 us)
Async XLA Ops:
  0.7 21.8 %copy-start.2 = (s32[3072]{0:T(1024)S(1)}, s32[3072]{0:T(1024)}, u32[]{:S(2)}) copy-start(s32[3072]{0:T(1024)} %partner_ref.1) | copy-start | bytes 36868
  0.7 21.8 %copy-start.3 = (f32[3,3072]{1,0:T(4,128)S(1)}, f32[3,3072]{1,0:T(4,128)}, u32[]{:S(2)}) copy-start(f32[3,3072]{1,0:T(4,128)} %normal_ref.1) | copy-start | bytes 110596
  0.7 21.8 %copy-start.4 = (f32[3,3,512]{2,1,0:T(4,128)S(1)}, f32[3,3,512]{2,1,0:T(4,128)}, u32[]{:S(2)}) copy-start(f32[3,3,512]{2,1,0:T(4,128)} %metric_ref.1) | copy-start | bytes 55300
  0.7 21.8 %copy-start.5 = (s32[3072]{0:T(1024)S(1)}, s32[3072]{0:T(1024)}, u32[]{:S(2)}) copy-start(s32[3072]{0:T(1024)} %param.13) | copy-start | bytes 36868
  7.8 19.0 %collective-permute-start = (f32[968,128]{1,0:T(8,128)}, f32[968,128]{1,0:T(8,128)S(1)}, u32[]{:S(2)}, u32[]{:S(2)}) collective-permute-start(f32[968,128]{1,0:T(8,128)} %get-tuple-element.23), channel_id=1, source_target_pairs={{0,32},{32,64},{64,96},{96,0},{1,33},{33,65},{65,97},{97,1},{2,34}... | collective-permute-start | bytes 1486856 | tf_op jit(solution)/shard_map/ppermute | solution.py:861
  10.0 16.8 %collective-permute-start.1 = (f32[968,128]{1,0:T(8,128)S(1)}, f32[968,128]{1,0:T(8,128)}, u32[]{:S(2)}, u32[]{:S(2)}) collective-permute-start(f32[968,128]{1,0:T(8,128)S(1)} %get-tuple-element.24), channel_id=1, source_target_pairs={{0,96},{32,0},{64,32},{96,64},{1,97},{33,1},{65,33},{97,65},{2,98}... | collective-permute-start | bytes 1486856 | tf_op jit(solution)/shard_map/ppermute | solution.py:861
  11.5 11.0 %copy-start = (f32[64,5,512]{2,0,1:T(8,128)S(1)}, f32[64,5,512]{2,0,1:T(8,128)}, u32[]{:S(2)}) copy-start(f32[64,5,512]{2,0,1:T(8,128)} %param.8) | copy-start | bytes 1966084
  11.6 11.0 %copy-start.1 = (f32[64,5,512]{2,0,1:T(8,128)S(1)}, f32[64,5,512]{2,0,1:T(8,128)}, u32[]{:S(2)}) copy-start(f32[64,5,512]{2,0,1:T(8,128)} %param.9) | copy-start | bytes 1966084
  11.6 21.7 %all-to-all-start = ((f32[32,40,128]{2,1,0:T(8,128)}), f32[32,40,128]{2,1,0:T(8,128)S(1)}, u32[]{:S(2)}, u32[]{:S(2)}) async-start(f32[32,40,128]{2,1,0:T(8,128)} %bitcast.18), calls=%async_computation | async-start | bytes 1310720 | tf_op jit(solution)/shard_map/all_to_all | solution.py:874
  20.7 8.1 %collective-permute-start.2 = (f32[8,128]{1,0:T(8,128)S(1)}, f32[8,128]{1,0:T(8,128)S(1)}, u32[]{:S(2)}, u32[]{:S(2)}) collective-permute-start(f32[8,128]{1,0:T(8,128)S(1)} %get-tuple-element.25.best_ref), channel_id=1, source_target_pairs={{0,64},{32,96},{64,0},{96,32},{1,65},{33,97},{65,1},{97,33},{2,66}... | collective-permute-start | bytes 12296 | tf_op jit(solution)/shard_map/ppermute | solution.py:861
  33.2 18.2 %all-to-all-start.1 = ((f32[32,48,128]{2,1,0:T(8,128)}), f32[32,48,128]{2,1,0:T(8,128)S(1)}, u32[]{:S(2)}, u32[]{:S(2)}) async-start(f32[32,48,128]{2,1,0:T(8,128)} %top.1), calls=%async_computation.1 | async-start | bytes 1572864 | tf_op jit(solution)/shard_map/all_to_all | solution.py:886

commit v5 on v4

--- a/solution.py
+++ b/solution.py
@@ -23,7 +23,7 @@
 GROUP = COLUMNS // 3
 MESSAGE = TRACE * SLOTS // LANES
 UNROLL = 32
-SIDE = 48
+SIDE = 24
 BATCH = 4
 AXES = ("y", "r", "x")
 PLANE = 32
@@ -63,7 +63,7 @@
 
 
 def tile_lanes(block):
-    return slice(block * LANES, (block + 1) * LANES)
+    return pl.ds(aligned(block * LANES, LANES), LANES)
 
 
 def spread_nodes(state_ref, rows_ref):
@@ -84,11 +84,11 @@
         return jnp.concatenate(
             [state_ref[v, i * 16 + side * 4 : i * 16 + side * 4 + 4, lanes] for i in range(4)], axis=0
         )
-    return flat_ref[pl.ds(block * 320 + v * 64 + side, 16, stride=4), :]
-
-
-def aligned(row):
-    return row if isinstance(row, int) else pl.multiple_of(row, 8)
+    return flat_ref[pl.ds(aligned(block * 320, 64) + v * 64 + side, 16, stride=4), :]
+
+
+def aligned(row, step=8):
+    return row if isinstance(row, int) else pl.multiple_of(row, step)
 
 
 def lane_index(shape):
@@ -191,18 +191,26 @@
         copy.start()
     for copy in copies[1:]:
         copy.wait()
-    build_tables(state_ref, flat_ref, table_ref)
+    spread_flat(state_ref, flat_ref)
     copies[0].wait()
-
-    def scatter(step, carry):
-        base = step * UNROLL
-        targets = [partner_ref[base + k] for k in range(UNROLL)]
-        rows = [table_ref[pl.ds(base + k, 1), :] for k in range(UNROLL)]
-        for k in range(UNROLL):
-            board_ref[pl.ds(targets[k], 1), :] = rows[k]
-        return carry
-
-    lax.fori_loop(0, COLUMNS // UNROLL, scatter, 0)
+    padding = jnp.zeros((LANES - TRACE, LANES), jnp.float32)
+
+    def build(face, block, slot):
+        square = jnp.concatenate([face_trace(state_ref, flat_ref, face, block), padding], axis=0)
+        table_ref[slot] = square.T
+
+    def scatter(block, carry):
+        for face in range(6):
+            build(face, block, face)
+            base = face * ELEMENTS + block * LANES
+            for start in range(0, LANES, UNROLL):
+                targets = [partner_ref[base + start + k] for k in range(UNROLL)]
+                rows = [table_ref[face, start + k : start + k + 1, :] for k in range(UNROLL)]
+                for k in range(UNROLL):
+                    board_ref[pl.ds(targets[k], 1), :] = rows[k]
+        return carry
+
+    lax.fori_loop(0, BLOCKS, scatter, 0)
 
     def speeds(step, best):
         density, mom_x, mom_y, mom_z, energy = [
@@ -340,10 +348,10 @@
 
 def lift(tiles, flux_ref, field_ref, v, block):
     first = sublane_index() < 4
-    start = pl.multiple_of(v * 16, 16)
 
     def piece(face, half):
-        return flux_ref[pl.ds((face * BLOCKS + block) * TRACE + half * 8 + start, 8), :]
+        start = aligned((face * BLOCKS + block) * TRACE + v * 16)
+        return flux_ref[pl.ds(start + half * 8, 8), :]
 
     tiles = list(tiles)
     for half in range(2):
@@ -354,7 +362,7 @@
         tiles[4 * half + 2] = tiles[4 * half + 2] + jnp.where(first, pltpu.roll(low, 4, 0), 0.0)
         tiles[4 * half + 1] = tiles[4 * half + 1] + jnp.where(first, 0.0, pltpu.roll(high, 4, 0))
         tiles[4 * half + 3] = tiles[4 * half + 3] + jnp.where(first, 0.0, high)
-    base = pl.multiple_of(v * 64, 64) + block * 320
+    base = aligned(v * 64 + block * 320)
     for tile in range(8):
         field_ref[pl.ds(base + tile * 8, 8), :] = tiles[tile]
     for half in range(2):
@@ -409,9 +417,9 @@
             place = face * BLOCKS + block
             normal, length = face_normals(normal_ref, place)
             start = pl.multiple_of(place * TRACE, TRACE)
-            side = pl.multiple_of(place * SIDE, 16)
-            for k, value in enumerate(normal + [length]):
-                side_ref[pl.ds(side + 16 + 8 * k, 8), :] = value
+            side = pl.multiple_of(place * SIDE, 8)
+            rows = [value[0:1] for value in normal + [length]]
+            side_ref[pl.ds(side + 16, 8), :] = jnp.concatenate(rows + rows, axis=0)
             partner = wide(partner_ref[pl.ds(place, 1), :])
             late = (partner >= COLUMNS) & ((partner < low) | (partner >= low + PLANE * SLOTS))
             late = jnp.where(late, 16, 0)
@@ -532,10 +540,10 @@
     owner_hbm,
     other_hbm,
     own_hbm,
-    side_hbm,
-    turn_hbm,
-    rate_hbm,
-    state_hbm,
+    side_ref,
+    turn_ref,
+    rate_ref,
+    state_ref,
     relay_ref,
     section_hbm,
     advanced_hbm,
@@ -547,10 +555,6 @@
     picked_ref,
     other_ref,
     own_ref,
-    side_ref,
-    turn_ref,
-    rate_ref,
-    state_ref,
     term_ref,
     field_ref,
     sems,
@@ -564,10 +568,6 @@
         (owner_hbm.at[pl.ds(pl.multiple_of(high_slot, 512), window)], high_ref),
         (other_hbm, other_ref),
         (own_hbm, own_ref),
-        (turn_hbm, turn_ref),
-        (side_hbm, side_ref),
-        (rate_hbm, rate_ref),
-        (state_hbm, state_ref),
     ]
     copies = [
         pltpu.make_async_copy(source, target, sems.at[k])
@@ -627,12 +627,23 @@
     for copy in copies[2:]:
         copy.wait()
 
-    def far_fluxes(face, carry):
-        for block in range(BLOCKS):
+    top = jnp.max(jnp.max(relay_ref[:, MESSAGE:, :], axis=0))
+    scale = CFL_NUMBER / top * SECTION_STEP
+
+    def results(block):
+        lanes = tile_lanes(block)
+        pairs = ((section_ref, section_hbm), (advanced_ref, advanced_hbm))
+        return [
+            pltpu.make_async_copy(source.at[:, :, lanes], target.at[:, :, lanes], sems.at[2 * block + k])
+            for k, (source, target) in enumerate(pairs)
+        ]
+
+    def element_block(block):
+        for face in range(6):
             place = face * BLOCKS + block
             square = picked_ref[pl.ds(pl.multiple_of(place * LANES, LANES), LANES), :].T
             start = pl.multiple_of(place * TRACE, TRACE)
-            side = pl.multiple_of(place * SIDE, 16)
+            side = pl.multiple_of(place * SIDE, 8)
             at = pl.multiple_of(place * 16, 16)
             turns = [turn_ref[pl.ds(at + half * 8, 8), :] for half in range(2)]
             late = turns[0] >= 16
@@ -640,8 +651,9 @@
                 jnp.where(late, square[8 * k : 8 * k + 8], other_ref[pl.ds(start + 8 * k, 8), :])
                 for k in range(10)
             ]
-            normal = [side_ref[pl.ds(side + 16 + 8 * k, 8), :] for k in range(3)]
-            length = side_ref[pl.ds(side + 40, 8), :]
+            rows = side_ref[pl.ds(side + 16, 8), :]
+            normal = [wide(rows[k : k + 1]) for k in range(3)]
+            length = wide(rows[3:4])
             for half in range(2):
                 upper = turns[half] % 16 >= 8
                 sublane = turns[half] % 8
@@ -661,22 +673,9 @@
                     term_ref[rows, :] = (0.5 * LIFT_FACTOR) * (
                         weight * (far[v] - own_ref[rows, :]) - far_terms[v]
                     )
-        return carry
-
-    lax.fori_loop(0, 6, far_fluxes, 0)
-    top = jnp.max(jnp.max(relay_ref[:, MESSAGE:, :], axis=0))
-    scale = CFL_NUMBER / top * SECTION_STEP
-
-    def results(v):
-        return [
-            pltpu.make_async_copy(section_ref.at[v], section_hbm.at[v], sems.at[2 * v]),
-            pltpu.make_async_copy(advanced_ref.at[v], advanced_hbm.at[v], sems.at[2 * v + 1]),
-        ]
-
-    def update(v, carry):
-        for block in range(BLOCKS):
-            lanes = tile_lanes(block)
-            base = pl.multiple_of(v * 64, 64) + block * 320
+        lanes = tile_lanes(block)
+        for v in range(5):
+            base = block * 320 + v * 64
             tiles = [rate_ref[pl.ds(base + tile * 8, 8), :] for tile in range(8)]
             lift(tiles, term_ref, field_ref, v, block)
             for tile in range(8):
@@ -684,13 +683,13 @@
                 section = field_ref[pl.ds(base + tile * 8, 8), :]
                 section_ref[v, nodes, lanes] = section
                 advanced_ref[v, nodes, lanes] = state_ref[v, nodes, lanes] + scale * section
-        for copy in results(v):
+        for copy in results(block):
             copy.start()
-        return carry
-
-    lax.fori_loop(0, 5, update, 0)
-    for v in range(5):
-        for copy in results(v):
+
+    for block in range(BLOCKS):
+        element_block(block)
+    for block in range(BLOCKS):
+        for copy in results(block):
             copy.wait()
 
 
@@ -741,7 +740,7 @@
             scratch(PLANE * MESSAGE, LANES),
             pltpu.SMEM((COLUMNS,), jnp.int32),
             scratch(5, 64, ELEMENTS),
-            scratch(COLUMNS, LANES),
+            scratch(6, LANES, LANES),
             scratch(COLUMNS + (DEVICES + CROSS) * SLOTS, LANES),
             scratch(1280, LANES),
             pltpu.SemaphoreType.DMA((5 + PLANE // BATCH,)),
@@ -755,10 +754,10 @@
     return pl.pallas_call(
         volume_kernel,
         out_shape=(
-            in_hbm_shape(1280, LANES),
+            shape(1280, LANES),
             in_hbm_shape(24 * TRACE, LANES),
-            in_hbm_shape(24 * SIDE, LANES),
-            pltpu.HBM((24 * 16, LANES), jnp.int32),
+            shape(24 * SIDE, LANES),
+            jax.ShapeDtypeStruct((24 * 16, LANES), jnp.int32),
         ),
         in_specs=[smem()] + [vmem()] * 6,
         out_specs=(vmem(),) * 4,
@@ -779,7 +778,7 @@
     return pl.pallas_call(
         relay_kernel,
         out_shape=(in_hbm_shape(PLANE, MESSAGE + 8, LANES), shape(8, LANES)),
-        in_specs=[smem()] + [vmem()] * 3 + [hbm()],
+        in_specs=[smem()] + [vmem()] * 3 + [anywhere()],
         out_specs=(vmem(), vmem()),
         compiler_params=params(),
         cost_estimate=pl.CostEstimate(flops=10**11, bytes_accessed=10**8, transcendentals=0),
@@ -821,11 +820,11 @@
 
 
 def finish(place, owner, other, own, side, turn, rate, state, relayed):
-    held = [in_hbm(value) for value in (owner, other, own, side, turn, rate, state)]
+    held = [in_hbm(value) for value in (owner, other, own)]
     return pl.pallas_call(
         finish_kernel,
         out_shape=(in_hbm_shape(5, 64, ELEMENTS),) * 2,
-        in_specs=[smem()] + [hbm()] * 7 + [vmem()],
+        in_specs=[smem()] + [hbm()] * 3 + [vmem()] * 5,
         out_specs=(hbm(), hbm()),
         scratch_shapes=[
             pltpu.SMEM((CROSS * SLOTS,), jnp.int32),
@@ -836,17 +835,13 @@
             scratch(COLUMNS + 8, LANES),
             scratch(24 * TRACE, LANES),
             scratch(24 * TRACE, LANES),
-            scratch(24 * SIDE, LANES),
-            pltpu.VMEM((24 * 16, LANES), jnp.int32),
-            scratch(1280, LANES),
-            scratch(5, 64, ELEMENTS),
             scratch(24 * TRACE, LANES),
             scratch(1280, LANES),
             pltpu.SemaphoreType.DMA((10,)),
         ],
         compiler_params=params(),
         name="finish",
-    )(place, *held, relayed)
+    )(place, *held, side, turn, rate, state, relayed)
 
 
 def in_hbm(value):
@@ -881,7 +876,7 @@
         flip_code.reshape(rows),
         partner.reshape(rows),
     )
-    relayed, three = relay(place, from_below, from_above, best, in_hbm(rate))
+    relayed, three = relay(place, from_below, from_above, best, rate)
     relayed = spread_top(three, far, in_hbm(relayed))
     relayed = lax.all_to_all(relayed, ("r", "x"), 0, 0, tiled=True)
     blank = jnp.full((COLUMNS + DEVICES * SLOTS,), COLUMNS, jnp.int32)

time: 56.9 us -> 55.4 us (0.974)
  Pallas kernels: 27 us -> 25.3 us
    pallas_call x1, Pallas kernels: 5.05 us -> 3.91 us  [finish(): pl.pallas_call(finish_kernel, out_shape=(in_hbm_shape(5, 64, ELEMENTS),)...]
  transfers between devices with their start and end apart: 5 -> 5, of which waited for: 2 -> 2; matrix products, arithmetic and copies ran while one was open for 0% -> 0% of each run, Pallas kernels for 26% -> 27%
where the time goes in v5:
time: 55.4 us; the launch traced here: 55 us
  Pallas kernels  25.3 us (46%)
  starting transfers between devices  19.2 us (35%)
  waiting for transfers between devices  9.74 us (18%)
  between operations  0.72 us (1%)
    all_to_all x1, starting transfers between devices, on_device(): got = lax.all_to_all(in_plane, ('r', 'x'), 0, 0, tiled=True)  9.15 us
    pallas_call x1, Pallas kernels, early(): pl.pallas_call(early_kernel, out_shape=(in_hbm_shape(24 * TRACE, LANES),...  7.84 us
    pallas_call x1, Pallas kernels, pack(): pl.pallas_call(pack_kernel, out_shape=(in_hbm_shape(PLANE * MESSAGE, LANE...  6.74 us
    all_to_all x1, waiting for transfers between devices, on_device(): relayed = lax.all_to_all(relayed, ('r', 'x'), 0, 0, tiled=True)  5.8 us
    ppermute x3, starting transfers between devices, along_y(): return lax.ppermute(value, 'y', [(i, (i + steps) % 4) for i in range(4)])  5.5 us
    all_to_all x1, starting transfers between devices, on_device(): relayed = lax.all_to_all(relayed, ('r', 'x'), 0, 0, tiled=True)  4.57 us
    all_to_all x1, waiting for transfers between devices, on_device(): got = lax.all_to_all(in_plane, ('r', 'x'), 0, 0, tiled=True)  3.93 us
    pallas_call x1, Pallas kernels, finish(): pl.pallas_call(finish_kernel, out_shape=(in_hbm_shape(5, 64, ELEMENTS),)...  3.91 us
  transfers between devices with their start and end apart: 5, of which 2 were waited for; matrix products, arithmetic and copies ran while one was open for 0% of the time, Pallas kernels for 27%

profile of v5, /device:TPU:1, one launch (start us, length us, event | category | flops | bytes accessed | tf_op | source)
XLA Modules:
  0.0 55.0 jit_solution(11532725227237384630)
XLA Ops:
  0.6 0.1 pad_add_fusion.place_ref
  0.7 0.0 copy-start.2
  0.7 0.0 copy-start.3
  0.7 0.0 copy-start.4
  0.7 0.0 copy-start.5
  0.7 6.7 %pack.1 = (f32[1280,128]{1,0:T(8,128)}, f32[968,128]{1,0:T(8,128)}, f32[968,128]{1,0:T(8,128)}, f32[8,128]{1,0:T(8,128)S(1)}) custom-call(s32[2]{0:T(128)S(1)} %pad_add_fusion.place_ref, s32[3072]{0:T(1024)} %partner_ref.1, f32[5,64,512]{2,1,0:T(8,128)} %bitcast.10), custom_call_target="tpu_custom_call" | custom-call | tf_op jit(solution)/shard_map/pack/pallas_call | solution.py:729
  7.5 2.2 %collective-permute-start = (f32[968,128]{1,0:T(8,128)}, f32[968,128]{1,0:T(8,128)}, u32[]{:S(2)}, u32[]{:S(2)}) collective-permute-start(f32[968,128]{1,0:T(8,128)} %get-tuple-element.23), channel_id=1, source_target_pairs={{0,32},{32,64},{64,96},{96,0},{1,33},{33,65},{65,97},{97,1},{2,34}... | collective-permute-start | bytes 1486856 | tf_op jit(solution)/shard_map/ppermute | solution.py:856
  9.7 1.5 %collective-permute-start.1 = (f32[968,128]{1,0:T(8,128)}, f32[968,128]{1,0:T(8,128)}, u32[]{:S(2)}, u32[]{:S(2)}) collective-permute-start(f32[968,128]{1,0:T(8,128)} %get-tuple-element.24), channel_id=1, source_target_pairs={{0,96},{32,0},{64,32},{96,64},{1,97},{33,1},{65,33},{97,65},{2,98}... | collective-permute-start | bytes 1486856 | tf_op jit(solution)/shard_map/ppermute | solution.py:856
  11.2 0.0 copy-start
  11.2 0.0 copy-start.1
  11.2 9.2 %all-to-all-start = ((f32[32,40,128]{2,1,0:T(8,128)}), f32[32,40,128]{2,1,0:T(8,128)S(1)}, u32[]{:S(2)}, u32[]{:S(2)}) async-start(f32[32,40,128]{2,1,0:T(8,128)} %bitcast.18), calls=%async_computation | async-start | bytes 1310720 | tf_op jit(solution)/shard_map/all_to_all | solution.py:869
  20.4 1.8 %collective-permute-start.2 = (f32[8,128]{1,0:T(8,128)S(1)}, f32[8,128]{1,0:T(8,128)S(1)}, u32[]{:S(2)}, u32[]{:S(2)}) collective-permute-start(f32[8,128]{1,0:T(8,128)S(1)} %get-tuple-element.25.best_ref), channel_id=1, source_target_pairs={{0,64},{32,96},{64,0},{96,32},{1,65},{33,97},{65,1},{97,33},{2,66}... | collective-permute-start | bytes 12296 | tf_op jit(solution)/shard_map/ppermute | solution.py:856
  22.1 0.0 copy-done.2
  22.1 0.0 copy-done.3
  22.1 0.0 copy-done.4
  22.1 0.0 copy-done.5
  22.2 0.0 copy-done
  22.2 0.0 copy-done.1
  22.2 3.8 %volume.1 = (f32[1280,128]{1,0:T(8,128)S(1)}, f32[1920,128]{1,0:T(8,128)}, f32[576,128]{1,0:T(8,128)S(1)}, s32[384,128]{1,0:T(8,128)S(1)}) custom-call(s32[2]{0:T(128)S(1)} %pad_add_fusion.place_ref, f32[5,64,512]{2,1,0:T(8,128)S(1)} %bitcast.11, f32[5,64,512]{2,1,0:T(8,128)S(1)} %bitcast.15, f32[3,3,512]{2,1,0:T(4,128)S(1)} %copy-done.4, ...), custom_call_target="tpu_custom_call" | custom-call | tf_op jit(solution)/shard_map/volume/pallas_call | solution.py:754
  26.0 0.0 collective-permute-done.up_ref
  26.0 0.0 collective-permute-done.1.down_ref
  26.0 2.3 %relay.1 = (f32[32,48,128]{2,1,0:T(8,128)}, f32[8,128]{1,0:T(8,128)S(1)}) custom-call(s32[2]{0:T(128)S(1)} %pad_add_fusion.place_ref, f32[968,128]{1,0:T(8,128)} %collective-permute-done.up_ref, f32[968,128]{1,0:T(8,128)} %collective-permute-done.1.down_ref, f32[8,128]{1,0:T(8,128)S(1)} %get-tuple-element.25.best_ref, ...), custom_call_target="tpu_custom_call" | custom-call | flops 99999997952 | bytes 100000000 | tf_op jit(solution)/shard_map/relay/pallas_call | solution.py:778
  28.3 0.0 collective-permute-done.2.far_ref
  28.3 0.7 %top.1 = f32[32,48,128]{2,1,0:T(8,128)} custom-call(f32[8,128]{1,0:T(8,128)S(1)} %get-tuple-element.26.three_ref, f32[8,128]{1,0:T(8,128)S(1)} %collective-permute-done.2.far_ref, f32[32,48,128]{2,1,0:T(8,128)} %get-tuple-element.27.relay_in), custom_call_target="tpu_custom_call", output_to_operand_aliasing={{}: (2, {})} | custom-call | tf_op jit(solution)/shard_map/top/pallas_call | solution.py:790
  29.0 3.9 %all-to-all-done = f32[32,40,128]{2,1,0:T(8,128)S(1)} async-done(((f32[32,40,128]{2,1,0:T(8,128)}), f32[32,40,128]{2,1,0:T(8,128)S(1)}, u32[]{:S(2)}, u32[]{:S(2)}) %all-to-all-start) | async-done | bytes 655392 | tf_op jit(solution)/shard_map/all_to_all | solution.py:869
  32.9 4.6 %all-to-all-start.1 = ((f32[32,48,128]{2,1,0:T(8,128)}), f32[32,48,128]{2,1,0:T(8,128)S(1)}, u32[]{:S(2)}, u32[]{:S(2)}) async-start(f32[32,48,128]{2,1,0:T(8,128)} %top.1), calls=%async_computation.1 | async-start | bytes 1572864 | tf_op jit(solution)/shard_map/all_to_all | solution.py:881
  37.5 7.8 %early.1 = (f32[1920,128]{1,0:T(8,128)}, s32[11264]{0:T(1024)}) custom-call(s32[2]{0:T(128)S(1)} %pad_add_fusion.place_ref, s32[3072]{0:T(1024)S(1)} %copy-done.2, s32[11264]{0:T(1024)S(1)} %broadcast_in_dim.3.blank_hbm, f32[5,64,512]{2,1,0:T(8,128)S(1)} %bitcast.12, f32[1280,128]{1,0:T(8,128)S(1)} %bitcast.14), custom_call_target="tpu_custom_call" | custom-call | tf_op jit(solution)/shard_map/early/pallas_call | solution.py:803
  45.3 5.8 %all-to-all-done.1.relay_ref = f32[32,48,128]{2,1,0:T(8,128)S(1)} async-done(((f32[32,48,128]{2,1,0:T(8,128)}), f32[32,48,128]{2,1,0:T(8,128)S(1)}, u32[]{:S(2)}, u32[]{:S(2)}) %all-to-all-start.1) | async-done | bytes 786464 | tf_op jit(solution)/shard_map/all_to_all | solution.py:881
  51.1 3.9 %finish.1 = (f32[5,64,512]{2,1,0:T(8,128)}, f32[5,64,512]{2,1,0:T(8,128)}) custom-call(s32[2]{0:T(128)S(1)} %pad_add_fusion.place_ref, s32[11264]{0:T(1024)} %get-tuple-element.17.owner_hbm, f32[1920,128]{1,0:T(8,128)} %get-tuple-element.18.other_hbm, f32[1920,128]{1,0:T(8,128)} %get-tuple-element.19.own_hbm, f32[576,128]{1,0:T(8,128)S(1)} %get-tuple-element.20.side_ref, ...), custom_call_target="tpu_custom_call" | custom-call | tf_op jit(solution)/shard_map/finish/pallas_call | solution.py:824
  (1 shorter events, 0.0 us)
Async XLA Ops:
  0.7 21.4 %copy-start.2 = (s32[3072]{0:T(1024)S(1)}, s32[3072]{0:T(1024)}, u32[]{:S(2)}) copy-start(s32[3072]{0:T(1024)} %partner_ref.1) | copy-start | bytes 36868
  0.7 21.4 %copy-start.3 = (f32[3,3072]{1,0:T(4,128)S(1)}, f32[3,3072]{1,0:T(4,128)}, u32[]{:S(2)}) copy-start(f32[3,3072]{1,0:T(4,128)} %normal_ref.1) | copy-start | bytes 110596
  0.7 21.4 %copy-start.4 = (f32[3,3,512]{2,1,0:T(4,128)S(1)}, f32[3,3,512]{2,1,0:T(4,128)}, u32[]{:S(2)}) copy-start(f32[3,3,512]{2,1,0:T(4,128)} %metric_ref.1) | copy-start | bytes 55300
  0.7 21.4 %copy-start.5 = (s32[3072]{0:T(1024)S(1)}, s32[3072]{0:T(1024)}, u32[]{:S(2)}) copy-start(s32[3072]{0:T(1024)} %param.13) | copy-start | bytes 36868
  7.5 18.5 %collective-permute-start = (f32[968,128]{1,0:T(8,128)}, f32[968,128]{1,0:T(8,128)}, u32[]{:S(2)}, u32[]{:S(2)}) collective-permute-start(f32[968,128]{1,0:T(8,128)} %get-tuple-element.23), channel_id=1, source_target_pairs={{0,32},{32,64},{64,96},{96,0},{1,33},{33,65},{65,97},{97,1},{2,34}... | collective-permute-start | bytes 1486856 | tf_op jit(solution)/shard_map/ppermute | solution.py:856
  9.7 16.3 %collective-permute-start.1 = (f32[968,128]{1,0:T(8,128)}, f32[968,128]{1,0:T(8,128)}, u32[]{:S(2)}, u32[]{:S(2)}) collective-permute-start(f32[968,128]{1,0:T(8,128)} %get-tuple-element.24), channel_id=1, source_target_pairs={{0,96},{32,0},{64,32},{96,64},{1,97},{33,1},{65,33},{97,65},{2,98}... | collective-permute-start | bytes 1486856 | tf_op jit(solution)/shard_map/ppermute | solution.py:856
  11.2 11.0 %copy-start = (f32[64,5,512]{2,0,1:T(8,128)S(1)}, f32[64,5,512]{2,0,1:T(8,128)}, u32[]{:S(2)}) copy-start(f32[64,5,512]{2,0,1:T(8,128)} %param.8) | copy-start | bytes 1966084
  11.2 11.0 %copy-start.1 = (f32[64,5,512]{2,0,1:T(8,128)S(1)}, f32[64,5,512]{2,0,1:T(8,128)}, u32[]{:S(2)}) copy-start(f32[64,5,512]{2,0,1:T(8,128)} %param.9) | copy-start | bytes 1966084
  11.2 21.7 %all-to-all-start = ((f32[32,40,128]{2,1,0:T(8,128)}), f32[32,40,128]{2,1,0:T(8,128)S(1)}, u32[]{:S(2)}, u32[]{:S(2)}) async-start(f32[32,40,128]{2,1,0:T(8,128)} %bitcast.18), calls=%async_computation | async-start | bytes 1310720 | tf_op jit(solution)/shard_map/all_to_all | solution.py:869
  20.4 7.9 %collective-permute-start.2 = (f32[8,128]{1,0:T(8,128)S(1)}, f32[8,128]{1,0:T(8,128)S(1)}, u32[]{:S(2)}, u32[]{:S(2)}) collective-permute-start(f32[8,128]{1,0:T(8,128)S(1)} %get-tuple-element.25.best_ref), channel_id=1, source_target_pairs={{0,64},{32,96},{64,0},{96,32},{1,65},{33,97},{65,1},{97,33},{2,66}... | collective-permute-start | bytes 12296 | tf_op jit(solution)/shard_map/ppermute | solution.py:856
  32.9 18.2 %all-to-all-start.1 = ((f32[32,48,128]{2,1,0:T(8,128)}), f32[32,48,128]{2,1,0:T(8,128)S(1)}, u32[]{:S(2)}, u32[]{:S(2)}) async-start(f32[32,48,128]{2,1,0:T(8,128)} %top.1), calls=%async_computation.1 | async-start | bytes 1572864 | tf_op jit(solution)/shard_map/all_to_all | solution.py:881

commit v6 on v5

--- a/solution.py
+++ b/solution.py
@@ -1,3 +1,5 @@
+import functools
+
 import jax
 import jax.numpy as jnp
 import numpy as np
@@ -22,6 +24,7 @@
 TRACE = 80
 GROUP = COLUMNS // 3
 MESSAGE = TRACE * SLOTS // LANES
+LONG = MESSAGE + 1
 UNROLL = 32
 SIDE = 24
 BATCH = 4
@@ -29,7 +32,7 @@
 PLANE = 32
 NEAR = PLANE - REACH
 CROSS = REACH
-MARGIN = CROSS
+MARGIN = PLANE
 VMEM_LIMIT = 24 * 1024 * 1024
 
 
@@ -199,7 +202,7 @@
         square = jnp.concatenate([face_trace(state_ref, flat_ref, face, block), padding], axis=0)
         table_ref[slot] = square.T
 
-    def scatter(block, carry):
+    def scatter(block):
         for face in range(6):
             build(face, block, face)
             base = face * ELEMENTS + block * LANES
@@ -208,9 +211,9 @@
                 rows = [table_ref[face, start + k : start + k + 1, :] for k in range(UNROLL)]
                 for k in range(UNROLL):
                     board_ref[pl.ds(targets[k], 1), :] = rows[k]
-        return carry
-
-    lax.fori_loop(0, BLOCKS, scatter, 0)
+
+    for block in range(BLOCKS):
+        scatter(block)
 
     def speeds(step, best):
         density, mom_x, mom_y, mom_z, energy = [
@@ -252,41 +255,40 @@
             pltpu.make_async_copy(plane_ref.at[part, :], plane_hbm.at[part, :], sems.at[5 + step])
         )
         sent[-1].start()
-    lax.fori_loop(0, (jnp.maximum(spot - NEAR + 1, 0) + BATCH - 1) // BATCH, send_up, 0)
-    lax.fori_loop(spot // BATCH, CROSS // BATCH, send_down, 0)
+    upward = (jnp.maximum(spot - NEAR + 1, 0) + BATCH - 1) // BATCH
+    lax.fori_loop(0, jnp.where(plane < 3, upward, 0), send_up, 0)
+    lax.fori_loop(jnp.where(plane > 0, spot // BATCH, CROSS // BATCH), CROSS // BATCH, send_down, 0)
     for copy in sent:
         copy.wait()
 
 
 def relay_kernel(place_ref, up_ref, down_ref, best_ref, rate_hbm, relay_ref, three_ref):
+    spot = place_ref[1]
+    for block in range(PLANE):
+        for k in range(5):
+            if block < CROSS:
+                value = up_ref[block * MESSAGE + 8 * k : block * MESSAGE + 8 * k + 8, :]
+            if block >= NEAR:
+                at = (block - NEAR) * MESSAGE + 8 * k
+                other = down_ref[at : at + 8, :]
+                value = other if block >= CROSS else jnp.where(block <= spot - NEAR, value, other)
+            relay_ref[block * LONG + 8 * k : block * LONG + 8 * k + 8, :] = value
     three_ref[...] = jnp.maximum(
         best_ref[...], jnp.maximum(up_ref[CROSS * MESSAGE :, :], down_ref[CROSS * MESSAGE :, :])
     )
-    spot = place_ref[1]
-
-    def from_up(block, carry):
-        for k in range(5):
-            at = pl.multiple_of(block * MESSAGE + 8 * k, 8)
-            relay_ref[block, 8 * k : 8 * k + 8, :] = up_ref[pl.ds(at, 8), :]
-        return carry
-
-    def from_down(block, carry):
-        for k in range(5):
-            at = pl.multiple_of(block * MESSAGE + 8 * k, 8)
-            relay_ref[block + NEAR, 8 * k : 8 * k + 8, :] = down_ref[pl.ds(at, 8), :]
-        return carry
-
-    lax.fori_loop(0, jnp.maximum(spot - NEAR + 1, 0), from_up, 0)
-    lax.fori_loop(spot, CROSS, from_down, 0)
-
-
-def top_kernel(three_ref, far_ref, relay_in, relay_hbm, top_ref, sem):
-    top = jnp.maximum(three_ref[...], far_ref[...])
-    for block in range(PLANE):
-        top_ref[block] = top
-    copy = pltpu.make_async_copy(top_ref, relay_hbm.at[:, pl.ds(MESSAGE, 8), :], sem)
-    copy.start()
-    copy.wait()
+
+
+def top_kernel(three_ref, far_ref, relay_in, relay_hbm, top_ref, sems):
+    top = jnp.max(jnp.maximum(three_ref[...], far_ref[...]), axis=0, keepdims=True)
+    top_ref[0] = top
+    copies = [
+        pltpu.make_async_copy(top_ref, relay_hbm.at[pl.ds(block * LONG + MESSAGE, 1)], sems.at[block])
+        for block in range(PLANE)
+    ]
+    for copy in copies:
+        copy.start()
+    for copy in copies:
+        copy.wait()
 
 
 def early_kernel(
@@ -576,26 +578,23 @@
     for copy in copies:
         copy.start()
 
-    def receive(peer, block):
-        parts = [relay_ref[block + k // 5, 8 * (k % 5) : 8 * (k % 5) + 8, :] for k in range(5 * BATCH)]
+    def receive(blocks):
+        parts = [relay_ref[b * LONG + 8 * k : b * LONG + 8 * k + 8, :] for b in blocks for k in range(5)]
         rows = []
         for k in range(BATCH):
             rows += expand(parts[5 * k : 5 * k + 5])
-        base = pl.multiple_of((peer + block + MARGIN) * SLOTS, SLOTS)
-        for k in range(8 * BATCH):
-            board_ref[pl.ds(base + 8 * k, 8), :] = rows[k]
-
-    def receive_low(step, carry):
-        receive((plane - 1) * PLANE, NEAR + step * BATCH)
-        return carry
-
-    def receive_high(step, carry):
-        receive((plane + 1) * PLANE, step * BATCH)
-        return carry
-
-    lax.fori_loop(spot // BATCH, CROSS // BATCH, receive_low, 0)
-    high = (jnp.maximum(spot - NEAR + 1, 0) + BATCH - 1) // BATCH
-    lax.fori_loop(0, high, receive_high, 0)
+        for k, block in enumerate(blocks):
+            side = jnp.where(block >= spot + NEAR, plane - 1, plane + 1)
+            base = pl.multiple_of((side * PLANE + block + MARGIN) * SLOTS, SLOTS)
+            for j in range(8):
+                board_ref[pl.ds(base + 8 * j, 8), :] = rows[8 * k + j]
+
+    for first in range(0, PLANE, BATCH):
+        last = first + BATCH - 1
+
+        @pl.when((first <= spot - NEAR) | (last >= spot + NEAR))
+        def _(first=first):
+            receive(range(first, first + BATCH))
 
     def place_rows(columns_ref, base, step):
         at = step * UNROLL
@@ -627,7 +626,8 @@
     for copy in copies[2:]:
         copy.wait()
 
-    top = jnp.max(jnp.max(relay_ref[:, MESSAGE:, :], axis=0))
+    tops = [relay_ref[b * LONG + MESSAGE : (b + 1) * LONG, :] for b in range(PLANE)]
+    top = jnp.max(functools.reduce(jnp.maximum, tops))
     scale = CFL_NUMBER / top * SECTION_STEP
 
     def results(block):
@@ -777,7 +777,7 @@
 def relay(place, up, down, best, rate):
     return pl.pallas_call(
         relay_kernel,
-        out_shape=(in_hbm_shape(PLANE, MESSAGE + 8, LANES), shape(8, LANES)),
+        out_shape=(in_hbm_shape(PLANE * LONG, LANES), shape(8, LANES)),
         in_specs=[smem()] + [vmem()] * 3 + [anywhere()],
         out_specs=(vmem(), vmem()),
         compiler_params=params(),
@@ -789,10 +789,10 @@
 def spread_top(three, far, relayed):
     return pl.pallas_call(
         top_kernel,
-        out_shape=in_hbm_shape(PLANE, MESSAGE + 8, LANES),
+        out_shape=in_hbm_shape(PLANE * LONG, 1, LANES),
         in_specs=[vmem(), vmem(), hbm()],
         out_specs=hbm(),
-        scratch_shapes=[scratch(PLANE, 8, LANES), pltpu.SemaphoreType.DMA],
+        scratch_shapes=[scratch(1, 1, LANES), pltpu.SemaphoreType.DMA((PLANE,))],
         input_output_aliases={2: 0},
         compiler_params=params(),
         name="top",
@@ -877,8 +877,8 @@
         partner.reshape(rows),
     )
     relayed, three = relay(place, from_below, from_above, best, rate)
-    relayed = spread_top(three, far, in_hbm(relayed))
-    relayed = lax.all_to_all(relayed, ("r", "x"), 0, 0, tiled=True)
+    relayed = spread_top(three, far, in_hbm(relayed.reshape(PLANE * LONG, 1, LANES))).reshape(PLANE, LONG, 1, LANES)
+    relayed = lax.all_to_all(relayed, ("r", "x"), 0, 0, tiled=True).reshape(PLANE * LONG, LANES)
     blank = jnp.full((COLUMNS + DEVICES * SLOTS,), COLUMNS, jnp.int32)
     other, owner = early(place, partner, blank, state, got)
     section, advanced = finish(place, owner, other, own, side, turn, rate, state, relayed)

time: 55.4 us -> 53.5 us (0.966)
  waiting for transfers between devices: 9.74 us -> 8.57 us
  Pallas kernels: 25.3 us -> 24.5 us
    all_to_all x1, waiting for transfers between devices: 5.8 us -> 4.79 us  [on_device(): lax.all_to_all(relayed, ('r', 'x'), 0, 0, tiled=True)]
    pallas_call x1, Pallas kernels: 6.74 us -> 5.79 us  [pack(): pl.pallas_call(pack_kernel, out_shape=(in_hbm_shape(PLANE * MESSAGE, LANE...]
  transfers between devices with their start and end apart: 5 -> 5, of which waited for: 2 -> 2; matrix products, arithmetic and copies ran while one was open for 0% -> 0% of each run, Pallas kernels for 27% -> 28%
where the time goes in v6:
time: 53.5 us; the launch traced here: 53.1 us
  Pallas kernels  24.5 us (46%)
  starting transfers between devices  19.2 us (36%)
  waiting for transfers between devices  8.57 us (16%)
  between operations  0.72 us (1%)
    all_to_all x1, starting transfers between devices, on_device(): got = lax.all_to_all(in_plane, ('r', 'x'), 0, 0, tiled=True)  9.15 us
    pallas_call x1, Pallas kernels, early(): pl.pallas_call(early_kernel, out_shape=(in_hbm_shape(24 * TRACE, LANES),...  7.86 us
    pallas_call x1, Pallas kernels, pack(): pl.pallas_call(pack_kernel, out_shape=(in_hbm_shape(PLANE * MESSAGE, LANE...  5.79 us
    ppermute x3, starting transfers between devices, along_y(): return lax.ppermute(value, 'y', [(i, (i + steps) % 4) for i in range(4)])  5.5 us
    all_to_all x1, waiting for transfers between devices, on_device(): lax.all_to_all(relayed, ('r', 'x'), 0, 0, tiled=True)  4.79 us
    all_to_all x1, starting transfers between devices, on_device(): lax.all_to_all(relayed, ('r', 'x'), 0, 0, tiled=True)  4.57 us
    pallas_call x1, Pallas kernels, finish(): pl.pallas_call(finish_kernel, out_shape=(in_hbm_shape(5, 64, ELEMENTS),)...  3.92 us
    pallas_call x1, Pallas kernels, volume(): pl.pallas_call(volume_kernel, out_shape=(shape(1280, LANES), in_hbm_shape...  3.82 us
  transfers between devices with their start and end apart: 5, of which 2 were waited for; matrix products, arithmetic and copies ran while one was open for 0% of the time, Pallas kernels for 28%

profile of v6, /device:TPU:1, one launch (start us, length us, event | category | flops | bytes accessed | tf_op | source)
XLA Modules:
  0.0 53.1 jit_solution(8565078752396907613)
XLA Ops:
  0.6 0.1 pad_add_fusion.place_ref
  0.7 0.0 copy-start.2
  0.7 0.0 copy-start.3
  0.7 0.0 copy-start.4
  0.7 0.0 copy-start.5
  0.7 5.8 %pack.1 = (f32[1280,128]{1,0:T(8,128)}, f32[968,128]{1,0:T(8,128)}, f32[968,128]{1,0:T(8,128)}, f32[8,128]{1,0:T(8,128)S(1)}) custom-call(s32[2]{0:T(128)S(1)} %pad_add_fusion.place_ref, s32[3072]{0:T(1024)} %partner_ref.1, f32[5,64,512]{2,1,0:T(8,128)} %bitcast.13), custom_call_target="tpu_custom_call" | custom-call | tf_op jit(solution)/shard_map/pack/pallas_call | solution.py:729
  6.5 2.2 %collective-permute-start = (f32[968,128]{1,0:T(8,128)}, f32[968,128]{1,0:T(8,128)}, u32[]{:S(2)}, u32[]{:S(2)}) collective-permute-start(f32[968,128]{1,0:T(8,128)} %get-tuple-element.23), channel_id=1, source_target_pairs={{0,32},{32,64},{64,96},{96,0},{1,33},{33,65},{65,97},{97,1},{2,34}... | collective-permute-start | bytes 1486856 | tf_op jit(solution)/shard_map/ppermute | solution.py:856
  8.7 1.5 %collective-permute-start.1 = (f32[968,128]{1,0:T(8,128)}, f32[968,128]{1,0:T(8,128)}, u32[]{:S(2)}, u32[]{:S(2)}) collective-permute-start(f32[968,128]{1,0:T(8,128)} %get-tuple-element.24), channel_id=1, source_target_pairs={{0,96},{32,0},{64,32},{96,64},{1,97},{33,1},{65,33},{97,65},{2,98}... | collective-permute-start | bytes 1486856 | tf_op jit(solution)/shard_map/ppermute | solution.py:856
  10.2 0.0 copy-start
  10.2 0.0 copy-start.1
  10.2 9.2 %all-to-all-start = ((f32[32,40,128]{2,1,0:T(8,128)}), f32[32,40,128]{2,1,0:T(8,128)S(1)}, u32[]{:S(2)}, u32[]{:S(2)}) async-start(f32[32,40,128]{2,1,0:T(8,128)} %bitcast.24), calls=%async_computation | async-start | bytes 1310720 | tf_op jit(solution)/shard_map/all_to_all | solution.py:869
  19.4 1.8 %collective-permute-start.2 = (f32[8,128]{1,0:T(8,128)S(1)}, f32[8,128]{1,0:T(8,128)S(1)}, u32[]{:S(2)}, u32[]{:S(2)}) collective-permute-start(f32[8,128]{1,0:T(8,128)S(1)} %get-tuple-element.25.best_ref), channel_id=1, source_target_pairs={{0,64},{32,96},{64,0},{96,32},{1,65},{33,97},{65,1},{97,33},{2,66}... | collective-permute-start | bytes 12296 | tf_op jit(solution)/shard_map/ppermute | solution.py:856
  21.2 0.0 copy-done.2
  21.2 0.0 copy-done.3
  21.2 0.0 copy-done.4
  21.2 0.0 copy-done.5
  21.2 0.0 copy-done
  21.2 0.0 copy-done.1
  21.2 3.8 %volume.1 = (f32[1280,128]{1,0:T(8,128)S(1)}, f32[1920,128]{1,0:T(8,128)}, f32[576,128]{1,0:T(8,128)S(1)}, s32[384,128]{1,0:T(8,128)S(1)}) custom-call(s32[2]{0:T(128)S(1)} %pad_add_fusion.place_ref, f32[5,64,512]{2,1,0:T(8,128)S(1)} %bitcast.14, f32[5,64,512]{2,1,0:T(8,128)S(1)} %bitcast.19, f32[3,3,512]{2,1,0:T(4,128)S(1)} %copy-done.4, ...), custom_call_target="tpu_custom_call" | custom-call | tf_op jit(solution)/shard_map/volume/pallas_call | solution.py:754
  25.0 0.0 collective-permute-done.up_ref
  25.0 0.0 collective-permute-done.1.down_ref
  25.0 2.1 %relay.1 = (f32[1312,128]{1,0:T(8,128)}, f32[8,128]{1,0:T(8,128)S(1)}) custom-call(s32[2]{0:T(128)S(1)} %pad_add_fusion.place_ref, f32[968,128]{1,0:T(8,128)} %collective-permute-done.up_ref, f32[968,128]{1,0:T(8,128)} %collective-permute-done.1.down_ref, f32[8,128]{1,0:T(8,128)S(1)} %get-tuple-element.25.best_ref, ...), custom_call_target="tpu_custom_call" | custom-call | flops 99999997952 | bytes 100000000 | tf_op jit(solution)/shard_map/relay/pallas_call | solution.py:778
  27.2 0.0 collective-permute-done.2.far_ref
  27.2 1.0 %top.1 = f32[1312,1,128]{2,1,0:T(1,128)} custom-call(f32[8,128]{1,0:T(8,128)S(1)} %get-tuple-element.26.three_ref, f32[8,128]{1,0:T(8,128)S(1)} %collective-permute-done.2.far_ref, f32[1312,1,128]{2,1,0:T(1,128)} %bitcast.22), custom_call_target="tpu_custom_call", output_to_operand_aliasing={{}: (2, {})} | custom-call | tf_op jit(solution)/shard_map/top/pallas_call | solution.py:790
  28.2 3.8 %all-to-all-done = f32[32,40,128]{2,1,0:T(8,128)S(1)} async-done(((f32[32,40,128]{2,1,0:T(8,128)}), f32[32,40,128]{2,1,0:T(8,128)S(1)}, u32[]{:S(2)}, u32[]{:S(2)}) %all-to-all-start) | async-done | bytes 655392 | tf_op jit(solution)/shard_map/all_to_all | solution.py:869
  31.9 4.6 %all-to-all-start.1 = ((f32[32,41,1,128]{3,2,1,0:T(1,128)}), f32[32,41,1,128]{3,2,1,0:T(1,128)S(1)}, u32[]{:S(2)}, u32[]{:S(2)}) async-start(f32[32,41,1,128]{3,2,1,0:T(1,128)} %bitcast.23), calls=%async_computation.1 | async-start | bytes 1343488 | tf_op jit(solution)/shard_map/all_to_all | solution.py:881
  36.5 7.9 %early.1 = (f32[1920,128]{1,0:T(8,128)}, s32[11264]{0:T(1024)}) custom-call(s32[2]{0:T(128)S(1)} %pad_add_fusion.place_ref, s32[3072]{0:T(1024)S(1)} %copy-done.2, s32[11264]{0:T(1024)S(1)} %broadcast_in_dim.3.blank_hbm, f32[5,64,512]{2,1,0:T(8,128)S(1)} %bitcast.15, f32[1280,128]{1,0:T(8,128)S(1)} %bitcast.18), custom_call_target="tpu_custom_call" | custom-call | tf_op jit(solution)/shard_map/early/pallas_call | solution.py:803
  44.4 4.8 %all-to-all-done.1 = f32[32,41,1,128]{3,2,1,0:T(1,128)S(1)} async-done(((f32[32,41,1,128]{3,2,1,0:T(1,128)}), f32[32,41,1,128]{3,2,1,0:T(1,128)S(1)}, u32[]{:S(2)}, u32[]{:S(2)}) %all-to-all-start.1) | async-done | bytes 671776 | tf_op jit(solution)/shard_map/all_to_all | solution.py:881
  49.2 3.9 %finish.1 = (f32[5,64,512]{2,1,0:T(8,128)}, f32[5,64,512]{2,1,0:T(8,128)}) custom-call(s32[2]{0:T(128)S(1)} %pad_add_fusion.place_ref, s32[11264]{0:T(1024)} %get-tuple-element.17.owner_hbm, f32[1920,128]{1,0:T(8,128)} %get-tuple-element.18.other_hbm, f32[1920,128]{1,0:T(8,128)} %get-tuple-element.19.own_hbm, f32[576,128]{1,0:T(8,128)S(1)} %get-tuple-element.20.side_ref, ...), custom_call_target="tpu_custom_call" | custom-call | tf_op jit(solution)/shard_map/finish/pallas_call | solution.py:824
  (1 shorter events, 0.0 us)
Async XLA Ops:
  0.7 20.5 %copy-start.2 = (s32[3072]{0:T(1024)S(1)}, s32[3072]{0:T(1024)}, u32[]{:S(2)}) copy-start(s32[3072]{0:T(1024)} %partner_ref.1) | copy-start | bytes 36868
  0.7 20.5 %copy-start.3 = (f32[3,3072]{1,0:T(4,128)S(1)}, f32[3,3072]{1,0:T(4,128)}, u32[]{:S(2)}) copy-start(f32[3,3072]{1,0:T(4,128)} %normal_ref.1) | copy-start | bytes 110596
  0.7 20.5 %copy-start.4 = (f32[3,3,512]{2,1,0:T(4,128)S(1)}, f32[3,3,512]{2,1,0:T(4,128)}, u32[]{:S(2)}) copy-start(f32[3,3,512]{2,1,0:T(4,128)} %metric_ref.1) | copy-start | bytes 55300
  0.7 20.5 %copy-start.5 = (s32[3072]{0:T(1024)S(1)}, s32[3072]{0:T(1024)}, u32[]{:S(2)}) copy-start(s32[3072]{0:T(1024)} %param.13) | copy-start | bytes 36868
  6.5 18.5 %collective-permute-start = (f32[968,128]{1,0:T(8,128)}, f32[968,128]{1,0:T(8,128)}, u32[]{:S(2)}, u32[]{:S(2)}) collective-permute-start(f32[968,128]{1,0:T(8,128)} %get-tuple-element.23), channel_id=1, source_target_pairs={{0,32},{32,64},{64,96},{96,0},{1,33},{33,65},{65,97},{97,1},{2,34}... | collective-permute-start | bytes 1486856 | tf_op jit(solution)/shard_map/ppermute | solution.py:856
  8.7 16.3 %collective-permute-start.1 = (f32[968,128]{1,0:T(8,128)}, f32[968,128]{1,0:T(8,128)}, u32[]{:S(2)}, u32[]{:S(2)}) collective-permute-start(f32[968,128]{1,0:T(8,128)} %get-tuple-element.24), channel_id=1, source_target_pairs={{0,96},{32,0},{64,32},{96,64},{1,97},{33,1},{65,33},{97,65},{2,98}... | collective-permute-start | bytes 1486856 | tf_op jit(solution)/shard_map/ppermute | solution.py:856
  10.2 11.0 %copy-start = (f32[64,5,512]{2,0,1:T(8,128)S(1)}, f32[64,5,512]{2,0,1:T(8,128)}, u32[]{:S(2)}) copy-start(f32[64,5,512]{2,0,1:T(8,128)} %param.8) | copy-start | bytes 1966084
  10.2 11.0 %copy-start.1 = (f32[64,5,512]{2,0,1:T(8,128)S(1)}, f32[64,5,512]{2,0,1:T(8,128)}, u32[]{:S(2)}) copy-start(f32[64,5,512]{2,0,1:T(8,128)} %param.9) | copy-start | bytes 1966084
  10.2 21.7 %all-to-all-start = ((f32[32,40,128]{2,1,0:T(8,128)}), f32[32,40,128]{2,1,0:T(8,128)S(1)}, u32[]{:S(2)}, u32[]{:S(2)}) async-start(f32[32,40,128]{2,1,0:T(8,128)} %bitcast.24), calls=%async_computation | async-start | bytes 1310720 | tf_op jit(solution)/shard_map/all_to_all | solution.py:869
  19.4 7.8 %collective-permute-start.2 = (f32[8,128]{1,0:T(8,128)S(1)}, f32[8,128]{1,0:T(8,128)S(1)}, u32[]{:S(2)}, u32[]{:S(2)}) collective-permute-start(f32[8,128]{1,0:T(8,128)S(1)} %get-tuple-element.25.best_ref), channel_id=1, source_target_pairs={{0,64},{32,96},{64,0},{96,32},{1,65},{33,97},{65,1},{97,33},{2,66}... | collective-permute-start | bytes 12296 | tf_op jit(solution)/shard_map/ppermute | solution.py:856
  31.9 17.2 %all-to-all-start.1 = ((f32[32,41,1,128]{3,2,1,0:T(1,128)}), f32[32,41,1,128]{3,2,1,0:T(1,128)S(1)}, u32[]{:S(2)}, u32[]{:S(2)}) async-start(f32[32,41,1,128]{3,2,1,0:T(1,128)} %bitcast.23), calls=%async_computation.1 | async-start | bytes 1343488 | tf_op jit(solution)/shard_map/all_to_all | solution.py:881

commit v7 on v6

--- a/solution.py
+++ b/solution.py
@@ -396,9 +396,9 @@
     code_ref,
     partner_ref,
     field_ref,
-    own_ref,
     side_ref,
     turn_ref,
+    own_ref,
     rows_ref,
     tensor_ref,
     flux_ref,
@@ -540,11 +540,10 @@
 def finish_kernel(
     place_ref,
     owner_hbm,
-    other_hbm,
-    own_hbm,
+    rate_hbm,
+    other_ref,
     side_ref,
     turn_ref,
-    rate_ref,
     state_ref,
     relay_ref,
     section_hbm,
@@ -555,8 +554,8 @@
     advanced_ref,
     board_ref,
     picked_ref,
-    other_ref,
-    own_ref,
+    rate_ref,
+    flat_ref,
     term_ref,
     field_ref,
     sems,
@@ -568,8 +567,7 @@
     sources = [
         (owner_hbm.at[pl.ds(pl.multiple_of(low_slot, 512), window)], low_ref),
         (owner_hbm.at[pl.ds(pl.multiple_of(high_slot, 512), window)], high_ref),
-        (other_hbm, other_ref),
-        (own_hbm, own_ref),
+        (rate_hbm, rate_ref),
     ]
     copies = [
         pltpu.make_async_copy(source, target, sems.at[k])
@@ -577,6 +575,7 @@
     ]
     for copy in copies:
         copy.start()
+    spread_flat(state_ref, flat_ref)
 
     def receive(blocks):
         parts = [relay_ref[b * LONG + 8 * k : b * LONG + 8 * k + 8, :] for b in blocks for k in range(5)]
@@ -623,9 +622,6 @@
     def _():
         lax.fori_loop(0, jnp.maximum(spot - NEAR + 1, 0) * chunk, place_high, 0)
 
-    for copy in copies[2:]:
-        copy.wait()
-
     tops = [relay_ref[b * LONG + MESSAGE : (b + 1) * LONG, :] for b in range(PLANE)]
     top = jnp.max(functools.reduce(jnp.maximum, tops))
     scale = CFL_NUMBER / top * SECTION_STEP
@@ -634,7 +630,7 @@
         lanes = tile_lanes(block)
         pairs = ((section_ref, section_hbm), (advanced_ref, advanced_hbm))
         return [
-            pltpu.make_async_copy(source.at[:, :, lanes], target.at[:, :, lanes], sems.at[2 * block + k])
+            pltpu.make_async_copy(source.at[:, :, lanes], target.at[:, :, lanes], sems.at[3 + 2 * block + k])
             for k, (source, target) in enumerate(pairs)
         ]
 
@@ -651,6 +647,7 @@
                 jnp.where(late, square[8 * k : 8 * k + 8], other_ref[pl.ds(start + 8 * k, 8), :])
                 for k in range(10)
             ]
+            own = [face_rows(state_ref, flat_ref, v, face, block) for v in range(5)]
             rows = side_ref[pl.ds(side + 16, 8), :]
             normal = [wide(rows[k : k + 1]) for k in range(3)]
             length = wide(rows[3:4])
@@ -671,8 +668,10 @@
                     rows = pl.ds(start + v * 16 + half * 8, 8)
                     weight = bound if v == 0 else viscous
                     term_ref[rows, :] = (0.5 * LIFT_FACTOR) * (
-                        weight * (far[v] - own_ref[rows, :]) - far_terms[v]
+                        weight * (far[v] - own[v][8 * half : 8 * half + 8]) - far_terms[v]
                     )
+        if block == 0:
+            copies[2].wait()
         lanes = tile_lanes(block)
         for v in range(5):
             base = block * 320 + v * 64
@@ -754,14 +753,14 @@
     return pl.pallas_call(
         volume_kernel,
         out_shape=(
-            shape(1280, LANES),
-            in_hbm_shape(24 * TRACE, LANES),
+            in_hbm_shape(1280, LANES),
             shape(24 * SIDE, LANES),
             jax.ShapeDtypeStruct((24 * 16, LANES), jnp.int32),
         ),
         in_specs=[smem()] + [vmem()] * 6,
-        out_specs=(vmem(),) * 4,
+        out_specs=(vmem(),) * 3,
         scratch_shapes=[
+            scratch(24 * TRACE, LANES),
             scratch(1280, LANES),
             scratch(72, LANES),
             scratch(3, 1280, LANES),
@@ -778,7 +777,7 @@
     return pl.pallas_call(
         relay_kernel,
         out_shape=(in_hbm_shape(PLANE * LONG, LANES), shape(8, LANES)),
-        in_specs=[smem()] + [vmem()] * 3 + [anywhere()],
+        in_specs=[smem()] + [vmem()] * 3 + [hbm()],
         out_specs=(vmem(), vmem()),
         compiler_params=params(),
         cost_estimate=pl.CostEstimate(flops=10**11, bytes_accessed=10**8, transcendentals=0),
@@ -803,7 +802,7 @@
     return pl.pallas_call(
         early_kernel,
         out_shape=(
-            in_hbm_shape(24 * TRACE, LANES),
+            shape(24 * TRACE, LANES),
             pltpu.HBM((COLUMNS + DEVICES * SLOTS,), jnp.int32),
         ),
         in_specs=[smem(), smem(), anywhere(), vmem(), vmem()],
@@ -819,12 +818,12 @@
     )(place, partner, blank, state, plane)
 
 
-def finish(place, owner, other, own, side, turn, rate, state, relayed):
-    held = [in_hbm(value) for value in (owner, other, own)]
+def finish(place, owner, other, side, turn, rate, state, relayed):
+    held = [in_hbm(value) for value in (owner, rate)]
     return pl.pallas_call(
         finish_kernel,
         out_shape=(in_hbm_shape(5, 64, ELEMENTS),) * 2,
-        in_specs=[smem()] + [hbm()] * 3 + [vmem()] * 5,
+        in_specs=[smem(), hbm(), hbm()] + [vmem()] * 5,
         out_specs=(hbm(), hbm()),
         scratch_shapes=[
             pltpu.SMEM((CROSS * SLOTS,), jnp.int32),
@@ -833,15 +832,15 @@
             scratch(5, 64, ELEMENTS),
             scratch((DEVICES + 2 * MARGIN) * SLOTS, LANES),
             scratch(COLUMNS + 8, LANES),
-            scratch(24 * TRACE, LANES),
-            scratch(24 * TRACE, LANES),
+            scratch(1280, LANES),
+            scratch(1280, LANES),
             scratch(24 * TRACE, LANES),
             scratch(1280, LANES),
-            pltpu.SemaphoreType.DMA((10,)),
+            pltpu.SemaphoreType.DMA((11,)),
         ],
         compiler_params=params(),
         name="finish",
-    )(place, *held, side, turn, rate, state, relayed)
+    )(place, *held, other, side, turn, state, relayed)
 
 
 def in_hbm(value):
@@ -867,7 +866,7 @@
     from_above = along_y(down, -1)
     far = along_y(best, 2)
     got = lax.all_to_all(in_plane, ("r", "x"), 0, 0, tiled=True)
-    rate, own, side, turn = volume(
+    rate, side, turn = volume(
         place,
         state,
         register.transpose(1, 0, 2),
@@ -876,12 +875,12 @@
         flip_code.reshape(rows),
         partner.reshape(rows),
     )
-    relayed, three = relay(place, from_below, from_above, best, rate)
+    relayed, three = relay(place, from_below, from_above, best, in_hbm(rate))
     relayed = spread_top(three, far, in_hbm(relayed.reshape(PLANE * LONG, 1, LANES))).reshape(PLANE, LONG, 1, LANES)
     relayed = lax.all_to_all(relayed, ("r", "x"), 0, 0, tiled=True).reshape(PLANE * LONG, LANES)
     blank = jnp.full((COLUMNS + DEVICES * SLOTS,), COLUMNS, jnp.int32)
     other, owner = early(place, partner, blank, state, got)
-    section, advanced = finish(place, owner, other, own, side, turn, rate, state, relayed)
+    section, advanced = finish(place, owner, other, side, turn, rate, state, relayed)
     return section.transpose(1, 0, 2), advanced.transpose(1, 0, 2)
 
 

time: 53.5 us -> 52.9 us (0.989)
  Pallas kernels: 24.5 us -> 23.5 us
  transfers between devices with their start and end apart: 5 -> 5, of which waited for: 2 -> 2; matrix products, arithmetic and copies ran while one was open for 0% -> 0% of each run, Pallas kernels for 28% -> 27%
where the time goes in v7:
time: 52.9 us; the launch traced here: 52.5 us
  Pallas kernels  23.5 us (44%)
  starting transfers between devices  19.2 us (36%)
  waiting for transfers between devices  9.02 us (17%)
  between operations  0.72 us (1%)
    all_to_all x1, starting transfers between devices, on_device(): got = lax.all_to_all(in_plane, ('r', 'x'), 0, 0, tiled=True)  9.15 us
    pallas_call x1, Pallas kernels, early(): pl.pallas_call(early_kernel, out_shape=(shape(24 * TRACE, LANES), pltpu.H...  7.67 us
    pallas_call x1, Pallas kernels, pack(): pl.pallas_call(pack_kernel, out_shape=(in_hbm_shape(PLANE * MESSAGE, LANE...  5.75 us
    ppermute x3, starting transfers between devices, along_y(): return lax.ppermute(value, 'y', [(i, (i + steps) % 4) for i in range(4)])  5.5 us
    all_to_all x1, waiting for transfers between devices, on_device(): lax.all_to_all(relayed, ('r', 'x'), 0, 0, tiled=True)  4.98 us
    all_to_all x1, starting transfers between devices, on_device(): lax.all_to_all(relayed, ('r', 'x'), 0, 0, tiled=True)  4.56 us
    all_to_all x1, waiting for transfers between devices, on_device(): got = lax.all_to_all(in_plane, ('r', 'x'), 0, 0, tiled=True)  4.03 us
    pallas_call x1, Pallas kernels, volume(): pl.pallas_call(volume_kernel, out_shape=(in_hbm_shape(1280, LANES), shape...  3.73 us
  transfers between devices with their start and end apart: 5, of which 2 were waited for; matrix products, arithmetic and copies ran while one was open for 0% of the time, Pallas kernels for 27%

profile of v7, /device:TPU:1, one launch (start us, length us, event | category | flops | bytes accessed | tf_op | source)
XLA Modules:
  0.0 52.5 jit_solution(8773182986110659230)
XLA Ops:
  0.6 0.1 pad_add_fusion.place_ref
  0.7 0.0 copy-start.2
  0.7 0.0 copy-start.3
  0.7 0.0 copy-start.4
  0.7 0.0 copy-start.5
  0.7 5.8 %pack.1 = (f32[1280,128]{1,0:T(8,128)}, f32[968,128]{1,0:T(8,128)}, f32[968,128]{1,0:T(8,128)}, f32[8,128]{1,0:T(8,128)S(1)}) custom-call(s32[2]{0:T(128)S(1)} %pad_add_fusion.place_ref, s32[3072]{0:T(1024)} %partner_ref.1, f32[5,64,512]{2,1,0:T(8,128)} %bitcast.13), custom_call_target="tpu_custom_call" | custom-call | tf_op jit(solution)/shard_map/pack/pallas_call | solution.py:728
  6.5 2.2 %collective-permute-start = (f32[968,128]{1,0:T(8,128)}, f32[968,128]{1,0:T(8,128)S(1)}, u32[]{:S(2)}, u32[]{:S(2)}) collective-permute-start(f32[968,128]{1,0:T(8,128)} %get-tuple-element.21), channel_id=1, source_target_pairs={{0,32},{32,64},{64,96},{96,0},{1,33},{33,65},{65,97},{97,1},{2,34}... | collective-permute-start | bytes 1486856 | tf_op jit(solution)/shard_map/ppermute | solution.py:855
  8.7 1.5 %collective-permute-start.1 = (f32[968,128]{1,0:T(8,128)}, f32[968,128]{1,0:T(8,128)}, u32[]{:S(2)}, u32[]{:S(2)}) collective-permute-start(f32[968,128]{1,0:T(8,128)} %get-tuple-element.22), channel_id=1, source_target_pairs={{0,96},{32,0},{64,32},{96,64},{1,97},{33,1},{65,33},{97,65},{2,98}... | collective-permute-start | bytes 1486856 | tf_op jit(solution)/shard_map/ppermute | solution.py:855
  10.2 0.0 copy-start
  10.2 0.0 copy-start.1
  10.2 9.2 %all-to-all-start = ((f32[32,40,128]{2,1,0:T(8,128)}), f32[32,40,128]{2,1,0:T(8,128)S(1)}, u32[]{:S(2)}, u32[]{:S(2)}) async-start(f32[32,40,128]{2,1,0:T(8,128)} %bitcast.24), calls=%async_computation | async-start | bytes 1310720 | tf_op jit(solution)/shard_map/all_to_all | solution.py:868
  19.4 1.8 %collective-permute-start.2 = (f32[8,128]{1,0:T(8,128)S(1)}, f32[8,128]{1,0:T(8,128)S(1)}, u32[]{:S(2)}, u32[]{:S(2)}) collective-permute-start(f32[8,128]{1,0:T(8,128)S(1)} %get-tuple-element.23.best_ref), channel_id=1, source_target_pairs={{0,64},{32,96},{64,0},{96,32},{1,65},{33,97},{65,1},{97,33},{2,66}... | collective-permute-start | bytes 12296 | tf_op jit(solution)/shard_map/ppermute | solution.py:855
  21.1 0.0 copy-done.2
  21.2 0.0 copy-done.3
  21.2 0.0 copy-done.4
  21.2 0.0 copy-done.5
  21.2 0.0 copy-done
  21.2 0.0 copy-done.1
  21.2 3.7 %volume.1 = (f32[1280,128]{1,0:T(8,128)}, f32[576,128]{1,0:T(8,128)S(1)}, s32[384,128]{1,0:T(8,128)S(1)}) custom-call(s32[2]{0:T(128)S(1)} %pad_add_fusion.place_ref, f32[5,64,512]{2,1,0:T(8,128)S(1)} %bitcast.14, f32[5,64,512]{2,1,0:T(8,128)S(1)} %bitcast.19, f32[3,3,512]{2,1,0:T(4,128)S(1)} %copy-done.4, f32[3,3072]{1,0:T(4,128)S(1)} %copy-done.3, ...), custom_call_target="tpu_custom_call" | custom-call | tf_op jit(solution)/shard_map/volume/pallas_call | solution.py:753
  24.9 0.0 collective-permute-done.up_ref
  24.9 0.0 collective-permute-done.1.down_ref
  24.9 1.9 %relay.1 = (f32[1312,128]{1,0:T(8,128)}, f32[8,128]{1,0:T(8,128)S(1)}) custom-call(s32[2]{0:T(128)S(1)} %pad_add_fusion.place_ref, f32[968,128]{1,0:T(8,128)S(1)} %collective-permute-done.up_ref, f32[968,128]{1,0:T(8,128)} %collective-permute-done.1.down_ref, f32[8,128]{1,0:T(8,128)S(1)} %get-tuple-element.23.best_ref, f32[1280,128]{1,0:T(8,128)} %get-tuple-element.17.rate_hbm), custom_call_target="tpu_custom_call" | custom-call | flops 99999997952 | bytes 100000000 | tf_op jit(solution)/shard_map/relay/pallas_call | solution.py:777
  26.9 0.0 collective-permute-done.2.far_ref
  26.9 1.0 %top.1 = f32[1312,1,128]{2,1,0:T(1,128)} custom-call(f32[8,128]{1,0:T(8,128)S(1)} %get-tuple-element.24.three_ref, f32[8,128]{1,0:T(8,128)S(1)} %collective-permute-done.2.far_ref, f32[1312,1,128]{2,1,0:T(1,128)} %bitcast.22), custom_call_target="tpu_custom_call", output_to_operand_aliasing={{}: (2, {})} | custom-call | tf_op jit(solution)/shard_map/top/pallas_call | solution.py:789
  27.9 4.0 %all-to-all-done = f32[32,40,128]{2,1,0:T(8,128)S(1)} async-done(((f32[32,40,128]{2,1,0:T(8,128)}), f32[32,40,128]{2,1,0:T(8,128)S(1)}, u32[]{:S(2)}, u32[]{:S(2)}) %all-to-all-start) | async-done | bytes 655392 | tf_op jit(solution)/shard_map/all_to_all | solution.py:868
  31.9 4.6 %all-to-all-start.1 = ((f32[32,41,1,128]{3,2,1,0:T(1,128)}), f32[32,41,1,128]{3,2,1,0:T(1,128)S(1)}, u32[]{:S(2)}, u32[]{:S(2)}) async-start(f32[32,41,1,128]{3,2,1,0:T(1,128)} %bitcast.23), calls=%async_computation.1 | async-start | bytes 1343488 | tf_op jit(solution)/shard_map/all_to_all | solution.py:880
  36.5 7.7 %early.1 = (f32[1920,128]{1,0:T(8,128)S(1)}, s32[11264]{0:T(1024)}) custom-call(s32[2]{0:T(128)S(1)} %pad_add_fusion.place_ref, s32[3072]{0:T(1024)S(1)} %copy-done.2, s32[11264]{0:T(1024)S(1)} %broadcast_in_dim.3.blank_hbm, f32[5,64,512]{2,1,0:T(8,128)S(1)} %bitcast.15, f32[1280,128]{1,0:T(8,128)S(1)} %bitcast.18), custom_call_target="tpu_custom_call" | custom-call | tf_op jit(solution)/shard_map/early/pallas_call | solution.py:802
  44.2 5.0 %all-to-all-done.1 = f32[32,41,1,128]{3,2,1,0:T(1,128)S(1)} async-done(((f32[32,41,1,128]{3,2,1,0:T(1,128)}), f32[32,41,1,128]{3,2,1,0:T(1,128)S(1)}, u32[]{:S(2)}, u32[]{:S(2)}) %all-to-all-start.1) | async-done | bytes 671776 | tf_op jit(solution)/shard_map/all_to_all | solution.py:880
  49.1 3.4 %finish.1 = (f32[5,64,512]{2,1,0:T(8,128)}, f32[5,64,512]{2,1,0:T(8,128)}) custom-call(s32[2]{0:T(128)S(1)} %pad_add_fusion.place_ref, s32[11264]{0:T(1024)} %get-tuple-element.16.owner_hbm, f32[1280,128]{1,0:T(8,128)} %get-tuple-element.17.rate_hbm, f32[1920,128]{1,0:T(8,128)S(1)} %get-tuple-element.18.other_ref, ...), custom_call_target="tpu_custom_call" | custom-call | tf_op jit(solution)/shard_map/finish/pallas_call | solution.py:823
  (1 shorter events, 0.0 us)
Async XLA Ops:
  0.7 20.4 %copy-start.2 = (s32[3072]{0:T(1024)S(1)}, s32[3072]{0:T(1024)}, u32[]{:S(2)}) copy-start(s32[3072]{0:T(1024)} %partner_ref.1) | copy-start | bytes 36868
  0.7 20.4 %copy-start.3 = (f32[3,3072]{1,0:T(4,128)S(1)}, f32[3,3072]{1,0:T(4,128)}, u32[]{:S(2)}) copy-start(f32[3,3072]{1,0:T(4,128)} %normal_ref.1) | copy-start | bytes 110596
  0.7 20.4 %copy-start.4 = (f32[3,3,512]{2,1,0:T(4,128)S(1)}, f32[3,3,512]{2,1,0:T(4,128)}, u32[]{:S(2)}) copy-start(f32[3,3,512]{2,1,0:T(4,128)} %metric_ref.1) | copy-start | bytes 55300
  0.7 20.4 %copy-start.5 = (s32[3072]{0:T(1024)S(1)}, s32[3072]{0:T(1024)}, u32[]{:S(2)}) copy-start(s32[3072]{0:T(1024)} %param.13) | copy-start | bytes 36868
  6.5 18.4 %collective-permute-start = (f32[968,128]{1,0:T(8,128)}, f32[968,128]{1,0:T(8,128)S(1)}, u32[]{:S(2)}, u32[]{:S(2)}) collective-permute-start(f32[968,128]{1,0:T(8,128)} %get-tuple-element.21), channel_id=1, source_target_pairs={{0,32},{32,64},{64,96},{96,0},{1,33},{33,65},{65,97},{97,1},{2,34}... | collective-permute-start | bytes 1486856 | tf_op jit(solution)/shard_map/ppermute | solution.py:855
  8.7 16.2 %collective-permute-start.1 = (f32[968,128]{1,0:T(8,128)}, f32[968,128]{1,0:T(8,128)}, u32[]{:S(2)}, u32[]{:S(2)}) collective-permute-start(f32[968,128]{1,0:T(8,128)} %get-tuple-element.22), channel_id=1, source_target_pairs={{0,96},{32,0},{64,32},{96,64},{1,97},{33,1},{65,33},{97,65},{2,98}... | collective-permute-start | bytes 1486856 | tf_op jit(solution)/shard_map/ppermute | solution.py:855
  10.2 11.0 %copy-start = (f32[64,5,512]{2,0,1:T(8,128)S(1)}, f32[64,5,512]{2,0,1:T(8,128)}, u32[]{:S(2)}) copy-start(f32[64,5,512]{2,0,1:T(8,128)} %param.8) | copy-start | bytes 1966084
  10.2 11.0 %copy-start.1 = (f32[64,5,512]{2,0,1:T(8,128)S(1)}, f32[64,5,512]{2,0,1:T(8,128)}, u32[]{:S(2)}) copy-start(f32[64,5,512]{2,0,1:T(8,128)} %param.9) | copy-start | bytes 1966084
  10.2 21.7 %all-to-all-start = ((f32[32,40,128]{2,1,0:T(8,128)}), f32[32,40,128]{2,1,0:T(8,128)S(1)}, u32[]{:S(2)}, u32[]{:S(2)}) async-start(f32[32,40,128]{2,1,0:T(8,128)} %bitcast.24), calls=%async_computation | async-start | bytes 1310720 | tf_op jit(solution)/shard_map/all_to_all | solution.py:868
  19.4 7.5 %collective-permute-start.2 = (f32[8,128]{1,0:T(8,128)S(1)}, f32[8,128]{1,0:T(8,128)S(1)}, u32[]{:S(2)}, u32[]{:S(2)}) collective-permute-start(f32[8,128]{1,0:T(8,128)S(1)} %get-tuple-element.23.best_ref), channel_id=1, source_target_pairs={{0,64},{32,96},{64,0},{96,32},{1,65},{33,97},{65,1},{97,33},{2,66}... | collective-permute-start | bytes 12296 | tf_op jit(solution)/shard_map/ppermute | solution.py:855
  31.9 17.2 %all-to-all-start.1 = ((f32[32,41,1,128]{3,2,1,0:T(1,128)}), f32[32,41,1,128]{3,2,1,0:T(1,128)S(1)}, u32[]{:S(2)}, u32[]{:S(2)}) async-start(f32[32,41,1,128]{3,2,1,0:T(1,128)} %bitcast.23), calls=%async_computation.1 | async-start | bytes 1343488 | tf_op jit(solution)/shard_map/all_to_all | solution.py:880

commit v8 on v7

--- a/solution.py
+++ b/solution.py
@@ -220,9 +220,11 @@
             state_ref[v, pl.ds(pl.multiple_of(step * 8, 8), 8), :] for v in range(5)
         ]
         inverse = 1.0 / density
-        square = (mom_x * mom_x + mom_y * mom_y + mom_z * mom_z) * inverse
-        pressure = (HEAT_RATIO - 1.0) * (energy - 0.5 * square)
-        wave = jnp.sqrt(square * inverse) + jnp.sqrt(HEAT_RATIO * pressure * inverse)
+        speed_x, speed_y, speed_z = mom_x * inverse, mom_y * inverse, mom_z * inverse
+        square = speed_x * speed_x + speed_y * speed_y + speed_z * speed_z
+        kinetic = mom_x * speed_x + mom_y * speed_y + mom_z * speed_z
+        pressure = (HEAT_RATIO - 1.0) * (energy - 0.5 * kinetic)
+        wave = jnp.sqrt(square) + jnp.sqrt(HEAT_RATIO * pressure * inverse)
         return jnp.maximum(best, wave)
 
     best = lax.fori_loop(0, 8, speeds, jnp.zeros((8, ELEMENTS), jnp.float32))

time: 52.9 us -> 53 us (level)
  no operation moved by 1% of the time
where the time goes in v8:
time: 53 us; the launch traced here: 52.6 us
  Pallas kernels  23.5 us (44%)
  starting transfers between devices  19.2 us (36%)
  waiting for transfers between devices  9.02 us (17%)
  between operations  0.72 us (1%)
    all_to_all x1, starting transfers between devices, on_device(): got = lax.all_to_all(in_plane, ('r', 'x'), 0, 0, tiled=True)  9.15 us
    pallas_call x1, Pallas kernels, early(): pl.pallas_call(early_kernel, out_shape=(shape(24 * TRACE, LANES), pltpu.H...  7.67 us
    pallas_call x1, Pallas kernels, pack(): pl.pallas_call(pack_kernel, out_shape=(in_hbm_shape(PLANE * MESSAGE, LANE...  5.79 us
    ppermute x3, starting transfers between devices, along_y(): return lax.ppermute(value, 'y', [(i, (i + steps) % 4) for i in range(4)])  5.5 us
    all_to_all x1, waiting for transfers between devices, on_device(): lax.all_to_all(relayed, ('r', 'x'), 0, 0, tiled=True)  4.98 us
    all_to_all x1, starting transfers between devices, on_device(): lax.all_to_all(relayed, ('r', 'x'), 0, 0, tiled=True)  4.56 us
    all_to_all x1, waiting for transfers between devices, on_device(): got = lax.all_to_all(in_plane, ('r', 'x'), 0, 0, tiled=True)  4.03 us
    pallas_call x1, Pallas kernels, volume(): pl.pallas_call(volume_kernel, out_shape=(in_hbm_shape(1280, LANES), shape...  3.73 us
  transfers between devices with their start and end apart: 5, of which 2 were waited for; matrix products, arithmetic and copies ran while one was open for 0% of the time, Pallas kernels for 27%

profile of v8, /device:TPU:1, one launch (start us, length us, event | category | flops | bytes accessed | tf_op | source)
XLA Modules:
  0.0 52.6 jit_solution(14830279658822137976)
XLA Ops:
  0.6 0.1 pad_add_fusion.place_ref
  0.7 0.0 copy-start.2
  0.7 0.0 copy-start.3
  0.7 0.0 copy-start.4
  0.7 0.0 copy-start.5
  0.7 5.8 %pack.1 = (f32[1280,128]{1,0:T(8,128)}, f32[968,128]{1,0:T(8,128)}, f32[968,128]{1,0:T(8,128)}, f32[8,128]{1,0:T(8,128)S(1)}) custom-call(s32[2]{0:T(128)S(1)} %pad_add_fusion.place_ref, s32[3072]{0:T(1024)} %partner_ref.1, f32[5,64,512]{2,1,0:T(8,128)} %bitcast.13), custom_call_target="tpu_custom_call" | custom-call | tf_op jit(solution)/shard_map/pack/pallas_call | solution.py:730
  6.5 2.2 %collective-permute-start = (f32[968,128]{1,0:T(8,128)}, f32[968,128]{1,0:T(8,128)S(1)}, u32[]{:S(2)}, u32[]{:S(2)}) collective-permute-start(f32[968,128]{1,0:T(8,128)} %get-tuple-element.21), channel_id=1, source_target_pairs={{0,32},{32,64},{64,96},{96,0},{1,33},{33,65},{65,97},{97,1},{2,34}... | collective-permute-start | bytes 1486856 | tf_op jit(solution)/shard_map/ppermute | solution.py:857
  8.7 1.5 %collective-permute-start.1 = (f32[968,128]{1,0:T(8,128)}, f32[968,128]{1,0:T(8,128)}, u32[]{:S(2)}, u32[]{:S(2)}) collective-permute-start(f32[968,128]{1,0:T(8,128)} %get-tuple-element.22), channel_id=1, source_target_pairs={{0,96},{32,0},{64,32},{96,64},{1,97},{33,1},{65,33},{97,65},{2,98}... | collective-permute-start | bytes 1486856 | tf_op jit(solution)/shard_map/ppermute | solution.py:857
  10.2 0.0 copy-start
  10.2 0.0 copy-start.1
  10.2 9.2 %all-to-all-start = ((f32[32,40,128]{2,1,0:T(8,128)}), f32[32,40,128]{2,1,0:T(8,128)S(1)}, u32[]{:S(2)}, u32[]{:S(2)}) async-start(f32[32,40,128]{2,1,0:T(8,128)} %bitcast.24), calls=%async_computation | async-start | bytes 1310720 | tf_op jit(solution)/shard_map/all_to_all | solution.py:870
  19.4 1.8 %collective-permute-start.2 = (f32[8,128]{1,0:T(8,128)S(1)}, f32[8,128]{1,0:T(8,128)S(1)}, u32[]{:S(2)}, u32[]{:S(2)}) collective-permute-start(f32[8,128]{1,0:T(8,128)S(1)} %get-tuple-element.23.best_ref), channel_id=1, source_target_pairs={{0,64},{32,96},{64,0},{96,32},{1,65},{33,97},{65,1},{97,33},{2,66}... | collective-permute-start | bytes 12296 | tf_op jit(solution)/shard_map/ppermute | solution.py:857
  21.2 0.0 copy-done.2
  21.2 0.0 copy-done.3
  21.2 0.0 copy-done.4
  21.2 0.0 copy-done.5
  21.2 0.0 copy-done
  21.2 0.0 copy-done.1
  21.2 3.7 %volume.1 = (f32[1280,128]{1,0:T(8,128)}, f32[576,128]{1,0:T(8,128)S(1)}, s32[384,128]{1,0:T(8,128)S(1)}) custom-call(s32[2]{0:T(128)S(1)} %pad_add_fusion.place_ref, f32[5,64,512]{2,1,0:T(8,128)S(1)} %bitcast.14, f32[5,64,512]{2,1,0:T(8,128)S(1)} %bitcast.19, f32[3,3,512]{2,1,0:T(4,128)S(1)} %copy-done.4, f32[3,3072]{1,0:T(4,128)S(1)} %copy-done.3, ...), custom_call_target="tpu_custom_call" | custom-call | tf_op jit(solution)/shard_map/volume/pallas_call | solution.py:755
  25.0 0.0 collective-permute-done.up_ref
  25.0 0.0 collective-permute-done.1.down_ref
  25.0 1.9 %relay.1 = (f32[1312,128]{1,0:T(8,128)}, f32[8,128]{1,0:T(8,128)S(1)}) custom-call(s32[2]{0:T(128)S(1)} %pad_add_fusion.place_ref, f32[968,128]{1,0:T(8,128)S(1)} %collective-permute-done.up_ref, f32[968,128]{1,0:T(8,128)} %collective-permute-done.1.down_ref, f32[8,128]{1,0:T(8,128)S(1)} %get-tuple-element.23.best_ref, f32[1280,128]{1,0:T(8,128)} %get-tuple-element.17.rate_hbm), custom_call_target="tpu_custom_call" | custom-call | flops 99999997952 | bytes 100000000 | tf_op jit(solution)/shard_map/relay/pallas_call | solution.py:779
  26.9 0.0 collective-permute-done.2.far_ref
  26.9 1.0 %top.1 = f32[1312,1,128]{2,1,0:T(1,128)} custom-call(f32[8,128]{1,0:T(8,128)S(1)} %get-tuple-element.24.three_ref, f32[8,128]{1,0:T(8,128)S(1)} %collective-permute-done.2.far_ref, f32[1312,1,128]{2,1,0:T(1,128)} %bitcast.22), custom_call_target="tpu_custom_call", output_to_operand_aliasing={{}: (2, {})} | custom-call | tf_op jit(solution)/shard_map/top/pallas_call | solution.py:791
  27.9 4.0 %all-to-all-done = f32[32,40,128]{2,1,0:T(8,128)S(1)} async-done(((f32[32,40,128]{2,1,0:T(8,128)}), f32[32,40,128]{2,1,0:T(8,128)S(1)}, u32[]{:S(2)}, u32[]{:S(2)}) %all-to-all-start) | async-done | bytes 655392 | tf_op jit(solution)/shard_map/all_to_all | solution.py:870
  31.9 4.6 %all-to-all-start.1 = ((f32[32,41,1,128]{3,2,1,0:T(1,128)}), f32[32,41,1,128]{3,2,1,0:T(1,128)S(1)}, u32[]{:S(2)}, u32[]{:S(2)}) async-start(f32[32,41,1,128]{3,2,1,0:T(1,128)} %bitcast.23), calls=%async_computation.1 | async-start | bytes 1343488 | tf_op jit(solution)/shard_map/all_to_all | solution.py:882
  36.5 7.7 %early.1 = (f32[1920,128]{1,0:T(8,128)S(1)}, s32[11264]{0:T(1024)}) custom-call(s32[2]{0:T(128)S(1)} %pad_add_fusion.place_ref, s32[3072]{0:T(1024)S(1)} %copy-done.2, s32[11264]{0:T(1024)S(1)} %broadcast_in_dim.3.blank_hbm, f32[5,64,512]{2,1,0:T(8,128)S(1)} %bitcast.15, f32[1280,128]{1,0:T(8,128)S(1)} %bitcast.18), custom_call_target="tpu_custom_call" | custom-call | tf_op jit(solution)/shard_map/early/pallas_call | solution.py:804
  44.2 5.0 %all-to-all-done.1 = f32[32,41,1,128]{3,2,1,0:T(1,128)S(1)} async-done(((f32[32,41,1,128]{3,2,1,0:T(1,128)}), f32[32,41,1,128]{3,2,1,0:T(1,128)S(1)}, u32[]{:S(2)}, u32[]{:S(2)}) %all-to-all-start.1) | async-done | bytes 671776 | tf_op jit(solution)/shard_map/all_to_all | solution.py:882
  49.2 3.4 %finish.1 = (f32[5,64,512]{2,1,0:T(8,128)}, f32[5,64,512]{2,1,0:T(8,128)}) custom-call(s32[2]{0:T(128)S(1)} %pad_add_fusion.place_ref, s32[11264]{0:T(1024)} %get-tuple-element.16.owner_hbm, f32[1280,128]{1,0:T(8,128)} %get-tuple-element.17.rate_hbm, f32[1920,128]{1,0:T(8,128)S(1)} %get-tuple-element.18.other_ref, ...), custom_call_target="tpu_custom_call" | custom-call | tf_op jit(solution)/shard_map/finish/pallas_call | solution.py:825
  (1 shorter events, 0.0 us)
Async XLA Ops:
  0.7 20.5 %copy-start.2 = (s32[3072]{0:T(1024)S(1)}, s32[3072]{0:T(1024)}, u32[]{:S(2)}) copy-start(s32[3072]{0:T(1024)} %partner_ref.1) | copy-start | bytes 36868
  0.7 20.5 %copy-start.3 = (f32[3,3072]{1,0:T(4,128)S(1)}, f32[3,3072]{1,0:T(4,128)}, u32[]{:S(2)}) copy-start(f32[3,3072]{1,0:T(4,128)} %normal_ref.1) | copy-start | bytes 110596
  0.7 20.5 %copy-start.4 = (f32[3,3,512]{2,1,0:T(4,128)S(1)}, f32[3,3,512]{2,1,0:T(4,128)}, u32[]{:S(2)}) copy-start(f32[3,3,512]{2,1,0:T(4,128)} %metric_ref.1) | copy-start | bytes 55300
  0.7 20.5 %copy-start.5 = (s32[3072]{0:T(1024)S(1)}, s32[3072]{0:T(1024)}, u32[]{:S(2)}) copy-start(s32[3072]{0:T(1024)} %param.13) | copy-start | bytes 36868
  6.5 18.4 %collective-permute-start = (f32[968,128]{1,0:T(8,128)}, f32[968,128]{1,0:T(8,128)S(1)}, u32[]{:S(2)}, u32[]{:S(2)}) collective-permute-start(f32[968,128]{1,0:T(8,128)} %get-tuple-element.21), channel_id=1, source_target_pairs={{0,32},{32,64},{64,96},{96,0},{1,33},{33,65},{65,97},{97,1},{2,34}... | collective-permute-start | bytes 1486856 | tf_op jit(solution)/shard_map/ppermute | solution.py:857
  8.7 16.2 %collective-permute-start.1 = (f32[968,128]{1,0:T(8,128)}, f32[968,128]{1,0:T(8,128)}, u32[]{:S(2)}, u32[]{:S(2)}) collective-permute-start(f32[968,128]{1,0:T(8,128)} %get-tuple-element.22), channel_id=1, source_target_pairs={{0,96},{32,0},{64,32},{96,64},{1,97},{33,1},{65,33},{97,65},{2,98}... | collective-permute-start | bytes 1486856 | tf_op jit(solution)/shard_map/ppermute | solution.py:857
  10.2 11.0 %copy-start = (f32[64,5,512]{2,0,1:T(8,128)S(1)}, f32[64,5,512]{2,0,1:T(8,128)}, u32[]{:S(2)}) copy-start(f32[64,5,512]{2,0,1:T(8,128)} %param.8) | copy-start | bytes 1966084
  10.2 11.0 %copy-start.1 = (f32[64,5,512]{2,0,1:T(8,128)S(1)}, f32[64,5,512]{2,0,1:T(8,128)}, u32[]{:S(2)}) copy-start(f32[64,5,512]{2,0,1:T(8,128)} %param.9) | copy-start | bytes 1966084
  10.2 21.7 %all-to-all-start = ((f32[32,40,128]{2,1,0:T(8,128)}), f32[32,40,128]{2,1,0:T(8,128)S(1)}, u32[]{:S(2)}, u32[]{:S(2)}) async-start(f32[32,40,128]{2,1,0:T(8,128)} %bitcast.24), calls=%async_computation | async-start | bytes 1310720 | tf_op jit(solution)/shard_map/all_to_all | solution.py:870
  19.4 7.5 %collective-permute-start.2 = (f32[8,128]{1,0:T(8,128)S(1)}, f32[8,128]{1,0:T(8,128)S(1)}, u32[]{:S(2)}, u32[]{:S(2)}) collective-permute-start(f32[8,128]{1,0:T(8,128)S(1)} %get-tuple-element.23.best_ref), channel_id=1, source_target_pairs={{0,64},{32,96},{64,0},{96,32},{1,65},{33,97},{65,1},{97,33},{2,66}... | collective-permute-start | bytes 12296 | tf_op jit(solution)/shard_map/ppermute | solution.py:857
  31.9 17.2 %all-to-all-start.1 = ((f32[32,41,1,128]{3,2,1,0:T(1,128)}), f32[32,41,1,128]{3,2,1,0:T(1,128)S(1)}, u32[]{:S(2)}, u32[]{:S(2)}) async-start(f32[32,41,1,128]{3,2,1,0:T(1,128)} %bitcast.23), calls=%async_computation.1 | async-start | bytes 1343488 | tf_op jit(solution)/shard_map/all_to_all | solution.py:882

commit v9 on v8

--- a/solution.py
+++ b/solution.py
@@ -613,16 +613,18 @@
         return carry
 
     chunk = SLOTS // UNROLL
-    for copy in copies[:2]:
-        copy.wait()
-
-    @pl.when(plane > 0)
+    from_low = (plane > 0) & (spot < CROSS)
+    from_high = (plane < 3) & (spot >= NEAR)
+
+    @pl.when(from_low)
     def _():
+        copies[0].wait()
         lax.fori_loop(spot * chunk, CROSS * chunk, place_low, 0)
 
-    @pl.when(plane < 3)
+    @pl.when(from_high)
     def _():
-        lax.fori_loop(0, jnp.maximum(spot - NEAR + 1, 0) * chunk, place_high, 0)
+        copies[1].wait()
+        lax.fori_loop(0, (spot - NEAR + 1) * chunk, place_high, 0)
 
     tops = [relay_ref[b * LONG + MESSAGE : (b + 1) * LONG, :] for b in range(PLANE)]
     top = jnp.max(functools.reduce(jnp.maximum, tops))
@@ -689,6 +691,8 @@
 
     for block in range(BLOCKS):
         element_block(block)
+    pl.when(jnp.logical_not(from_low))(copies[0].wait)
+    pl.when(jnp.logical_not(from_high))(copies[1].wait)
     for block in range(BLOCKS):
         for copy in results(block):
             copy.wait()

time: 53 us -> 52.9 us (level)
  no operation moved by 1% of the time
where the time goes in v9:
time: 52.9 us; the launch traced here: 52.5 us
  Pallas kernels  23.5 us (44%)
  starting transfers between devices  19.2 us (36%)
  waiting for transfers between devices  9.02 us (17%)
  between operations  0.72 us (1%)
    all_to_all x1, starting transfers between devices, on_device(): got = lax.all_to_all(in_plane, ('r', 'x'), 0, 0, tiled=True)  9.15 us
    pallas_call x1, Pallas kernels, early(): pl.pallas_call(early_kernel, out_shape=(shape(24 * TRACE, LANES), pltpu.H...  7.67 us
    pallas_call x1, Pallas kernels, pack(): pl.pallas_call(pack_kernel, out_shape=(in_hbm_shape(PLANE * MESSAGE, LANE...  5.79 us
    ppermute x3, starting transfers between devices, along_y(): return lax.ppermute(value, 'y', [(i, (i + steps) % 4) for i in range(4)])  5.5 us
    all_to_all x1, waiting for transfers between devices, on_device(): lax.all_to_all(relayed, ('r', 'x'), 0, 0, tiled=True)  4.98 us
    all_to_all x1, starting transfers between devices, on_device(): lax.all_to_all(relayed, ('r', 'x'), 0, 0, tiled=True)  4.56 us
    all_to_all x1, waiting for transfers between devices, on_device(): got = lax.all_to_all(in_plane, ('r', 'x'), 0, 0, tiled=True)  4.03 us
    pallas_call x1, Pallas kernels, volume(): pl.pallas_call(volume_kernel, out_shape=(in_hbm_shape(1280, LANES), shape...  3.73 us
  transfers between devices with their start and end apart: 5, of which 2 were waited for; matrix products, arithmetic and copies ran while one was open for 0% of the time, Pallas kernels for 27%

profile of v9, /device:TPU:1, one launch (start us, length us, event | category | flops | bytes accessed | tf_op | source)
XLA Modules:
  0.0 52.5 jit_solution(10139109443236124559)
XLA Ops:
  0.6 0.1 pad_add_fusion.place_ref
  0.7 0.0 copy-start.2
  0.7 0.0 copy-start.3
  0.7 0.0 copy-start.4
  0.7 0.0 copy-start.5
  0.7 5.8 %pack.1 = (f32[1280,128]{1,0:T(8,128)}, f32[968,128]{1,0:T(8,128)}, f32[968,128]{1,0:T(8,128)}, f32[8,128]{1,0:T(8,128)S(1)}) custom-call(s32[2]{0:T(128)S(1)} %pad_add_fusion.place_ref, s32[3072]{0:T(1024)} %partner_ref.1, f32[5,64,512]{2,1,0:T(8,128)} %bitcast.13), custom_call_target="tpu_custom_call" | custom-call | tf_op jit(solution)/shard_map/pack/pallas_call | solution.py:734
  6.5 2.2 %collective-permute-start = (f32[968,128]{1,0:T(8,128)}, f32[968,128]{1,0:T(8,128)S(1)}, u32[]{:S(2)}, u32[]{:S(2)}) collective-permute-start(f32[968,128]{1,0:T(8,128)} %get-tuple-element.21), channel_id=1, source_target_pairs={{0,32},{32,64},{64,96},{96,0},{1,33},{33,65},{65,97},{97,1},{2,34}... | collective-permute-start | bytes 1486856 | tf_op jit(solution)/shard_map/ppermute | solution.py:861
  8.7 1.5 %collective-permute-start.1 = (f32[968,128]{1,0:T(8,128)}, f32[968,128]{1,0:T(8,128)}, u32[]{:S(2)}, u32[]{:S(2)}) collective-permute-start(f32[968,128]{1,0:T(8,128)} %get-tuple-element.22), channel_id=1, source_target_pairs={{0,96},{32,0},{64,32},{96,64},{1,97},{33,1},{65,33},{97,65},{2,98}... | collective-permute-start | bytes 1486856 | tf_op jit(solution)/shard_map/ppermute | solution.py:861
  10.2 0.0 copy-start
  10.2 0.0 copy-start.1
  10.2 9.2 %all-to-all-start = ((f32[32,40,128]{2,1,0:T(8,128)}), f32[32,40,128]{2,1,0:T(8,128)S(1)}, u32[]{:S(2)}, u32[]{:S(2)}) async-start(f32[32,40,128]{2,1,0:T(8,128)} %bitcast.24), calls=%async_computation | async-start | bytes 1310720 | tf_op jit(solution)/shard_map/all_to_all | solution.py:874
  19.4 1.8 %collective-permute-start.2 = (f32[8,128]{1,0:T(8,128)S(1)}, f32[8,128]{1,0:T(8,128)S(1)}, u32[]{:S(2)}, u32[]{:S(2)}) collective-permute-start(f32[8,128]{1,0:T(8,128)S(1)} %get-tuple-element.23.best_ref), channel_id=1, source_target_pairs={{0,64},{32,96},{64,0},{96,32},{1,65},{33,97},{65,1},{97,33},{2,66}... | collective-permute-start | bytes 12296 | tf_op jit(solution)/shard_map/ppermute | solution.py:861
  21.2 0.0 copy-done.2
  21.2 0.0 copy-done.3
  21.2 0.0 copy-done.4
  21.2 0.0 copy-done.5
  21.2 0.0 copy-done
  21.2 0.0 copy-done.1
  21.2 3.7 %volume.1 = (f32[1280,128]{1,0:T(8,128)}, f32[576,128]{1,0:T(8,128)S(1)}, s32[384,128]{1,0:T(8,128)S(1)}) custom-call(s32[2]{0:T(128)S(1)} %pad_add_fusion.place_ref, f32[5,64,512]{2,1,0:T(8,128)S(1)} %bitcast.14, f32[5,64,512]{2,1,0:T(8,128)S(1)} %bitcast.19, f32[3,3,512]{2,1,0:T(4,128)S(1)} %copy-done.4, f32[3,3072]{1,0:T(4,128)S(1)} %copy-done.3, ...), custom_call_target="tpu_custom_call" | custom-call | tf_op jit(solution)/shard_map/volume/pallas_call | solution.py:759
  25.0 0.0 collective-permute-done.up_ref
  25.0 0.0 collective-permute-done.1.down_ref
  25.0 1.9 %relay.1 = (f32[1312,128]{1,0:T(8,128)}, f32[8,128]{1,0:T(8,128)S(1)}) custom-call(s32[2]{0:T(128)S(1)} %pad_add_fusion.place_ref, f32[968,128]{1,0:T(8,128)S(1)} %collective-permute-done.up_ref, f32[968,128]{1,0:T(8,128)} %collective-permute-done.1.down_ref, f32[8,128]{1,0:T(8,128)S(1)} %get-tuple-element.23.best_ref, f32[1280,128]{1,0:T(8,128)} %get-tuple-element.17.rate_hbm), custom_call_target="tpu_custom_call" | custom-call | flops 99999997952 | bytes 100000000 | tf_op jit(solution)/shard_map/relay/pallas_call | solution.py:783
  26.9 0.0 collective-permute-done.2.far_ref
  26.9 1.0 %top.1 = f32[1312,1,128]{2,1,0:T(1,128)} custom-call(f32[8,128]{1,0:T(8,128)S(1)} %get-tuple-element.24.three_ref, f32[8,128]{1,0:T(8,128)S(1)} %collective-permute-done.2.far_ref, f32[1312,1,128]{2,1,0:T(1,128)} %bitcast.22), custom_call_target="tpu_custom_call", output_to_operand_aliasing={{}: (2, {})} | custom-call | tf_op jit(solution)/shard_map/top/pallas_call | solution.py:795
  27.9 4.0 %all-to-all-done = f32[32,40,128]{2,1,0:T(8,128)S(1)} async-done(((f32[32,40,128]{2,1,0:T(8,128)}), f32[32,40,128]{2,1,0:T(8,128)S(1)}, u32[]{:S(2)}, u32[]{:S(2)}) %all-to-all-start) | async-done | bytes 655392 | tf_op jit(solution)/shard_map/all_to_all | solution.py:874
  31.9 4.6 %all-to-all-start.1 = ((f32[32,41,1,128]{3,2,1,0:T(1,128)}), f32[32,41,1,128]{3,2,1,0:T(1,128)S(1)}, u32[]{:S(2)}, u32[]{:S(2)}) async-start(f32[32,41,1,128]{3,2,1,0:T(1,128)} %bitcast.23), calls=%async_computation.1 | async-start | bytes 1343488 | tf_op jit(solution)/shard_map/all_to_all | solution.py:886
  36.5 7.7 %early.1 = (f32[1920,128]{1,0:T(8,128)S(1)}, s32[11264]{0:T(1024)}) custom-call(s32[2]{0:T(128)S(1)} %pad_add_fusion.place_ref, s32[3072]{0:T(1024)S(1)} %copy-done.2, s32[11264]{0:T(1024)S(1)} %broadcast_in_dim.3.blank_hbm, f32[5,64,512]{2,1,0:T(8,128)S(1)} %bitcast.15, f32[1280,128]{1,0:T(8,128)S(1)} %bitcast.18), custom_call_target="tpu_custom_call" | custom-call | tf_op jit(solution)/shard_map/early/pallas_call | solution.py:808
  44.2 5.0 %all-to-all-done.1 = f32[32,41,1,128]{3,2,1,0:T(1,128)S(1)} async-done(((f32[32,41,1,128]{3,2,1,0:T(1,128)}), f32[32,41,1,128]{3,2,1,0:T(1,128)S(1)}, u32[]{:S(2)}, u32[]{:S(2)}) %all-to-all-start.1) | async-done | bytes 671776 | tf_op jit(solution)/shard_map/all_to_all | solution.py:886
  49.2 3.3 %finish.1 = (f32[5,64,512]{2,1,0:T(8,128)}, f32[5,64,512]{2,1,0:T(8,128)}) custom-call(s32[2]{0:T(128)S(1)} %pad_add_fusion.place_ref, s32[11264]{0:T(1024)} %get-tuple-element.16.owner_hbm, f32[1280,128]{1,0:T(8,128)} %get-tuple-element.17.rate_hbm, f32[1920,128]{1,0:T(8,128)S(1)} %get-tuple-element.18.other_ref, ...), custom_call_target="tpu_custom_call" | custom-call | tf_op jit(solution)/shard_map/finish/pallas_call | solution.py:829
  (1 shorter events, 0.0 us)
Async XLA Ops:
  0.7 20.5 %copy-start.2 = (s32[3072]{0:T(1024)S(1)}, s32[3072]{0:T(1024)}, u32[]{:S(2)}) copy-start(s32[3072]{0:T(1024)} %partner_ref.1) | copy-start | bytes 36868
  0.7 20.5 %copy-start.3 = (f32[3,3072]{1,0:T(4,128)S(1)}, f32[3,3072]{1,0:T(4,128)}, u32[]{:S(2)}) copy-start(f32[3,3072]{1,0:T(4,128)} %normal_ref.1) | copy-start | bytes 110596
  0.7 20.5 %copy-start.4 = (f32[3,3,512]{2,1,0:T(4,128)S(1)}, f32[3,3,512]{2,1,0:T(4,128)}, u32[]{:S(2)}) copy-start(f32[3,3,512]{2,1,0:T(4,128)} %metric_ref.1) | copy-start | bytes 55300
  0.7 20.5 %copy-start.5 = (s32[3072]{0:T(1024)S(1)}, s32[3072]{0:T(1024)}, u32[]{:S(2)}) copy-start(s32[3072]{0:T(1024)} %param.13) | copy-start | bytes 36868
  6.5 18.4 %collective-permute-start = (f32[968,128]{1,0:T(8,128)}, f32[968,128]{1,0:T(8,128)S(1)}, u32[]{:S(2)}, u32[]{:S(2)}) collective-permute-start(f32[968,128]{1,0:T(8,128)} %get-tuple-element.21), channel_id=1, source_target_pairs={{0,32},{32,64},{64,96},{96,0},{1,33},{33,65},{65,97},{97,1},{2,34}... | collective-permute-start | bytes 1486856 | tf_op jit(solution)/shard_map/ppermute | solution.py:861
  8.7 16.2 %collective-permute-start.1 = (f32[968,128]{1,0:T(8,128)}, f32[968,128]{1,0:T(8,128)}, u32[]{:S(2)}, u32[]{:S(2)}) collective-permute-start(f32[968,128]{1,0:T(8,128)} %get-tuple-element.22), channel_id=1, source_target_pairs={{0,96},{32,0},{64,32},{96,64},{1,97},{33,1},{65,33},{97,65},{2,98}... | collective-permute-start | bytes 1486856 | tf_op jit(solution)/shard_map/ppermute | solution.py:861
  10.2 11.0 %copy-start = (f32[64,5,512]{2,0,1:T(8,128)S(1)}, f32[64,5,512]{2,0,1:T(8,128)}, u32[]{:S(2)}) copy-start(f32[64,5,512]{2,0,1:T(8,128)} %param.8) | copy-start | bytes 1966084
  10.2 11.0 %copy-start.1 = (f32[64,5,512]{2,0,1:T(8,128)S(1)}, f32[64,5,512]{2,0,1:T(8,128)}, u32[]{:S(2)}) copy-start(f32[64,5,512]{2,0,1:T(8,128)} %param.9) | copy-start | bytes 1966084
  10.2 21.7 %all-to-all-start = ((f32[32,40,128]{2,1,0:T(8,128)}), f32[32,40,128]{2,1,0:T(8,128)S(1)}, u32[]{:S(2)}, u32[]{:S(2)}) async-start(f32[32,40,128]{2,1,0:T(8,128)} %bitcast.24), calls=%async_computation | async-start | bytes 1310720 | tf_op jit(solution)/shard_map/all_to_all | solution.py:874
  19.4 7.5 %collective-permute-start.2 = (f32[8,128]{1,0:T(8,128)S(1)}, f32[8,128]{1,0:T(8,128)S(1)}, u32[]{:S(2)}, u32[]{:S(2)}) collective-permute-start(f32[8,128]{1,0:T(8,128)S(1)} %get-tuple-element.23.best_ref), channel_id=1, source_target_pairs={{0,64},{32,96},{64,0},{96,32},{1,65},{33,97},{65,1},{97,33},{2,66}... | collective-permute-start | bytes 12296 | tf_op jit(solution)/shard_map/ppermute | solution.py:861
  31.9 17.2 %all-to-all-start.1 = ((f32[32,41,1,128]{3,2,1,0:T(1,128)}), f32[32,41,1,128]{3,2,1,0:T(1,128)S(1)}, u32[]{:S(2)}, u32[]{:S(2)}) async-start(f32[32,41,1,128]{3,2,1,0:T(1,128)} %bitcast.23), calls=%async_computation.1 | async-start | bytes 1343488 | tf_op jit(solution)/shard_map/all_to_all | solution.py:886
